TPU v7x, 128 devices: a whole 4x4x4 slice. The times are simulated.
128 devices in a mesh: tm: 8 (over y, z_lo), space: 16 (over z_hi, x, core).
Axes of the slice: x: 4, y: 4, z: 4 (z_hi: 2, z_lo: 2; z = z_hi * 2 + z_lo), core: 2. Of those that a mesh axis runs over, the one named last changes fastest.
Arguments:
- video_query: bfloat16 [48, 16, 64, 1536], P('tm', 'space'), may hold values from -8 to 8
- video_key: bfloat16 [48, 16, 64, 1536], P('tm', 'space'), may hold values from -8 to 8
- video_value: bfloat16 [48, 16, 64, 1536], P('tm', 'space'), may hold values from -6 to 6
- text_query: bfloat16 [256, 1536], P(('tm', 'space')), may hold values from -8 to 8
- text_key: bfloat16 [256, 1536], P(('tm', 'space')), may hold values from -8 to 8
- text_value: bfloat16 [256, 1536], P(('tm', 'space')), may hold values from -6 to 6
- window_lists: int32 [8, 16, 27], P('tm'), may hold values from -1 to 127, as said below
- valid_columns: int32 [8], replicated, may hold values from 2 to 8, as said below
- video_weight: bfloat16 [1536, 3072], replicated, may hold values from -0.15625 to 0.15625
- text_weight: bfloat16 [1536, 3072], replicated, may hold values from -0.15625 to 0.15625
Outputs:
- video_output: bfloat16 [8, 16, 1, 384, 3072], P('tm', 'space')
- text_output: bfloat16 [256, 3072], P(('tm', 'space'))
Inputs may be any that keep to these rules, and one draw needn't show every extreme that they name: window_lists[t, b * 8 + w] names, each once and in any order, the tile t * 16 + b * 8 + w itself and some of the tiles t2 * 16 + b2 * 8 + w2 with t2 within one of t, b2 within one of b and w2 within one of w (0 <= b2 < 2, 0 <= w2 < 8); its other entries are -1. `valid_columns`: 8 in every tile column except column 7.
All inputs are finite; a program needn't handle non-finite values.
Results may differ from a plain program's by a relative error of at most 0.0085.
Values may be sent and summed in bfloat16 or wider, within the bound.
No kernel may reach another device: no remote copies, remote signals or barrier semaphores. Data moves between devices by JAX's collectives and lax.ppermute only.
A program may use at most 192 MiB of HBM per device.

v0:
```python
import jax
import jax.numpy as jnp
from jax import lax
from jax.sharding import PartitionSpec as P

HD = 128
TF = 6
TR = 8
TC = 8
SW = 8


def padded(cells, sides, width):
    for axis, dim in sides:
        count = lax.axis_size(axis)
        ends = count - 1
        head = lax.slice_in_dim(cells, 0, width, axis=dim)
        tail = lax.slice_in_dim(cells, cells.shape[dim] - width, cells.shape[dim], axis=dim)
        cells = jnp.concatenate(
            [
                lax.ppermute(tail, axis, [(i, (i + 1) % count) for i in range(ends)]),
                cells,
                lax.ppermute(head, axis, [((i + 1) % count, i) for i in range(ends)]),
            ],
            axis=dim,
        )
    return cells


def shifted(value, axis, steps):
    count = lax.axis_size(axis)
    first, last = (max(0, -steps), min(count, count - steps))
    return lax.ppermute(value, axis, [(source, source + steps) for source in range(first, last)])


def partner(block, axis, apart):
    count = lax.axis_size(axis)
    route = []
    for low in range(count):
        high = low | 1 << apart
        if high != low and high < count:
            route += [(low, high), (high, low)]
    return lax.ppermute(block, axis, route)


def attend(queries, window_keys, window_values, allowed, text_keys, text_values):
    scaling = HD ** (-0.5)
    head_count = queries.shape[2] // HD

    def one_head(head_index):
        offset = head_index * HD
        query_portion = lax.dynamic_slice_in_dim(queries, offset, HD, 2)
        key_portion = lax.dynamic_slice_in_dim(window_keys, offset, HD, 1)
        value_part = lax.dynamic_slice_in_dim(window_values, offset, HD, 1)
        text_key_portion = lax.dynamic_slice_in_dim(text_keys, offset, HD, 1)
        text_value_part = lax.dynamic_slice_in_dim(text_values, offset, HD, 1)
        near_scores = (
            jnp.einsum(
                "wot,lt->wol", query_portion, key_portion, preferred_element_type=jnp.float32
            )
            * scaling
        )
        near_scores = jnp.where(allowed[:, None, :], near_scores, -jnp.inf)
        text_scores = (
            jnp.einsum(
                "wot,lt->wol", query_portion, text_key_portion, preferred_element_type=jnp.float32
            )
            * scaling
        )
        highest = jnp.maximum(jnp.max(near_scores, axis=2), jnp.max(text_scores, axis=2))
        near_weights = jnp.where(
            allowed[:, None, :], jnp.exp(near_scores - highest[:, :, None]), 0.0
        )
        text_weights = jnp.exp(text_scores - highest[:, :, None])
        totals = jnp.sum(near_weights, axis=2) + jnp.sum(text_weights, axis=2)
        summed = jnp.einsum(
            "whu,um->whm",
            near_weights.astype(jnp.bfloat16),
            value_part,
            preferred_element_type=jnp.float32,
        )
        summed = summed + jnp.einsum(
            "whu,um->whm",
            text_weights.astype(jnp.bfloat16),
            text_value_part,
            preferred_element_type=jnp.float32,
        )
        return summed / totals[:, :, None]

    per_head = lax.map(one_head, jnp.arange(head_count, dtype=jnp.int32))
    per_head = per_head.transpose(1, 2, 0, 3)
    return per_head.reshape(queries.shape[0], queries.shape[1], head_count * HD)


def shards(
    video_query,
    video_key,
    video_value,
    text_query,
    text_key,
    text_value,
    window_lists,
    valid_columns,
    video_weight,
    text_weight,
):
    space_count = lax.axis_size("space")
    time_count = lax.axis_size("tm")
    group_count = space_count // SW
    place_index = lax.axis_index("space")
    group_index = place_index % group_count
    column_index = place_index // group_count
    slab_index = lax.axis_index("tm")
    frame_count = video_query.shape[0]
    row_count = video_query.shape[1]
    feature_vectors = video_query.shape[3]
    local_slabs = frame_count // TF
    tile_size = TF * TR * TC
    band_count = row_count * space_count // TR
    group_width = feature_vectors // group_count
    group_heads = group_width // HD
    all_heads = feature_vectors // HD
    slab_tiles = band_count * SW
    per_block = band_count // group_count
    model_width = video_weight.shape[1]
    scaling = HD ** (-0.5)

    def regroup(raster):
        split_portions = raster.reshape(frame_count, row_count, SW, TC, group_count, group_width)
        split_portions = split_portions.transpose(0, 1, 2, 4, 3, 5)
        return split_portions.reshape(frame_count, row_count, space_count, TC, group_width)

    def tiles_of(received_part):
        blocks = received_part.reshape(local_slabs, TF, band_count, TR, TC, group_width)
        return blocks.transpose(0, 2, 1, 3, 4, 5).reshape(
            local_slabs, band_count, tile_size, group_width
        )

    received = (
        lax.all_to_all(regroup(video_query), "space", split_axis=2, concat_axis=1, tiled=True),
        lax.all_to_all(regroup(video_key), "space", split_axis=2, concat_axis=1, tiled=True),
        lax.all_to_all(regroup(video_value), "space", split_axis=2, concat_axis=1, tiled=True),
    )
    query_tiles = tiles_of(received[0])
    key_tiles = tiles_of(received[1])
    value_tiles = tiles_of(received[2])
    all_queries, all_text_keys, all_text_values = (
        lax.all_gather(text_query, ("tm", "space"), axis=0, tiled=True),
        lax.all_gather(text_key, ("tm", "space"), axis=0, tiled=True),
        lax.all_gather(text_value, ("tm", "space"), axis=0, tiled=True),
    )
    group_queries = lax.dynamic_slice_in_dim(all_queries, group_index * group_width, group_width, 1)
    group_text_keys = lax.dynamic_slice_in_dim(
        all_text_keys, group_index * group_width, group_width, 1
    )
    group_text_values = lax.dynamic_slice_in_dim(
        all_text_values, group_index * group_width, group_width, 1
    )
    stacked = jnp.stack([key_tiles, value_tiles])
    timed = padded(stacked, (("tm", 1),), 1)
    lower_side = shifted(timed, "space", group_count)
    upper_side = shifted(timed, "space", -group_count)
    extended = jnp.stack([lower_side, timed, upper_side], axis=2)
    token_column = jnp.arange(tile_size, dtype=jnp.int32) % TC
    places = jnp.arange(SW, dtype=jnp.int32)
    own_valid = jnp.sum(jnp.where(places == column_index, valid_columns, 0))
    own_usable = token_column < own_valid
    beside = column_index + jnp.arange(3, dtype=jnp.int32) - 1
    beside_valid = jnp.sum(
        jnp.where(places[None, :] == beside[:, None], valid_columns[None, :], 0), axis=1
    )
    key_fine = token_column[None, :] < beside_valid[:, None]
    time_step = jnp.arange(3, dtype=jnp.int32)[:, None, None] - 1
    column_step = jnp.arange(3, dtype=jnp.int32)[None, :, None] - 1
    key_band = jnp.arange(band_count, dtype=jnp.int32)[None, None, :]
    key_count = 9 * band_count * tile_size
    collected = []
    moment = slab_index * local_slabs + 0 + time_step
    neighbour = column_index + column_step
    inside = (
        (moment >= 0) & (moment < time_count * local_slabs) & (neighbour >= 0) & (neighbour < SW)
    )
    idents = moment * slab_tiles + key_band * SW + neighbour
    lists = lax.dynamic_index_in_dim(
        window_lists[0].reshape(band_count, SW, -1), column_index, 1, keepdims=False
    )
    listed = (
        jnp.any(lists[:, None, None, None, :] == idents[None, :, :, :, None], axis=4) & inside[None]
    )
    allowed = (listed[:, :, :, :, None] & key_fine[None, None, :, None, :]).reshape(
        band_count, key_count
    )
    window_keys = extended[0, 0:3].reshape(key_count, group_width)
    window_values = extended[1, 0:3].reshape(key_count, group_width)
    attended = attend(
        query_tiles[0], window_keys, window_values, allowed, group_text_keys, group_text_values
    )
    collected.append(jnp.where(own_usable[None, :, None], attended, 0.0).astype(jnp.bfloat16))
    collected = jnp.stack(collected)
    own_rows = lax.dynamic_slice_in_dim(video_weight, group_index * group_width, group_width, 0)
    partial_value = jnp.dot(
        collected.reshape(local_slabs * band_count * tile_size, group_width),
        own_rows,
        preferred_element_type=jnp.float32,
    )
    partial_value = partial_value.reshape(local_slabs, band_count, tile_size, model_width)
    mine = lax.dynamic_slice_in_dim(partial_value, group_index * per_block, per_block, 1)
    other = lax.dynamic_slice_in_dim(partial_value, (1 - group_index) * per_block, per_block, 1)
    combined = mine + partner(other.astype(jnp.bfloat16), "space", 0).astype(other.dtype)
    video_output = combined.astype(jnp.bfloat16).reshape(
        local_slabs, 1, per_block, tile_size, model_width
    )
    key_usable = jnp.tile(own_usable, local_slabs * band_count)
    key_rows = key_tiles.reshape(local_slabs * band_count * tile_size, group_heads, HD)
    value_rows = value_tiles.reshape(local_slabs * band_count * tile_size, group_heads, HD)
    text_total = all_queries.shape[0]
    query_heads = group_queries.reshape(text_total, group_heads, HD)
    share = text_total // (SW * time_count)
    member = slab_index * SW + column_index
    own_text_keys = lax.dynamic_slice_in_dim(group_text_keys, member * share, share, 0).reshape(
        share, group_heads, HD
    )
    local_text_value_rows = lax.dynamic_slice_in_dim(
        group_text_values, member * share, share, 0
    ).reshape(share, group_heads, HD)
    video_scores = (
        jnp.einsum("qhd,khd->hqk", query_heads, key_rows, preferred_element_type=jnp.float32)
        * scaling
    )
    video_scores = jnp.where(key_usable[None, None, :], video_scores, -jnp.inf)
    text_scores = (
        jnp.einsum("qhd,khd->hqk", query_heads, own_text_keys, preferred_element_type=jnp.float32)
        * scaling
    )
    local_peak = jnp.maximum(jnp.max(video_scores, axis=2), jnp.max(text_scores, axis=2))
    padded_peak = lax.dynamic_update_slice(
        jnp.full((all_heads, text_total), -jnp.inf, jnp.float32),
        local_peak,
        (group_index * group_heads, 0),
    )
    highest_all = lax.pmax(padded_peak, ("tm", "space"))
    highest = lax.dynamic_slice_in_dim(highest_all, group_index * group_heads, group_heads, 0)
    video_weights = jnp.where(
        key_usable[None, None, :], jnp.exp(video_scores - highest[:, :, None]), 0.0
    )
    text_weights = jnp.exp(text_scores - highest[:, :, None])
    totals = (jnp.sum(video_weights, axis=2) + jnp.sum(text_weights, axis=2)).T
    summed = jnp.einsum(
        "hqk,khd->qhd",
        video_weights.astype(jnp.bfloat16),
        value_rows,
        preferred_element_type=jnp.float32,
    )
    summed = summed + jnp.einsum(
        "hqk,khd->qhd",
        text_weights.astype(jnp.bfloat16),
        local_text_value_rows,
        preferred_element_type=jnp.float32,
    )
    summed = summed.reshape(text_total, group_width)
    row_count_text = text_query.shape[0]
    part_sums, part_totals = (
        lax.psum_scatter(summed, "tm", scatter_dimension=0, tiled=True),
        lax.psum_scatter(totals, "tm", scatter_dimension=0, tiled=True),
    )
    placed_sums = part_sums.reshape(space_count, row_count_text, group_width)
    placed_totals = part_totals.reshape(space_count, row_count_text, group_heads)
    got_sums, got_totals = (
        lax.all_to_all(placed_sums, "space", split_axis=0, concat_axis=0, tiled=True),
        lax.all_to_all(placed_totals, "space", split_axis=0, concat_axis=0, tiled=True),
    )
    row_sums = jnp.sum(got_sums.reshape(SW, group_count, row_count_text, group_width), axis=0)
    row_sums = row_sums.transpose(1, 0, 2).reshape(row_count_text, feature_vectors)
    row_totals = jnp.sum(got_totals.reshape(SW, group_count, row_count_text, group_heads), axis=0)
    row_totals = row_totals.transpose(1, 0, 2).reshape(row_count_text, all_heads)
    text_attn = (row_sums.reshape(row_count_text, all_heads, HD) / row_totals[:, :, None]).reshape(
        row_count_text, feature_vectors
    )
    text_attn = text_attn.astype(jnp.bfloat16)
    text_output = jnp.dot(text_attn, text_weight, preferred_element_type=jnp.float32).astype(
        jnp.bfloat16
    )
    return (video_output, text_output)


def solution(mesh):
    in_specs = (
        P("tm", "space", None, None),
        P("tm", "space", None, None),
        P("tm", "space", None, None),
        P(("tm", "space"), None),
        P(("tm", "space"), None),
        P(("tm", "space"), None),
        P("tm", None, None),
        P(),
        P(),
        P(),
    )
    out_specs = (P("tm", "space", None, None, None), P(("tm", "space"), None))
    return jax.shard_map(shards, mesh=mesh, in_specs=in_specs, out_specs=out_specs, check_vma=False)
```

profile of v0, /device:TPU:14, one launch (start us, length us, event | category | flops | bytes accessed | tf_op | source)
XLA Modules:
  0.0 1173.0 jit_solution(4294757774099327019)
XLA Ops:
  7.2 2.5 copy.101
  9.6 8.1 all-to-all-start.1
  18.9 15.4 %all-to-all-done.1 = bf16[6,1,16,8,768]{4,3,0,1,2:T(8,128)(2,1)S(1)} async-done(((bf16[6,1,16,8,768]{4,3,0,1,2:T(8,128)(2,1)}), bf16[6,1,16,8,768]{4,3,0,1,2:T(8,128)(2,1)S(1)}, u32[]{:S(2)}, u32[]{:S(2)}) %all-to-all-start.1) | async-done | bytes 1179680 | tf_op jit(solution)/shard_map/all_to_all | solution.py:141
  34.3 6.5 all-to-all-start.2
  40.9 16.4 %all-to-all-done.2 = bf16[6,1,16,8,768]{4,3,0,1,2:T(8,128)(2,1)S(1)} async-done(((bf16[6,1,16,8,768]{4,3,0,1,2:T(8,128)(2,1)}), bf16[6,1,16,8,768]{4,3,0,1,2:T(8,128)(2,1)S(1)}, u32[]{:S(2)}, u32[]{:S(2)}) %all-to-all-start.2) | async-done | bytes 1179680 | tf_op jit(solution)/shard_map/all_to_all | solution.py:142
  57.7 2.9 collective-permute-start.1
  60.7 3.0 collective-permute-start
  63.7 100.2 %collective-permute-done.1 = bf16[2,1,2,384,768]{4,3,2,1,0:T(8,128)(2,1)S(1)} collective-permute-done((bf16[2,1,2,384,768]{4,3,2,1,0:T(8,128)(2,1)S(1)}, bf16[2,1,2,384,768]{4,3,2,1,0:T(8,128)(2,1)S(1)}, u32[]{:S(2)}, u32[]{:S(2)}) %collective-permute-start.1) | collective-permute-done | bytes 2359328 | tf_op jit(solution)/shard_map/ppermute | solution.py:23
  163.9 5.2 fusion.87
  169.1 2.6 collective-permute-start.3
  171.7 7.0 collective-permute-start.2
  179.8 5.9 all-to-all-start
  188.6 294.0 %all-gather.2 = bf16[128,2,1536]{2,1,0:T(2,128)(2,1)S(1)} all-gather(bf16[1,2,1536]{2,1,0:T(2,128)(2,1)S(1)} %bitcast.156), channel_id=1, replica_groups=mesh['tm'=8,'space'=16] {'tm','space'}, dimensions={0}, use_global_device_ids=true | all-gather | bytes 792576 | tf_op jit(solution)/shard_map/all_gather | solution.py:148
  482.6 1.2 reshape.328
  485.0 168.3 %all-gather = bf16[128,2,1536]{2,1,0:T(2,128)(2,1)} all-gather(bf16[1,2,1536]{2,1,0:T(2,128)(2,1)S(1)} %bitcast.157), channel_id=1, replica_groups=mesh['tm'=8,'space'=16] {'tm','space'}, dimensions={0}, use_global_device_ids=true | all-gather | bytes 792576 | tf_op jit(solution)/shard_map/all_gather | solution.py:149
  653.4 3.0 reshape.324
  656.3 181.1 %all-gather.1 = bf16[128,2,1536]{2,1,0:T(2,128)(2,1)} all-gather(bf16[1,2,1536]{2,1,0:T(2,128)(2,1)S(1)} %bitcast.158), channel_id=1, replica_groups=mesh['tm'=8,'space'=16] {'tm','space'}, dimensions={0}, use_global_device_ids=true | all-gather | bytes 792576 | tf_op jit(solution)/shard_map/all_gather | solution.py:150
  837.4 2.9 reshape.326
  841.6 1.8 constant_dynamic-slice_fusion.2
  843.4 2.2 fusion.90
  845.6 2.2 reshape_reshape.10
  847.8 1.4 reshape_reshape.9
  849.2 3.8 fusion.50
  853.2 104.4 %pmax.7 = f32[12,256]{1,0:T(8,128)S(1)} all-reduce(f32[12,256]{1,0:T(8,128)S(1)} %dynamic_update_slice.7), channel_id=1, replica_groups=mesh['tm'=8,'space'=16] {'tm','space'}, use_global_device_ids=true, to_apply=%region_11.12 | all-reduce | flops 3072 | bytes 24576 | tf_op jit(solution)/shard_map/pmax | solution.py:241
  957.6 3.6 fusion.51
  962.1 3.8 fusion.59
  965.9 1.2 fusion.62
  967.1 1.3 copy.99
  969.7 10.2 pad_maximum_fusion
  979.9 5.0 fusion.89
  984.9 9.3 copy.108
  994.2 4.6 copy.107
  998.8 121.8 %while.11 = (s32[]{:T(128)}, bf16[6,2,384,128]{2,3,0,1:T(8,128)(2,1)S(1)}, s32[6]{0:T(128)S(1)}, bf16[2,384,768]{2,1,0:T(8,128)(2,1)S(1)}, bf16[6912,768]{1,0:T(...) while((s32[]{:T(128)}, ...), condition=%wide.region_8.9_spmd.clone, body=%wide.region_3.8_spmd.clone.sunk | while | flops 2889068544 | bytes 72039288 | solution.py:90
  1000.5 5.2 fusion.110
  1006.9 5.8 fusion.112
  1012.8 6.1 fusion.114
  1020.9 5.2 fusion.110
  1026.2 1.2 fusion.111
  1027.3 5.8 fusion.112
  1033.2 6.1 fusion.114
  1041.2 5.1 fusion.110
  1046.5 1.2 fusion.111
  1047.6 5.8 fusion.112
  1053.5 6.1 fusion.114
  1061.5 5.1 fusion.110
  1067.9 5.8 fusion.112
  1073.8 6.1 fusion.114
  1081.8 5.0 fusion.110
  1087.0 1.2 fusion.111
  1088.1 5.8 fusion.112
  1094.0 6.1 fusion.114
  1102.0 5.0 fusion.110
  1107.2 1.2 fusion.111
  1108.4 5.8 fusion.112
  1114.2 6.1 fusion.114
  1120.9 5.9 fusion.47
  1126.8 3.6 copy-done.2
  1131.2 6.3 all-to-all-start.4
  1137.5 5.6 all-to-all-done.4
  1143.2 1.6 reshape.319
  1144.8 5.3 all-to-all-start.3
  1150.2 5.8 all-to-all-done.3
  1156.0 5.8 convolution_convert_fusion
  1162.3 3.8 fusion.54
  (148 shorter events, 22.7 us)
Async XLA Ops:
  7.2 178.8 %copy-start = (s32[1,16,27]{2,1,0:T(8,128)S(1)}, s32[1,16,27]{2,1,0:T(8,128)}, u32[]{:S(2)}) copy-start(s32[1,16,27]{2,1,0:T(8,128)} %param.18) | copy-start | bytes 5188
  7.2 10.6 copy-start.6
  9.6 24.7 %all-to-all-start.1 = ((bf16[6,1,16,8,768]{4,3,0,1,2:T(8,128)(2,1)}), bf16[6,1,16,8,768]{4,3,0,1,2:T(8,128)(2,1)S(1)}, u32[]{:S(2)}, u32[]{:S(2)}) async-start(bf16[6,1,16,8,768]{4,3,0,1,2:T(8,128)(2,1)} %bitcast.8), calls=%async_computation.1 | async-start | bytes 2359296 | tf_op jit(solution)/shard_map/all_to_all | solution.py:141
  34.3 23.0 %all-to-all-start.2 = ((bf16[6,1,16,8,768]{4,3,0,1,2:T(8,128)(2,1)}), bf16[6,1,16,8,768]{4,3,0,1,2:T(8,128)(2,1)S(1)}, u32[]{:S(2)}, u32[]{:S(2)}) async-start(bf16[6,1,16,8,768]{4,3,0,1,2:T(8,128)(2,1)} %bitcast.14), calls=%async_computation.2 | async-start | bytes 2359296 | tf_op jit(solution)/shard_map/all_to_all | solution.py:142
  57.7 121.0 %copy-start.7 = (bf16[6,1,64,1536]{3,2,1,0:T(8,128)(2,1)S(1)}, bf16[6,1,64,1536]{3,2,1,0:T(8,128)(2,1)}, u32[]{:S(2)}) copy-start(bf16[6,1,64,1536]{3,2,1,0:T(8,128)(2,1)} %param.12) | copy-start | bytes 3538948
  57.7 106.2 %collective-permute-start.1 = (bf16[2,1,2,384,768]{4,3,2,1,0:T(8,128)(2,1)S(1)}, bf16[2,1,2,384,768]{4,3,2,1,0:T(8,128)(2,1)S(1)}, u32[]{:S(2)}, u32[]{:S(2)}) collective-permute-start(bf16[2,1,2,384,768]{4,3,2,1,0:T(8,128)(2,1)S(1)} %pad_maximum_fusion.2), channel_id=1, source_target_pairs={{16,0},{32,16},{48,32},{64,48},{80,64},{96,80},{112,96},{17,1},{33... | collective-permute-start | bytes 7077896 | tf_op jit(solution)/shard_map/ppermute | solution.py:23
  60.7 103.2 %collective-permute-start = (bf16[2,1,2,384,768]{4,3,2,1,0:T(8,128)(2,1)S(1)}, bf16[2,1,2,384,768]{4,3,2,1,0:T(8,128)(2,1)S(1)}, u32[]{:S(2)}, u32[]{:S(2)}) collective-permute-start(bf16[2,1,2,384,768]{4,3,2,1,0:T(8,128)(2,1)S(1)} %pad_maximum_fusion.2), channel_id=1, source_target_pairs={{0,16},{16,32},{32,48},{48,64},{64,80},{80,96},{96,112},{1,17},{17... | collective-permute-start | bytes 7077896 | tf_op jit(solution)/shard_map/ppermute | solution.py:21
  169.1 17.6 %copy-start.16 = (s32[8]{0:T(128)S(1)}, s32[8]{0:T(128)}, u32[]{:S(2)}) copy-start(s32[8]{0:T(128)} %param.19) | copy-start | bytes 100
  169.1 19.5 %copy-start.11 = (bf16[2,1536]{1,0:T(2,128)(2,1)S(1)}, bf16[2,1536]{1,0:T(2,128)(2,1)}, u32[]{:S(2)}) copy-start(bf16[2,1536]{1,0:T(2,128)(2,1)} %param.15) | copy-start | bytes 18436
  169.1 315.9 %copy-start.12 = (bf16[2,1536]{1,0:T(2,128)(2,1)S(1)}, bf16[2,1536]{1,0:T(2,128)(2,1)}, u32[]{:S(2)}) copy-start(bf16[2,1536]{1,0:T(2,128)(2,1)} %param.16) | copy-start | bytes 18436
  169.1 800.6 %collective-permute-start.3 = (bf16[2,3,2,384,768]{4,3,2,1,0:T(8,128)(2,1)}, bf16[2,3,2,384,768]{4,3,2,1,0:T(8,128)(2,1)}, u32[]{:S(2)}, u32[]{:S(2)}) collective-permute-start(bf16[2,3,2,384,768]{4,3,2,1,0:T(8,128)(2,1)} %get-tuple-element.111), channel_id=1, source_target_pairs={{2,0},{3,1},{4,2},{5,3},{6,4},{7,5},{8,6},{9,7},{10,8},{11,9},{12,... | collective-permute-start | bytes 21233672 | tf_op jit(solution)/shard_map/ppermute | solution.py:33
  171.7 798.0 %collective-permute-start.2 = (bf16[2,3,2,384,768]{4,3,2,1,0:T(8,128)(2,1)}, bf16[2,3,2,384,768]{4,3,2,1,0:T(8,128)(2,1)}, u32[]{:S(2)}, u32[]{:S(2)}) collective-permute-start(bf16[2,3,2,384,768]{4,3,2,1,0:T(8,128)(2,1)} %get-tuple-element.111), channel_id=1, source_target_pairs={{0,2},{1,3},{2,4},{3,5},{4,6},{5,7},{6,8},{7,9},{8,10},{9,11},{10,... | collective-permute-start | bytes 21233672 | tf_op jit(solution)/shard_map/ppermute | solution.py:33
  179.8 476.5 %copy-start.13 = (bf16[2,1536]{1,0:T(2,128)(2,1)S(1)}, bf16[2,1536]{1,0:T(2,128)(2,1)}, u32[]{:S(2)}) copy-start(bf16[2,1536]{1,0:T(2,128)(2,1)} %param.17) | copy-start | bytes 18436
  179.8 787.3 %all-to-all-start = ((bf16[6,1,16,8,768]{4,3,0,1,2:T(8,128)(2,1)}), bf16[6,1,16,8,768]{4,3,0,1,2:T(8,128)(2,1)}, u32[]{:S(2)}, u32[]{:S(2)}) async-start(bf16[6,1,16,8,768]{4,3,0,1,2:T(8,128)(2,1)} %bitcast.2), calls=%async_computation | async-start | bytes 2359296 | tf_op jit(solution)/shard_map/all_to_all | solution.py:140
  185.7 945.5 %reduce-scatter.7.cloned.1.call-start = ((), (), s32[]{:S(2)}) async-start(), calls=%async_computation.8 | async-start | bytes 147456 | tf_op jit(solution)/shard_map/reduce_scatter | solution.py:264
  188.0 653.6 %copy-start.14 = (pred[384]{0:T(512)(128)(4,1)}, pred[384]{0:T(512)(128)(4,1)S(1)}, u32[]{:S(2)}) copy-start(pred[384]{0:T(512)(128)(4,1)S(1)} %broadcast_compare_fusion.1) | copy-start | bytes 1156
  849.2 3.8 copy-start.9
  853.0 108.2 %copy-start.8 = (f32[6,256,4]{1,2,0:T(4,128)S(1)}, f32[6,256,4]{1,2,0:T(4,128)}, u32[]{:S(2)}) copy-start(f32[6,256,4]{1,2,0:T(4,128)} %get-tuple-element.115) | copy-start | bytes 73732
  853.0 109.1 %copy-start.4 = (bf16[768,6,128]{2,1,0:T(8,128)(2,1)S(1)}, bf16[768,6,128]{2,1,0:T(8,128)(2,1)}, u32[]{:S(2)}) copy-start(bf16[768,6,128]{2,1,0:T(8,128)(2,1)} %reshape_reshape.10) | copy-start | bytes 3538948
  853.0 109.1 %copy-start.10 = (pred[768]{0:T(1024)(128)(4,1)S(1)}, pred[768]{0:T(1024)(128)(4,1)}, u32[]{:S(2)}) copy-start(pred[768]{0:T(1024)(128)(4,1)} %broadcast_in_dim.103) | copy-start | bytes 2308
  962.0 181.2 %reduce-scatter.5.cloned.1.call-start = ((), (), s32[]{:S(2)}) async-start(), calls=%async_computation.7 | async-start | bytes 884736 | tf_op jit(solution)/shard_map/reduce_scatter | solution.py:263
  994.2 4.6 copy-start.5
  998.8 121.8 %copy-start.15 = (pred[384]{0:T(512)(128)(4,1)S(1)}, pred[384]{0:T(512)(128)(4,1)}, u32[]{:S(2)}) copy-start(pred[384]{0:T(512)(128)(4,1)} %copy-done.14) | copy-start | bytes 1156
  1126.8 3.6 copy-start.2
  1130.7 31.0 %collective-permute-start.4 = (bf16[1,1,384,3072]{3,2,1,0:T(8,128)(2,1)S(1)}, bf16[1,1,384,3072]{3,2,1,0:T(8,128)(2,1)}, u32[]{:S(2)}, u32[]{:S(2)}) collective-permute-start(bf16[1,1,384,3072]{3,2,1,0:T(8,128)(2,1)S(1)} %fusion.53), channel_id=1, source_target_pairs={{0,1},{1,0},{2,3},{3,2},{4,5},{5,4},{6,7},{7,6},{8,9},{9,8},{10,11... | collective-permute-start | bytes 7077896 | tf_op jit(solution)/shard_map/ppermute | solution.py:43
  1131.2 11.9 %all-to-all-start.4 = ((f32[16,2,6]{2,1,0:T(2,128)}), f32[16,2,6]{2,1,0:T(2,128)S(1)}, u32[]{:S(2)}, u32[]{:S(2)}) async-start(f32[16,2,6]{2,1,0:T(2,128)} %bitcast.154), calls=%async_computation.5 | async-start | bytes 32768 | tf_op jit(solution)/shard_map/all_to_all | solution.py:270
  1144.8 11.1 all-to-all-start.3
  1156.0 6.4 copy-start.3
  1156.0 10.2 copy-start.1
Sparse Core Ops, SparseCore 0:
  962.1 34.2 reduce-scatter.6
  999.5 37.2 reduce-scatter.4
where the time goes:
time: 1180 us; the launch traced here: 1170 us
  blocking collectives  748 us (63%)
  waiting for transfers between devices  143 us (12%)
  matrix products  98.5 us (8%)
  other arithmetic  61.9 us (5%)
  local copies, waits for them, and re-layouts  54.2 us (5%)
  starting transfers between devices  48.1 us (4%)
  between operations  14.6 us (1%)
    all_gather x1, blocking collectives, shards(): lax.all_gather(text_query, ('tm', 'space'), axis=0, tiled=True)  294 us
    all_gather x1, blocking collectives, shards(): lax.all_gather(text_value, ('tm', 'space'), axis=0, tiled=True)  181 us
    all_gather x1, blocking collectives, shards(): lax.all_gather(text_key, ('tm', 'space'), axis=0, tiled=True)  168 us
    pmax x1, blocking collectives, shards(): highest_all = lax.pmax(padded_peak, ('tm', 'space'))  104 us
    ppermute x1, waiting for transfers between devices, padded(): lax.ppermute(head, axis, [((i + 1) % count, i) for i in range(ends)])  100 us
    dot_general x6, matrix products, one_head(): jnp.einsum('whu,um->whm', near_weights.astype(jnp.bfloat16), value_part,...  36.8 us
    reduce_sum x12, other arithmetic, one_head(): totals = jnp.sum(near_weights, axis=2) + jnp.sum(text_weights, axis=2)  35.7 us
    dot_general x6, matrix products, one_head(): jnp.einsum('wot,lt->wol', query_portion, key_portion, preferred_element_t...  30.5 us
  transfers between devices with their start and end apart: 12, of which 5 were waited for; matrix products, arithmetic and copies ran while one was open for 17% of the time, Pallas kernels for 0%

commit v1 on v0

v1 whole, which is shorter than its diff:
```python
import functools
import math

import jax
import jax.numpy as jnp
from jax import lax
from jax.experimental import pallas as pl
from jax.experimental.pallas import tpu as pltpu
from jax.sharding import PartitionSpec as P

HD = 128
TF = 6
TC = 8
TILE = 384
CELL = 2 * TILE
GW = 384
GH = GW // HD
TXT = 256
AXES = ("tm", "space")
SCALE = HD**-0.5 * math.log2(math.e)
MASKED = -1e30
CONTRACT_LAST = (((1,), (1,)), ((), ()))


def device(y, z, x, c):
    return (2 * y + z % 2) * 16 + 8 * (z // 2) + 2 * x + c


PLACES = [(y, z, x, c) for y in range(4) for z in range(4) for x in range(4) for c in range(2)]
PLANES = [
    [device(y, z, x, c) for z in range(4) for x in range(4)] for y in range(4) for c in range(2)
]


def route(target):
    pairs = []
    for place in PLACES:
        goal = target(*place)
        if goal is not None:
            pairs.append((device(*place), device(*goal)))
    return pairs


def in_time(steps):
    def target(y, z, x, c):
        moment = 2 * y + c + steps
        return (moment // 2, z, x, moment % 2) if 0 <= moment < 8 else None

    return route(target)


def in_columns(steps):
    return route(lambda y, z, x, c: (y, z, x + steps, c) if 0 <= x + steps < 4 else None)


def to_owner(turn):
    def target(y, z, x, c):
        tile = (z + turn) % 4
        return (y, 2 * (x // 2) + c, 2 * (x % 2) + tile // 2, tile % 2)

    return route(target)


OTHER_CORE = route(lambda y, z, x, c: (y, z, x, 1 - c))


def along_y(steps):
    return route(lambda y, z, x, c: ((y + steps) % 4, z, x, c))


def send(value, pairs):
    return lax.ppermute(value, AXES, pairs)


def spread(value):
    return lax.all_to_all(
        value, AXES, split_axis=0, concat_axis=0, tiled=True, axis_index_groups=PLANES
    )


def attend_kernel(rows, lane, groups, has_text, has_state, final, *refs):
    refs = list(refs)
    valid_ref = refs.pop(0)
    q_ref = refs.pop(0)
    step = pl.program_id(1)
    lanes = lax.broadcasted_iota(jnp.int32, (rows, HD), 1)
    hot = jnp.where(lanes == (step if lane is None else lane), 1.0, 0.0).astype(jnp.bfloat16)
    query = jnp.concatenate([q_ref[0], hot], axis=1)
    if has_state:
        old_sum, old_mark = refs.pop(0)[0], refs.pop(0)[0]
        peak = old_mark[:, :1]
        total = jnp.concatenate(
            [old_sum, jnp.broadcast_to(old_mark[:, HD // 2 : HD // 2 + 1], (rows, HD))], axis=1
        )
    else:
        peak, total = None, None
    blocks = []
    if has_text:
        k_ref, v_ref, b_ref = refs.pop(0), refs.pop(0), refs.pop(0)
        blocks.append((k_ref.at[0], v_ref.at[0], b_ref))
    for cells in groups:
        k_ref, v_ref, b_ref = refs.pop(0), refs.pop(0), refs.pop(0)
        for i in range(cells):
            blocks.append((k_ref.at[0, i], v_ref.at[0, i], b_ref.at[0, i]))
    for keys, values, bias in blocks:
        count = keys.shape[0]
        wide_keys = jnp.concatenate([keys[...], bias[...]], axis=1)
        wide_values = jnp.concatenate([values[...], jnp.ones((count, HD), jnp.bfloat16)], axis=1)
        scores = lax.dot_general(
            query, wide_keys, CONTRACT_LAST, preferred_element_type=jnp.float32
        )
        top = jnp.max(scores, axis=1, keepdims=True)
        if peak is not None:
            top = jnp.maximum(top, peak)
        weights = jnp.exp2((scores - top) * SCALE).astype(jnp.bfloat16)
        part = jnp.dot(weights, wide_values, preferred_element_type=jnp.float32)
        if peak is not None:
            part = part + total * jnp.exp2((peak - top) * SCALE)
        peak, total = top, part
    if final:
        (out_ref,) = refs
        row = lax.broadcasted_iota(jnp.int32, (rows, HD), 0)
        usable = row % TC < valid_ref[step // 2]
        out_ref[0] = jnp.where(usable, total[:, :HD] / total[:, HD:], 0.0).astype(jnp.bfloat16)
    else:
        sum_ref, mark_ref = refs
        sum_ref[0] = total[:, :HD]
        mark_ref[0] = jnp.where(
            lanes < HD // 2, jnp.broadcast_to(peak, (rows, HD)), total[:, HD:]
        )


def attend(name, valid, queries, state, text, groups, lane=None, final=False):
    steps, rows, width = queries.shape
    heads = width // HD
    tall = pl.BlockSpec((1, rows, HD), lambda h, i: (i, 0, h))
    specs = [pl.BlockSpec(memory_space=pltpu.SMEM), tall]
    operands = [valid, queries]
    if state is not None:
        specs += [tall, tall]
        operands += list(state)
    keys = 0
    if text is not None:
        text_keys, text_values, text_bias = text
        specs += [
            pl.BlockSpec((1, TXT, HD), lambda h, i: (1, 0, h)),
            pl.BlockSpec((1, TXT, HD), lambda h, i: (2, 0, h)),
            pl.BlockSpec((TXT, HD), lambda h, i: (0, 0)),
        ]
        operands += [text_keys, text_values, text_bias]
        keys += TXT
    counts = []
    for cells, bias, sided in groups:
        number = 1 if sided else cells.shape[1]
        counts.append(number)
        keys += number * CELL
        if sided:
            for kind in range(2):
                specs.append(
                    pl.BlockSpec(
                        (1, 1, CELL, HD),
                        functools.partial(lambda kind, h, i: (i // 2, kind, 0, h), kind),
                    )
                )
            specs.append(pl.BlockSpec((1, 1, CELL, HD), lambda h, i: (0, i // 2, 0, 0)))
        else:
            for kind in range(2):
                specs.append(
                    pl.BlockSpec(
                        (1, number, CELL, HD),
                        functools.partial(lambda kind, h, i: (kind, 0, 0, h), kind),
                    )
                )
            specs.append(pl.BlockSpec((1, number, CELL, HD), lambda h, i: (0, 0, 0, 0)))
        operands += [cells, cells, bias[None]]
    if final:
        out_shape = jax.ShapeDtypeStruct((steps, rows, width), jnp.bfloat16)
        out_specs = tall
    else:
        out_shape = [jax.ShapeDtypeStruct((steps, rows, width), jnp.float32)] * 2
        out_specs = [tall, tall]
    scores = steps * heads * rows * keys
    return pl.pallas_call(
        functools.partial(
            attend_kernel, rows, lane, counts, text is not None, state is not None, final
        ),
        grid=(heads, steps),
        in_specs=specs,
        out_specs=out_specs,
        out_shape=out_shape,
        compiler_params=pltpu.CompilerParams(vmem_limit_bytes=48 * 2**20),
        cost_estimate=pl.CostEstimate(
            flops=scores * 4 * 256, bytes_accessed=2 * keys * width * 2, transcendentals=scores
        ),
        name=name,
    )(*operands)


def shards(
    video_query,
    video_key,
    video_value,
    text_query,
    text_key,
    text_value,
    window_lists,
    valid_columns,
    video_weight,
    text_weight,
):
    tm, space = lax.axis_index("tm"), lax.axis_index("space")
    y, zl = tm // 2, tm % 2
    zh, x, c = space // 8, space // 2 % 4, space % 2
    moment = 2 * y + c
    even_core = c == 0

    def chunks(raster):
        cut = raster.reshape(TF, 4, 2 * TC, 4, GW).transpose(3, 1, 0, 2, 4)
        return cut.reshape(16, TF * 2 * TC, GW)

    def merged(mine, other, axis):
        return jnp.stack(
            [jnp.where(even_core, mine, other), jnp.where(even_core, other, mine)], axis=axis
        )

    text_rows = jnp.concatenate([text_query, text_key, text_value], axis=0)
    text_rows = text_rows.reshape(6, 4, GW).transpose(1, 0, 2)
    lists = jnp.pad(window_lists.astype(jnp.bfloat16).reshape(-1), (0, 2 * GW - 16 * 27))
    extras = jnp.concatenate(
        [text_rows, jnp.broadcast_to(lists.reshape(1, 2, GW), (4, 2, GW))], axis=1
    )
    extras = jnp.broadcast_to(extras[:, None], (4, 4, 8, GW)).reshape(16, 8, GW)
    first = spread(jnp.concatenate([chunks(video_key), chunks(video_value), extras], axis=1))
    second = spread(chunks(video_query))

    pieces = first[:, : 4 * TF * TC].reshape(2, 2, 4, 2, TF, 2, TC, GW)
    mine = lax.dynamic_index_in_dim(pieces, c, 1, keepdims=False)
    other = send(lax.dynamic_index_in_dim(pieces, 1 - c, 1, keepdims=False), OTHER_CORE)
    own = merged(mine, other, 2).transpose(3, 5, 0, 4, 1, 2, 6, 7).reshape(2, 2, CELL, GW)

    text_mine = first[:, 4 * TF * TC : 4 * TF * TC + 6]
    text_both = merged(text_mine, send(text_mine, OTHER_CORE), 0)
    turns = [send(text_both, along_y(steps)) for steps in (3, 2, 1)] + [text_both]
    turned = jnp.stack(turns + turns)
    text_all = lax.dynamic_slice_in_dim(turned, (3 - y) % 4, 4, 0)
    text_all = text_all.reshape(4, 2, 2, 2, 4, 3, 2, GW).transpose(5, 0, 3, 2, 4, 1, 6, 7)
    text_all = text_all.reshape(3, TXT, GW)

    query_pieces = second.reshape(2, 2, 4, TF, 2, TC, GW)
    query_mine = lax.dynamic_index_in_dim(query_pieces, c, 1, keepdims=False)
    query_other = send(
        lax.dynamic_index_in_dim(query_pieces, 1 - c, 1, keepdims=False), OTHER_CORE
    )
    queries = merged(query_mine, query_other, 2).transpose(4, 0, 3, 1, 2, 5, 6)
    queries = queries.reshape(4, TILE, GW)

    past = send(own, in_time(1))
    future = send(own, in_time(-1))
    sides = jnp.stack([send(own[:, 1], in_columns(1)), send(own[:, 0], in_columns(-1))])
    past_sides = send(sides, in_time(1))
    future_sides = send(sides, in_time(-1))

    got_lists = lax.dynamic_index_in_dim(first, 4 * c, 0, keepdims=False)[4 * TF * TC + 6 :]
    got_lists = got_lists.reshape(-1)[: 16 * 27].reshape(2, 8, 27).astype(jnp.int32)
    tile_lists = lax.dynamic_slice_in_dim(got_lists, 2 * x, 2, 1).transpose(1, 0, 2).reshape(4, 27)
    key_moment = moment + jnp.arange(-1, 2, dtype=jnp.int32)[:, None, None]
    key_column = 2 * x + jnp.arange(-1, 3, dtype=jnp.int32)[None, :, None]
    key_band = jnp.arange(2, dtype=jnp.int32)[None, None, :]
    inside = (key_moment >= 0) & (key_moment < 8) & (key_column >= 0) & (key_column < 8)
    idents = jnp.where(inside, 16 * key_moment + 8 * key_band + key_column, -2)
    listed = jnp.any(idents[..., None, None] == tile_lists, axis=-1)
    places = jnp.arange(8, dtype=jnp.int32)
    columns = 2 * x + jnp.arange(-1, 3, dtype=jnp.int32)
    valid = jnp.sum(
        jnp.where(places[None, :] == columns[:, None], valid_columns[None, :], 0), axis=1
    )
    fine = places[None, :] < valid[:, None]
    listed = jnp.concatenate([listed, jnp.ones((3, 4, 2, 1), bool)], axis=3)
    listed = jnp.pad(listed, ((0, 0), (0, 0), (0, 0), (0, HD - 5)))
    allowed = listed[:, :, :, None, None, :] & fine[None, :, None, None, :, None]
    bias = jnp.where(allowed, 0.0, MASKED).astype(jnp.bfloat16)
    bias = jnp.broadcast_to(bias, (3, 4, 2, TILE // TC, TC, HD)).reshape(3, 4, CELL, HD)
    near_bias = bias[:, 1:3]
    side_bias = jnp.stack([bias[:, 0], bias[:, 3]], axis=1)
    share = jnp.arange(TXT, dtype=jnp.int32)[:, None] // 8
    text_lane = jnp.arange(HD, dtype=jnp.int32)[None, :] == 4
    text_bias = jnp.where(text_lane & (share != 8 * y + 4 * c + x), MASKED, 0.0)
    text_bias = text_bias.astype(jnp.bfloat16)

    own_valid = valid[1:3]
    text = (text_all, text_all, text_bias)
    text_sum, text_mark = attend(
        "text_queries",
        own_valid,
        text_all[:1],
        None,
        text,
        [(own, near_bias[1], False)],
        lane=4,
    )
    text_parts = jnp.concatenate([text_sum[0], text_mark[0]], axis=1).reshape(128, 2, 2 * GW)
    text_parts = lax.all_to_all(text_parts, AXES, split_axis=0, concat_axis=0, tiled=True)
    text_parts = text_parts.reshape(4, 2, 2, 4, 2, 2, 2, GH, HD)
    text_sums = text_parts[..., 0, :, :]
    text_peaks = text_parts[..., 1, :, :1]
    text_totals = text_parts[..., 1, :, HD // 2 : HD // 2 + 1]
    text_top = jnp.max(text_peaks, axis=(0, 3, 4), keepdims=True)
    factors = jnp.exp2((text_peaks - text_top) * SCALE)
    text_attn = jnp.sum(text_sums * factors, axis=(0, 3, 4)) / jnp.sum(
        text_totals * factors, axis=(0, 3, 4)
    )
    text_attn = text_attn.transpose(2, 1, 0, 3, 4).reshape(2, 4 * GW).astype(jnp.bfloat16)
    text_output = jnp.dot(text_attn, text_weight, preferred_element_type=jnp.float32)
    text_output = text_output.astype(jnp.bfloat16)

    state = attend("own_cells", own_valid, queries, None, text, [(own, near_bias[1], False)])
    state = attend(
        "time_cells",
        own_valid,
        queries,
        state,
        None,
        [(past, near_bias[0], False), (future, near_bias[2], False)],
    )
    attended = attend(
        "side_cells",
        own_valid,
        queries,
        state,
        None,
        [
            (sides, side_bias[1], True),
            (past_sides, side_bias[0], True),
            (future_sides, side_bias[2], True),
        ],
        final=True,
    )

    z = 2 * zh + zl
    arrived = [
        send(lax.dynamic_index_in_dim(attended, (z + turn) % 4, 0, keepdims=False), to_owner(turn))
        for turn in (3, 2, 1, 0)
    ]
    ordered = jnp.stack(arrived + arrived)
    tile = 2 * (x % 2) + c
    ordered = lax.dynamic_slice_in_dim(ordered, (3 - tile) % 4, 4, 0)
    video_attn = ordered.transpose(1, 0, 2).reshape(TILE, 4 * GW)
    video_output = jnp.dot(video_attn, video_weight, preferred_element_type=jnp.float32)
    video_output = video_output.astype(jnp.bfloat16).reshape(1, 1, 1, TILE, -1)
    return (video_output, text_output)


def solution(mesh):
    in_specs = (
        P("tm", "space", None, None),
        P("tm", "space", None, None),
        P("tm", "space", None, None),
        P(("tm", "space"), None),
        P(("tm", "space"), None),
        P(("tm", "space"), None),
        P("tm", None, None),
        P(),
        P(),
        P(),
    )
    out_specs = (P("tm", "space", None, None, None), P(("tm", "space"), None))
    return jax.shard_map(shards, mesh=mesh, in_specs=in_specs, out_specs=out_specs, check_vma=False)
```

time: 1180 us -> 277 us (0.23)
  blocking collectives: 748 us -> 0 us
  matrix products: 98.5 us -> 10.8 us
  waiting for transfers between devices: 143 us -> 55.8 us
  Pallas kernels: 0 us -> 80.7 us
  other arithmetic: 61.9 us -> 20 us
  between operations: 14.6 us -> 1.5 us
    all_gather x3 -> x0, blocking collectives: 643 us -> none  [the longest x1 294 us: shards(): lax.all_gather(text_query, ('tm', 'space'), axis=0, tiled=True)]
    pmax x1 -> x0, blocking collectives: 104 us -> none  [shards(): highest_all = lax.pmax(padded_peak, ('tm', 'space'))]
    dot_general x29 -> x1, matrix products: 92.7 us -> 8.88 us  [shards(): jnp.dot(video_attn, video_weight, preferred_element_type=jnp.float32)]
    pallas_call x0 -> x4, Pallas kernels: none -> 80.7 us  [attend(): pl.pallas_call(functools.partial(attend_kernel, rows, lane, counts, text...]
    ppermute x5 -> x16, waiting for transfers between devices: 100 us -> 23 us  [send(): return lax.ppermute(value, AXES, pairs)]
    reduce_sum x18 -> x3, other arithmetic: 40.2 us -> 2.76 us  [the longest x1 1.41 us: shards(): jnp.sum(text_sums * factors, axis=(0, 3, 4))]
    ppermute x5 -> x16, starting transfers between devices: 16 us -> 30.6 us  [send(): return lax.ppermute(value, AXES, pairs)]
    all_to_all x5 -> x3, waiting for transfers between devices: 43.2 us -> 32.8 us  [the longest x2 32.8 us: spread(): lax.all_to_all(value, AXES, split_axis=0, concat_axis=0, tiled=True, axis...]
  transfers between devices with their start and end apart: 12 -> 19, of which waited for: 5 -> 10; matrix products, arithmetic and copies ran while one was open for 17% -> 20% of each run, Pallas kernels for 0% -> 20%
where the time goes in v1:
time: 277 us; the launch traced here: 274 us
  Pallas kernels  80.7 us (29%)
  starting transfers between devices  56.7 us (20%)
  waiting for transfers between devices  55.8 us (20%)
  local copies, waits for them, and re-layouts  48.7 us (18%)
  other arithmetic  20 us (7%)
  matrix products  10.8 us (4%)
    pallas_call x4, Pallas kernels, attend(): pl.pallas_call(functools.partial(attend_kernel, rows, lane, counts, text...  80.7 us
    all_to_all x2, waiting for transfers between devices, spread(): lax.all_to_all(value, AXES, split_axis=0, concat_axis=0, tiled=True, axis...  32.8 us
    ppermute x16, starting transfers between devices, send(): return lax.ppermute(value, AXES, pairs)  30.6 us
    ppermute x16, waiting for transfers between devices, send(): return lax.ppermute(value, AXES, pairs)  23 us
    all_to_all x2, starting transfers between devices, spread(): lax.all_to_all(value, AXES, split_axis=0, concat_axis=0, tiled=True, axis...  15.3 us
    all_to_all x1, starting transfers between devices, shards(): lax.all_to_all(text_parts, AXES, split_axis=0, concat_axis=0, tiled=True)  10.8 us
    dot_general x1, matrix products, shards(): jnp.dot(video_attn, video_weight, preferred_element_type=jnp.float32)  8.88 us
    unnamed x61, local copies, waits for them, and re-layouts  8.61 us
  transfers between devices with their start and end apart: 19, of which 10 were waited for; matrix products, arithmetic and copies ran while one was open for 20% of the time, Pallas kernels for 20%

profile of v1, /device:TPU:14, one launch (start us, length us, event | category | flops | bytes accessed | tf_op | source)
XLA Modules:
  0.0 274.2 jit_solution(3426810814058053423)
XLA Ops:
  0.6 2.5 reshape.320
  3.2 1.2 copy.68
  4.3 8.4 %all-to-all-start = ((bf16[16,96,384]{2,1,0:T(8,128)(2,1)}), bf16[16,96,384]{2,1,0:T(8,128)(2,1)S(1)}, u32[]{:S(2)}, u32[]{:S(2)}) async-start(bf16[16,96,384]{2,1,0:T(8,128)(2,1)} %bitcast.1), calls=%async_computation | async-start | bytes 2359296 | tf_op jit(solution)/shard_map/all_to_all | solution.py:76
  14.1 2.5 reshape.324
  16.6 1.2 copy.70
  18.6 3.0 %pad_maximum_fusion = bf16[16,200,384]{2,1,0:T(8,128)(2,1)} fusion(bf16[16,8,384]{2,1,0:T(8,128)(2,1)S(1)} %bitcast.165, bf16[16,96,384]{2,1,0:T(8,128)(2,1)S(1)} %bitcast.160, bf16[16,96,384]{2,1,0:T(8,128)(2,1)} %bitcast.161), kind=kLoop, calls=%fused_computation.3 | loop fusion | flops 7372800 | bytes 4915200 | tf_op jit(solution)/shard_map/concatenate | solution.py:233
  21.5 7.2 %all-to-all-done = bf16[16,96,384]{2,1,0:T(8,128)(2,1)S(1)} async-done(((bf16[16,96,384]{2,1,0:T(8,128)(2,1)}), bf16[16,96,384]{2,1,0:T(8,128)(2,1)S(1)}, u32[]{:S(2)}, u32[]{:S(2)}) %all-to-all-start) | async-done | bytes 1179680 | tf_op jit(solution)/shard_map/all_to_all | solution.py:76
  28.7 1.0 copy-done.14
  29.7 6.9 %all-to-all-start.1 = ((bf16[16,200,384]{2,1,0:T(8,128)(2,1)}), bf16[16,200,384]{2,1,0:T(8,128)(2,1)S(1)}, u32[]{:S(2)}, u32[]{:S(2)}) async-start(bf16[16,200,384]{2,1,0:T(8,128)(2,1)} %pad_maximum_fusion), calls=%async_computation.1 | async-start | bytes 4915200 | tf_op jit(solution)/shard_map/all_to_all | solution.py:76
  37.1 1.1 dynamic-slice_bitcast_fusion.2
  39.3 1.1 collective-permute-done
  40.4 1.4 fusion.3
  41.9 1.2 copy.69
  43.2 25.6 %all-to-all-done.1 = bf16[16,200,384]{2,1,0:T(8,128)(2,1)S(1)} async-done(((bf16[16,200,384]{2,1,0:T(8,128)(2,1)}), bf16[16,200,384]{2,1,0:T(8,128)(2,1)S(1)}, u32[]{:S(2)}, u32[]{:S(2)}) %all-to-all-start.1) | async-done | bytes 2457632 | tf_op jit(solution)/shard_map/all_to_all | solution.py:76
  70.2 1.0 fusion.20
  72.5 1.1 pad_maximum_fusion.3
  73.6 2.6 collective-permute-start.3
  76.2 1.9 collective-permute-start.4
  78.1 0.9 collective-permute-done.2
  79.0 5.2 %collective-permute-done.3 = bf16[2,16,6,384]{3,2,1,0:T(8,128)(2,1)S(1)} collective-permute-done((bf16[2,16,6,384]{3,2,1,0:T(8,128)(2,1)S(1)}, bf16[2,16,6,384]{3,2,1,0:T(8,128)(2,1)S(1)}, u32[]{:S(2)}, u32[]{:S(2)}) %collective-permute-start.3) | collective-permute-done | bytes 147488 | tf_op jit(solution)/shard_map/ppermute | solution.py:72
  84.2 2.4 collective-permute-done.4
  87.8 1.9 slice_bitcast_fusion.1
  89.7 3.1 %collective-permute-start.9 = (bf16[2,768,384]{2,1,0:T(8,128)(2,1)}, bf16[2,768,384]{2,1,0:T(8,128)(2,1)}, u32[]{:S(2)}, u32[]{:S(2)}) collective-permute-start(bf16[2,768,384]{2,1,0:T(8,128)(2,1)} %get-tuple-element.21), channel_id=1, source_target_pairs={{2,0},{3,1},{4,2},{5,3},{6,4},{7,5},{18,16},{19,17},{20,18},{21,19... | collective-permute-start | bytes 3538952 | tf_op jit(solution)/shard_map/ppermute | solution.py:72
  92.8 1.3 collective-permute-start.8
  94.8 1.4 copy.74
  96.4 2.0 reshape.332.refs_2_.refs_3_
  99.2 1.0 slice.82.refs_1_
  100.2 1.9 collective-permute-start.6
  102.2 4.3 %collective-permute-start.7 = (bf16[2,2,768,384]{3,2,1,0:T(8,128)(2,1)S(1)}, bf16[2,2,768,384]{3,2,1,0:T(8,128)(2,1)}, u32[]{:S(2)}, u32[]{:S(2)}) collective-permute-start(bf16[2,2,768,384]{3,2,1,0:T(8,128)(2,1)S(1)} %bitcast.141), channel_id=1, source_target_pairs={{1,0},{3,2},{5,4},{7,6},{17,16},{19,18},{21,20},{23,22},{9,8},{11,... | collective-permute-start | bytes 7077896 | tf_op jit(solution)/shard_map/ppermute | solution.py:72
  106.5 0.8 copy-done.10
  107.3 4.5 %text_queries.1 = (f32[1,256,384]{2,1,0:T(8,128)S(1)}, f32[1,256,384]{2,1,0:T(8,128)S(1)}) custom-call(s32[2]{0:T(128)S(1)} %slice.66.refs_0_, bf16[1,256,384]{2,1,0:T(8,128)(2,1)S(1)} %slice.82.refs_1_, bf16[3,256,384]{2,1,0:T(8,128)(2,1)S(1)} %reshape.332.refs_2_.refs_3_, bf16[3,256,384]{2,1,0:T(8,128)(2,1)S(1)} %reshape.332.refs_2_.refs_3_, ...), custom_call_target="tpu_custom_call" | custom-call | flops 1409286144 | bytes 2752512 | tf_op jit(solution)/shard_map/text_queries/pallas_call | solution.py:183
  113.3 2.0 concatenate.25
  115.3 2.0 concatenate.24
  117.3 2.4 pad_maximum_fusion.2
  119.7 10.8 %all-to-all-start.2 = ((f32[128,2,768]{2,1,0:T(2,128)}), f32[128,2,768]{2,1,0:T(2,128)}, u32[]{:S(2)}, u32[]{:S(2)}) async-start(f32[128,2,768]{2,1,0:T(2,128)} %pad_maximum_fusion.2), calls=%async_computation.2 | async-start | bytes 1572864 | tf_op jit(solution)/shard_map/all_to_all | solution.py:302
  130.6 1.3 copy-done.1
  131.8 20.0 %own_cells.1 = (f32[4,384,384]{2,1,0:T(8,128)S(1)}, f32[4,384,384]{2,1,0:T(8,128)}) custom-call(s32[2]{0:T(128)S(1)} %slice.66.refs_0_, bf16[4,384,384]{2,1,0:T(8,128)(2,1)S(1)} %bitcast.146, bf16[3,256,384]{2,1,0:T(8,128)(2,1)S(1)} %reshape.332.refs_2_.refs_3_, bf16[3,256,384]{2,1,0:T(8,128)(2,1)S(1)} %reshape.332.refs_2_.refs_3_, ...), custom_call_target="tpu_custom_call" | custom-call | flops 8455716864 | bytes 2752512 | tf_op jit(solution)/shard_map/own_cells/pallas_call | solution.py:183
  151.9 1.4 copy-done.12
  153.3 2.1 copy.80
  155.4 1.5 reshape.339
  156.9 3.7 %pad_maximum_fusion.1.refs_4_.refs_5_ = bf16[2,2,768,384]{3,2,1,0:T(8,128)(2,1)} fusion(bf16[1,2,768,384]{3,2,1,0:T(8,128)(2,1)} %bitcast.36, bf16[1,2,768,384]{3,2,1,0:T(8,128)(2,1)} %bitcast.34), kind=kLoop, calls=%fused_computation.5 | loop fusion | flops 1179648 | bytes 4718592 | tf_op jit(solution)/shard_map/stack | solution.py:259
  160.7 2.0 collective-permute-start.10
  162.7 3.5 %collective-permute-start.11 = (bf16[2,2,768,384]{3,2,1,0:T(8,128)(2,1)}, bf16[2,2,768,384]{3,2,1,0:T(8,128)(2,1)}, u32[]{:S(2)}, u32[]{:S(2)}) collective-permute-start(bf16[2,2,768,384]{3,2,1,0:T(8,128)(2,1)} %pad_maximum_fusion.1.refs_4_.refs_5_), channel_id=1, source_target_pairs={{1,0},{3,2},{5,4},{7,6},{17,16},{19,18},{21,20},{23,22},{9,8},{11,... | collective-permute-start | bytes 7077896 | tf_op jit(solution)/shard_map/ppermute | solution.py:72
  166.2 1.3 fusion.21
  167.6 3.0 %copy.81 = f32[4,2,2,4,2,2,1,3,1]{3,0,8,7,6,5,4,2,1:T(4,128)} copy(f32[4,2,2,4,2,2,1,3,1]{8,7,6,4,3,2,1,0,5:T(4,128)} %get-tuple-element.36) | data formatting | bytes 6144 | tf_op jit(solution)/shard_map/slice | solution.py:305
  170.6 1.6 fusion.14
  172.2 2.0 copy.83
  174.2 2.9 %copy.84 = f32[4,2,2,4,2,2,1,3,1]{3,0,8,7,6,5,4,2,1:T(4,128)} copy(f32[4,2,2,4,2,2,1,3,1]{8,7,6,4,3,2,1,0,5:T(4,128)} %get-tuple-element.34) | data formatting | bytes 6144 | tf_op jit(solution)/shard_map/slice | solution.py:306
  177.2 1.2 fusion.12
  178.3 1.4 fusion.6
  181.2 1.0 copy-done.3
  182.2 1.0 copy-done.4
  183.2 30.6 %time_cells.1 = (f32[4,384,384]{2,1,0:T(8,128)S(1)}, f32[4,384,384]{2,1,0:T(8,128)}) custom-call(s32[2]{0:T(128)S(1)} %slice.66.refs_0_, bf16[4,384,384]{2,1,0:T(8,128)(2,1)S(1)} %bitcast.147, f32[4,384,384]{2,1,0:T(8,128)} %copy-done.12, f32[4,384,384]{2,1,0:T(8,128)} %get-tuple-element.9.refs_3_, ...), custom_call_target="tpu_custom_call" | custom-call | flops 14495514624 | bytes 4718592 | tf_op jit(solution)/shard_map/time_cells/pallas_call | solution.py:183
  213.8 25.6 %side_cells.1 = bf16[4,384,384]{2,1,0:T(8,128)(2,1)S(1)} custom-call(s32[2]{0:T(128)S(1)} %slice.66.refs_0_, bf16[4,384,384]{2,1,0:T(8,128)(2,1)S(1)} %bitcast.148, f32[4,384,384]{2,1,0:T(8,128)S(1)} %get-tuple-element.10.refs_2_, f32[4,384,384]{2,1,0:T(8,128)} %get-tuple-element.11.refs_3_, bf16[2,2,768,384]{3,2,1,0:T(8,128)(2,1)} %pad_maximum_fusion.1.refs_4_.refs_5_, ...), custom_call_target="tpu_custom_call" | custom-call | flops 10871635968 | bytes 3538944 | tf_op jit(solution)/shard_map/side_cells/pallas_call | solution.py:183
  239.6 3.1 %collective-permute-start.12 = (bf16[384,384]{1,0:T(8,128)(2,1)S(1)}, bf16[384,384]{1,0:T(8,128)(2,1)S(1)}, u32[]{:S(2)}, u32[]{:S(2)}) collective-permute-start(bf16[384,384]{1,0:T(8,128)(2,1)S(1)} %get-tuple-element.30), channel_id=1, source_target_pairs={{0,3},{1,19},{2,7},{3,23},{4,11},{5,27},{6,15},{7,31},{16,0},{17,1... | collective-permute-start | bytes 884744 | tf_op jit(solution)/shard_map/ppermute | solution.py:72
  242.7 0.8 collective-permute-start.13
  243.6 1.9 convolution_convert_fusion.1
  245.5 1.7 collective-permute-start.14
  247.2 3.3 %collective-permute-start.15 = (bf16[384,384]{1,0:T(8,128)(2,1)S(1)}, bf16[384,384]{1,0:T(8,128)(2,1)S(1)}, u32[]{:S(2)}, u32[]{:S(2)}) collective-permute-start(bf16[384,384]{1,0:T(8,128)(2,1)S(1)} %get-tuple-element.27), channel_id=1, source_target_pairs={{0,0},{1,16},{2,4},{3,20},{4,8},{5,24},{6,12},{7,28},{16,1},{17,17... | collective-permute-start | bytes 884744 | tf_op jit(solution)/shard_map/ppermute | solution.py:72
  250.5 2.2 collective-permute-done.12
  252.7 3.8 %collective-permute-done.13 = bf16[384,384]{1,0:T(8,128)(2,1)S(1)} collective-permute-done((bf16[384,384]{1,0:T(8,128)(2,1)S(1)}, bf16[384,384]{1,0:T(8,128)(2,1)S(1)}, u32[]{:S(2)}, u32[]{:S(2)}) %collective-permute-start.13) | collective-permute-done | bytes 294944 | tf_op jit(solution)/shard_map/ppermute | solution.py:72
  256.5 4.1 %collective-permute-done.14 = bf16[384,384]{1,0:T(8,128)(2,1)S(1)} collective-permute-done((bf16[384,384]{1,0:T(8,128)(2,1)S(1)}, bf16[384,384]{1,0:T(8,128)(2,1)S(1)}, u32[]{:S(2)}, u32[]{:S(2)}) %collective-permute-start.14) | collective-permute-done | bytes 294944 | tf_op jit(solution)/shard_map/ppermute | solution.py:72
  260.6 3.4 %collective-permute-done.15 = bf16[384,384]{1,0:T(8,128)(2,1)S(1)} collective-permute-done((bf16[384,384]{1,0:T(8,128)(2,1)S(1)}, bf16[384,384]{1,0:T(8,128)(2,1)S(1)}, u32[]{:S(2)}, u32[]{:S(2)}) %collective-permute-start.15) | collective-permute-done | bytes 294944 | tf_op jit(solution)/shard_map/ppermute | solution.py:72
  265.3 8.9 %fusion = bf16[1,1,1,384,3072]{4,3,2,1,0:T(8,128)(2,1)} fusion(bf16[384,1536]{0,1:T(8,128)(2,1)S(1)} %bitcast.164, bf16[1536,3072]{1,0:T(8,128)(2,1)} %param.18), kind=kOutput, calls=%fused_computation.1 | convolution fusion | flops 3625058304 | bytes 12976128 | tf_op jit(solution)/shard_map/dot_general | solution.py:348
  (130 shorter events, 13.5 us)
Async XLA Ops:
  4.3 8.4 %copy-start.16 = (s32[1,16,27]{2,1,0:T(8,128)S(1)}, s32[1,16,27]{2,1,0:T(8,128)}, u32[]{:S(2)}) copy-start(s32[1,16,27]{2,1,0:T(8,128)} %param.16) | copy-start | bytes 5188
  4.3 8.6 %copy-start.17 = (bf16[2,1536]{1,0:T(2,128)(2,1)S(1)}, bf16[2,1536]{1,0:T(2,128)(2,1)}, u32[]{:S(2)}) copy-start(bf16[2,1536]{1,0:T(2,128)(2,1)} %param.15) | copy-start | bytes 18436
  4.3 8.6 %copy-start.18 = (bf16[2,1536]{1,0:T(2,128)(2,1)S(1)}, bf16[2,1536]{1,0:T(2,128)(2,1)}, u32[]{:S(2)}) copy-start(bf16[2,1536]{1,0:T(2,128)(2,1)} %param.14) | copy-start | bytes 18436
  4.3 8.6 %copy-start.19 = (bf16[2,1536]{1,0:T(2,128)(2,1)S(1)}, bf16[2,1536]{1,0:T(2,128)(2,1)}, u32[]{:S(2)}) copy-start(bf16[2,1536]{1,0:T(2,128)(2,1)} %param.13) | copy-start | bytes 18436
  4.3 9.3 %copy-start.15 = (bf16[6,1,64,1536]{3,2,1,0:T(8,128)(2,1)S(1)}, bf16[6,1,64,1536]{3,2,1,0:T(8,128)(2,1)}, u32[]{:S(2)}) copy-start(bf16[6,1,64,1536]{3,2,1,0:T(8,128)(2,1)} %param.12) | copy-start | bytes 3538948
  4.3 24.3 %all-to-all-start = ((bf16[16,96,384]{2,1,0:T(8,128)(2,1)}), bf16[16,96,384]{2,1,0:T(8,128)(2,1)S(1)}, u32[]{:S(2)}, u32[]{:S(2)}) async-start(bf16[16,96,384]{2,1,0:T(8,128)(2,1)} %bitcast.1), calls=%async_computation | async-start | bytes 2359296 | tf_op jit(solution)/shard_map/all_to_all | solution.py:76
  21.5 15.1 %copy-start.20 = (s32[8]{0:T(128)S(1)}, s32[8]{0:T(128)}, u32[]{:S(2)}) copy-start(s32[8]{0:T(128)} %param.17) | copy-start | bytes 100
  28.7 1.0 copy-start.14
  29.7 39.1 %all-to-all-start.1 = ((bf16[16,200,384]{2,1,0:T(8,128)(2,1)}), bf16[16,200,384]{2,1,0:T(8,128)(2,1)S(1)}, u32[]{:S(2)}, u32[]{:S(2)}) async-start(bf16[16,200,384]{2,1,0:T(8,128)(2,1)} %pad_maximum_fusion), calls=%async_computation.1 | async-start | bytes 4915200 | tf_op jit(solution)/shard_map/all_to_all | solution.py:76
  38.2 2.2 collective-permute-start
  68.8 2.7 collective-permute-start.1
  71.6 7.4 %collective-permute-start.2 = (bf16[2,16,6,384]{3,2,1,0:T(8,128)(2,1)S(1)}, bf16[2,16,6,384]{3,2,1,0:T(8,128)(2,1)S(1)}, u32[]{:S(2)}, u32[]{:S(2)}) collective-permute-start(bf16[2,16,6,384]{3,2,1,0:T(8,128)(2,1)S(1)} %pad_maximum_fusion.4), channel_id=1, source_target_pairs={{0,96},{1,97},{2,98},{3,99},{4,100},{5,101},{6,102},{7,103},{16,11... | collective-permute-start | bytes 442376 | tf_op jit(solution)/shard_map/ppermute | solution.py:72
  72.3 14.6 %collective-permute-start.5 = (bf16[2,4,2,6,2,8,384]{6,5,4,3,2,1,0:T(8,128)(2,1)S(1)}, bf16[2,4,2,6,2,8,384]{6,5,4,3,2,1,0:T(8,128)(2,1)S(1)}, u32[]{:S(2)}, u32[]{:S(2)}) collective-permute-start(bf16[2,4,2,6,2,8,384]{6,5,4,3,2,1,0:T(8,128)(2,1)S(1)} %dynamic-slice_bitcast_fusion.1), channel_id=1, source_target_pairs={{0,1},{1,0},{2,3},{3,2},{4,5},{5,4},{6,7},{7,6},{16,17},{17,16},{1... | collective-permute-start | bytes 3538952 | tf_op jit(solution)/shard_map/ppermute | solution.py:72
  73.6 10.6 %collective-permute-start.3 = (bf16[2,16,6,384]{3,2,1,0:T(8,128)(2,1)S(1)}, bf16[2,16,6,384]{3,2,1,0:T(8,128)(2,1)S(1)}, u32[]{:S(2)}, u32[]{:S(2)}) collective-permute-start(bf16[2,16,6,384]{3,2,1,0:T(8,128)(2,1)S(1)} %pad_maximum_fusion.4), channel_id=1, source_target_pairs={{0,64},{1,65},{2,66},{3,67},{4,68},{5,69},{6,70},{7,71},{16,80},{1... | collective-permute-start | bytes 442376 | tf_op jit(solution)/shard_map/ppermute | solution.py:72
  76.2 10.4 %collective-permute-start.4 = (bf16[2,16,6,384]{3,2,1,0:T(8,128)(2,1)S(1)}, bf16[2,16,6,384]{3,2,1,0:T(8,128)(2,1)S(1)}, u32[]{:S(2)}, u32[]{:S(2)}) collective-permute-start(bf16[2,16,6,384]{3,2,1,0:T(8,128)(2,1)S(1)} %pad_maximum_fusion.4), channel_id=1, source_target_pairs={{0,32},{1,33},{2,34},{3,35},{4,36},{5,37},{6,38},{7,39},{16,48},{1... | collective-permute-start | bytes 442376 | tf_op jit(solution)/shard_map/ppermute | solution.py:72
  87.8 18.6 %copy-start = (bf16[2,2,2,6,4,2,8,384]{7,6,5,4,3,2,1,0:T(8,128)(2,1)}, bf16[2,2,2,6,4,2,8,384]{7,6,5,4,3,2,1,0:T(8,128)(2,1)S(1)}, u32[]{:S(2)}) copy-start(bf16[2,2,2,6,4,2,8,384]{7,6,5,4,3,2,1,0:T(8,128)(2,1)S(1)} %copy.75) | copy-start | bytes 7077892
  89.7 67.2 %collective-permute-start.9 = (bf16[2,768,384]{2,1,0:T(8,128)(2,1)}, bf16[2,768,384]{2,1,0:T(8,128)(2,1)}, u32[]{:S(2)}, u32[]{:S(2)}) collective-permute-start(bf16[2,768,384]{2,1,0:T(8,128)(2,1)} %get-tuple-element.21), channel_id=1, source_target_pairs={{2,0},{3,1},{4,2},{5,3},{6,4},{7,5},{18,16},{19,17},{20,18},{21,19... | collective-permute-start | bytes 3538952 | tf_op jit(solution)/shard_map/ppermute | solution.py:72
  92.8 64.1 %collective-permute-start.8 = (bf16[2,768,384]{2,1,0:T(8,128)(2,1)}, bf16[2,768,384]{2,1,0:T(8,128)(2,1)}, u32[]{:S(2)}, u32[]{:S(2)}) collective-permute-start(bf16[2,768,384]{2,1,0:T(8,128)(2,1)} %get-tuple-element.20), channel_id=1, source_target_pairs={{0,2},{1,3},{2,4},{3,5},{4,6},{5,7},{16,18},{17,19},{18,20},{19,21... | collective-permute-start | bytes 3538952 | tf_op jit(solution)/shard_map/ppermute | solution.py:72
  100.2 80.9 %collective-permute-start.6 = (bf16[2,2,768,384]{3,2,1,0:T(8,128)(2,1)S(1)}, bf16[2,2,768,384]{3,2,1,0:T(8,128)(2,1)}, u32[]{:S(2)}, u32[]{:S(2)}) collective-permute-start(bf16[2,2,768,384]{3,2,1,0:T(8,128)(2,1)S(1)} %bitcast.140), channel_id=1, source_target_pairs={{0,1},{1,32},{2,3},{3,34},{4,5},{5,36},{6,7},{7,38},{16,17},{17,48... | collective-permute-start | bytes 7077896 | tf_op jit(solution)/shard_map/ppermute | solution.py:72
  102.2 79.0 %collective-permute-start.7 = (bf16[2,2,768,384]{3,2,1,0:T(8,128)(2,1)S(1)}, bf16[2,2,768,384]{3,2,1,0:T(8,128)(2,1)}, u32[]{:S(2)}, u32[]{:S(2)}) collective-permute-start(bf16[2,2,768,384]{3,2,1,0:T(8,128)(2,1)S(1)} %bitcast.141), channel_id=1, source_target_pairs={{1,0},{3,2},{5,4},{7,6},{17,16},{19,18},{21,20},{23,22},{9,8},{11,... | collective-permute-start | bytes 7077896 | tf_op jit(solution)/shard_map/ppermute | solution.py:72
  106.5 0.8 copy-start.10
  111.8 0.8 copy-start.8
  112.6 0.8 copy-start.9
  117.3 13.3 %copy-start.11 = (bf16[256,128]{1,0:T(8,128)(2,1)S(1)}, bf16[256,128]{1,0:T(8,128)(2,1)}, u32[]{:S(2)}) copy-start(bf16[256,128]{1,0:T(8,128)(2,1)} %select_convert_fusion.refs_4_) | copy-start | bytes 196612
  119.7 33.6 %all-to-all-start.2 = ((f32[128,2,768]{2,1,0:T(2,128)}), f32[128,2,768]{2,1,0:T(2,128)}, u32[]{:S(2)}, u32[]{:S(2)}) async-start(f32[128,2,768]{2,1,0:T(2,128)} %pad_maximum_fusion.2), calls=%async_computation.2 | async-start | bytes 1572864 | tf_op jit(solution)/shard_map/all_to_all | solution.py:302
  130.6 1.3 copy-start.1
  151.9 1.4 copy-start.12
  156.9 9.3 %copy-start.13 = (f32[4,2,2,4,2,2,2,3,128]{8,7,6,4,3,2,1,0,5:T(4,128)}, f32[4,2,2,4,2,2,2,3,128]{8,7,6,4,3,2,1,0,5:T(4,128)S(1)}, u32[]{:S(2)}) copy-start(f32[4,2,2,4,2,2,2,3,128]{8,7,6,4,3,2,1,0,5:T(4,128)S(1)} %reshape.339) | copy-start | bytes 2359300
  160.7 53.1 %collective-permute-start.10 = (bf16[2,2,768,384]{3,2,1,0:T(8,128)(2,1)}, bf16[2,2,768,384]{3,2,1,0:T(8,128)(2,1)}, u32[]{:S(2)}, u32[]{:S(2)}) collective-permute-start(bf16[2,2,768,384]{3,2,1,0:T(8,128)(2,1)} %pad_maximum_fusion.1.refs_4_.refs_5_), channel_id=1, source_target_pairs={{0,1},{1,32},{2,3},{3,34},{4,5},{5,36},{6,7},{7,38},{16,17},{17,48... | collective-permute-start | bytes 7077896 | tf_op jit(solution)/shard_map/ppermute | solution.py:72
  162.7 51.1 %collective-permute-start.11 = (bf16[2,2,768,384]{3,2,1,0:T(8,128)(2,1)}, bf16[2,2,768,384]{3,2,1,0:T(8,128)(2,1)}, u32[]{:S(2)}, u32[]{:S(2)}) collective-permute-start(bf16[2,2,768,384]{3,2,1,0:T(8,128)(2,1)} %pad_maximum_fusion.1.refs_4_.refs_5_), channel_id=1, source_target_pairs={{1,0},{3,2},{5,4},{7,6},{17,16},{19,18},{21,20},{23,22},{9,8},{11,... | collective-permute-start | bytes 7077896 | tf_op jit(solution)/shard_map/ppermute | solution.py:72
  167.6 13.6 %copy-start.2 = (bf16[2,2,6,4,2,8,384]{6,5,4,3,2,1,0:T(8,128)(2,1)S(1)}, bf16[2,2,6,4,2,8,384]{6,5,4,3,2,1,0:T(8,128)(2,1)}, u32[]{:S(2)}) copy-start(bf16[2,2,6,4,2,8,384]{6,5,4,3,2,1,0:T(8,128)(2,1)} %copy.69) | copy-start | bytes 3538948
  181.2 1.0 copy-start.3
  182.2 1.0 copy-start.4
  183.2 30.6 %copy-start.5 = (bf16[1,2,768,128]{3,2,1,0:T(8,128)(2,1)S(1)}, bf16[1,2,768,128]{3,2,1,0:T(8,128)(2,1)}, u32[]{:S(2)}) copy-start(bf16[1,2,768,128]{3,2,1,0:T(8,128)(2,1)} %get-tuple-element.31.refs_12_) | copy-start | bytes 1179652
  183.2 30.6 %copy-start.6 = (bf16[1,2,768,128]{3,2,1,0:T(8,128)(2,1)S(1)}, bf16[1,2,768,128]{3,2,1,0:T(8,128)(2,1)}, u32[]{:S(2)}) copy-start(bf16[1,2,768,128]{3,2,1,0:T(8,128)(2,1)} %get-tuple-element.32.refs_6_) | copy-start | bytes 1179652
  183.2 30.6 %copy-start.7 = (bf16[1,2,768,128]{3,2,1,0:T(8,128)(2,1)S(1)}, bf16[1,2,768,128]{3,2,1,0:T(8,128)(2,1)}, u32[]{:S(2)}) copy-start(bf16[1,2,768,128]{3,2,1,0:T(8,128)(2,1)} %get-tuple-element.33.refs_9_) | copy-start | bytes 1179652
  183.2 60.4 %slice-start = ((s8[9437184]{0:T(1024)(128)(4,1)}), s8[4194304]{0:T(1024)(128)(4,1)S(1)}, s32[]{:S(2)}) async-start(s8[9437184]{0:T(1024)(128)(4,1)} %bitcast.149), calls=%async_computation.3 | async-start | bytes 8388608
  183.2 60.4 %slice-start.1 = ((s8[9437184]{0:T(1024)(128)(4,1)}), s8[4194304]{0:T(1024)(128)(4,1)S(1)}, s32[]{:S(2)}) async-start(s8[9437184]{0:T(1024)(128)(4,1)} %bitcast.149), calls=%async_computation.4 | async-start | bytes 8388608
  213.8 29.7 %slice-start.2 = ((s8[9437184]{0:T(1024)(128)(4,1)}), s8[1048576]{0:T(1024)(128)(4,1)S(1)}, s32[]{:S(2)}) async-start(s8[9437184]{0:T(1024)(128)(4,1)} %bitcast.149), calls=%async_computation.5 | async-start | bytes 2097152
  239.6 13.0 %collective-permute-start.12 = (bf16[384,384]{1,0:T(8,128)(2,1)S(1)}, bf16[384,384]{1,0:T(8,128)(2,1)S(1)}, u32[]{:S(2)}, u32[]{:S(2)}) collective-permute-start(bf16[384,384]{1,0:T(8,128)(2,1)S(1)} %get-tuple-element.30), channel_id=1, source_target_pairs={{0,3},{1,19},{2,7},{3,23},{4,11},{5,27},{6,15},{7,31},{16,0},{17,1... | collective-permute-start | bytes 884744 | tf_op jit(solution)/shard_map/ppermute | solution.py:72
  242.7 13.8 %collective-permute-start.13 = (bf16[384,384]{1,0:T(8,128)(2,1)S(1)}, bf16[384,384]{1,0:T(8,128)(2,1)S(1)}, u32[]{:S(2)}, u32[]{:S(2)}) collective-permute-start(bf16[384,384]{1,0:T(8,128)(2,1)S(1)} %get-tuple-element.29), channel_id=1, source_target_pairs={{0,2},{1,18},{2,6},{3,22},{4,10},{5,26},{6,14},{7,30},{16,3},{17,1... | collective-permute-start | bytes 884744 | tf_op jit(solution)/shard_map/ppermute | solution.py:72
  245.5 15.1 %collective-permute-start.14 = (bf16[384,384]{1,0:T(8,128)(2,1)S(1)}, bf16[384,384]{1,0:T(8,128)(2,1)S(1)}, u32[]{:S(2)}, u32[]{:S(2)}) collective-permute-start(bf16[384,384]{1,0:T(8,128)(2,1)S(1)} %get-tuple-element.28), channel_id=1, source_target_pairs={{0,1},{1,17},{2,5},{3,21},{4,9},{5,25},{6,13},{7,29},{16,2},{17,18... | collective-permute-start | bytes 884744 | tf_op jit(solution)/shard_map/ppermute | solution.py:72
  247.2 16.8 %collective-permute-start.15 = (bf16[384,384]{1,0:T(8,128)(2,1)S(1)}, bf16[384,384]{1,0:T(8,128)(2,1)S(1)}, u32[]{:S(2)}, u32[]{:S(2)}) collective-permute-start(bf16[384,384]{1,0:T(8,128)(2,1)S(1)} %get-tuple-element.27), channel_id=1, source_target_pairs={{0,0},{1,16},{2,4},{3,20},{4,8},{5,24},{6,12},{7,28},{16,1},{17,17... | collective-permute-start | bytes 884744 | tf_op jit(solution)/shard_map/ppermute | solution.py:72

commit v2 on v1

v2 whole, which is shorter than its diff:
```python
import functools
import math

import jax
import jax.numpy as jnp
from jax import lax
from jax.experimental import pallas as pl
from jax.experimental.pallas import tpu as pltpu
from jax.sharding import PartitionSpec as P

HD = 128
TF = 6
TC = 8
TILE = 384
CELL = 2 * TILE
PIECE = TF * TC
GW = 384
GH = GW // HD
TXT = 256
EXTRA = 16
COLUMNS = 512
AXES = ("tm", "space")
SCALE = HD**-0.5 * math.log2(math.e)
MASKED = -1e30
TEXT_LANE = 4
CONTRACT_LAST = (((1,), (1,)), ((), ()))


def device(y, z, x, c):
    return (2 * y + z % 2) * 16 + 8 * (z // 2) + 2 * x + c


PLACES = [(y, z, x, c) for y in range(4) for z in range(4) for x in range(4) for c in range(2)]
PLANES = [
    [device(y, z, x, c) for z in range(4) for x in range(4)] for y in range(4) for c in range(2)
]


SAME_PLACE = [
    [device(y, z, x, c) for y in range(4) for c in range(2)] for z in range(4) for x in range(4)
]


def route(target):
    pairs = []
    for place in PLACES:
        goal = target(*place)
        if goal is not None:
            pairs.append((device(*place), device(*goal)))
    return pairs


def in_time(steps):
    def target(y, z, x, c):
        moment = 2 * y + c + steps
        return (moment // 2, z, x, moment % 2) if 0 <= moment < 8 else None

    return route(target)


def in_columns(steps):
    return route(lambda y, z, x, c: (y, z, x + steps, c) if 0 <= x + steps < 4 else None)


def to_owner(turn):
    def target(y, z, x, c):
        tile = (z + turn) % 4
        return (y, 2 * (x // 2) + c, 2 * (x % 2) + tile // 2, tile % 2)

    return route(target)


OTHER_CORE = route(lambda y, z, x, c: (y, z, x, 1 - c))


TIME_PARTNER = route(lambda y, z, x, c: (y, z ^ 1, x, c))


def send(value, pairs):
    return lax.ppermute(value, AXES, pairs)


def exchange(value, groups):
    return lax.all_to_all(
        value, AXES, split_axis=0, concat_axis=0, tiled=True, axis_index_groups=groups
    )


def pack_kernel(k_ref, v_ref, out_ref):
    for p in range(4):
        columns = slice(2 * TC * p, 2 * TC * (p + 1))
        for kind, ref in enumerate((k_ref, v_ref)):
            cut = ref[:, columns, :].astype(jnp.float32).reshape(TF, 2, TC, GW)
            for w in range(2):
                piece = cut[:, w].reshape(PIECE, GW).astype(jnp.bfloat16)
                out_ref[p, (2 * w + kind) * PIECE : (2 * w + kind + 1) * PIECE] = piece


def pack_queries_kernel(q_ref, text_ref, out_ref):
    for p in range(4):
        rows = q_ref[:, 2 * TC * p : 2 * TC * (p + 1), :].reshape(2 * PIECE, GW)
        out_ref[p, : 2 * PIECE] = rows
        out_ref[p, 2 * PIECE :] = text_ref[...]


def pack(kernel, rows, rasters, *text):
    raster = pl.BlockSpec((TF, 8 * TC, GW), lambda g: (0, 0, g))
    text_spec = pl.BlockSpec((PIECE, GW), lambda g: (0, g))
    return pl.pallas_call(
        kernel,
        grid=(4,),
        in_specs=[raster] * len(rasters) + [text_spec] * len(text),
        out_specs=pl.BlockSpec((4, rows, GW), lambda g: (g, 0, 0)),
        out_shape=jax.ShapeDtypeStruct((16, rows, GW), jnp.bfloat16),
        compiler_params=pltpu.CompilerParams(vmem_limit_bytes=56 * 2**20),
        cost_estimate=pl.CostEstimate(flops=0, bytes_accessed=16 * rows * GW * 4, transcendentals=0),
        name="pack",
    )(*[array.reshape(TF, 8 * TC, 4 * GW) for array in rasters], *text)


def merge_sides_kernel(c_ref, mine_ref, other_ref, low_ref, high_ref):
    for x in range(4):
        for part, get in enumerate((lambda s: mine_ref[0, 0, x, s], lambda s: other_ref[0, x, s])):
            for w, ref in enumerate((low_ref, high_ref)):
                for kind in range(2):
                    start = (2 * x + part) * PIECE
                    rows = slice((2 * w + kind) * PIECE, (2 * w + kind + 1) * PIECE)
                    ref[kind, start : start + PIECE] = get(rows)


def merge_kernel(c_ref, mine_ref, other_ref, own_ref):
    for x in range(4):
        for part, get in enumerate((lambda s: mine_ref[0, 0, x, s], lambda s: other_ref[0, x, s])):
            for w in range(2):
                for kind in range(2):
                    start = (2 * x + part) * PIECE
                    rows = slice((2 * w + kind) * PIECE, (2 * w + kind + 1) * PIECE)
                    own_ref[kind, w, start : start + PIECE] = get(rows)


def merge_queries_kernel(c_ref, mine_ref, other_ref, q_ref):
    even_core = c_ref[0] == 0
    for x in range(4):
        for f in range(TF):
            rows = slice(2 * TC * f, 2 * TC * (f + 1))
            mine = mine_ref[0, 0, x, rows].astype(jnp.float32)
            other = other_ref[0, x, rows].astype(jnp.float32)
            even = jnp.where(even_core, mine, other)
            odd = jnp.where(even_core, other, mine)
            start = (4 * f + x) * 2 * TC
            for w in range(2):
                both = [part[w * TC : (w + 1) * TC] for part in (even, odd)]
                q_ref[w, 0, start : start + 2 * TC] = jnp.concatenate(both).astype(jnp.bfloat16)


def from_other_core(core, got):
    rows = got.shape[1]
    pieces = got.reshape(2, 2, 4, rows, GW)
    other = send(lax.dynamic_index_in_dim(pieces, 1 - core[0], 1, keepdims=False), OTHER_CORE)
    return pieces, other


def merge(core, pieces, other, kernel, out_specs, out_shape):
    rows = pieces.shape[3]
    return pl.pallas_call(
        kernel,
        grid_spec=pltpu.PrefetchScalarGridSpec(
            num_scalar_prefetch=1,
            grid=(2,),
            in_specs=[
                pl.BlockSpec((1, 1, 4, rows, GW), lambda b, c: (b, c[0], 0, 0, 0)),
                pl.BlockSpec((1, 4, rows, GW), lambda b, c: (b, 0, 0, 0)),
            ],
            out_specs=out_specs,
        ),
        out_shape=out_shape,
        compiler_params=pltpu.CompilerParams(vmem_limit_bytes=56 * 2**20),
        cost_estimate=pl.CostEstimate(flops=0, bytes_accessed=16 * rows * GW * 4, transcendentals=0),
        name="merge",
    )(core, pieces, other)


def merge_sides(core, pieces, other):
    cell = pl.BlockSpec((2, TILE, GW), lambda b, c: (0, b, 0))
    shape = jax.ShapeDtypeStruct((2, CELL, GW), jnp.bfloat16)
    return merge(core, pieces, other, merge_sides_kernel, [cell, cell], [shape, shape])


def merge_keys(core, pieces, other):
    both = pl.BlockSpec((2, 2, TILE, GW), lambda b, c: (0, 0, b, 0))
    shape = jax.ShapeDtypeStruct((2, 2, CELL, GW), jnp.bfloat16)
    return merge(core, pieces, other, merge_kernel, both, shape)


def merge_queries(core, pieces, other):
    spec = pl.BlockSpec((2, 1, TILE, GW), lambda b, c: (0, b, 0, 0))
    shape = jax.ShapeDtypeStruct((2, 2, TILE, GW), jnp.bfloat16)
    return merge(core, pieces, other, merge_queries_kernel, spec, shape)


def join_kernel(left_ref, right_ref, out_ref):
    out_ref[:, 0] = left_ref[...]
    out_ref[:, 1] = right_ref[...]


def join(left, right):
    half = pl.BlockSpec((1, CELL, GW), lambda k: (k, 0, 0))
    return pl.pallas_call(
        join_kernel,
        grid=(2,),
        in_specs=[half, half],
        out_specs=pl.BlockSpec((1, 2, CELL, GW), lambda k: (k, 0, 0, 0)),
        out_shape=jax.ShapeDtypeStruct((2, 2, CELL, GW), jnp.bfloat16),
        compiler_params=pltpu.CompilerParams(vmem_limit_bytes=56 * 2**20),
        cost_estimate=pl.CostEstimate(flops=0, bytes_accessed=16 * CELL * GW, transcendentals=0),
        name="join",
    )(left, right)


def project_kernel(from_ref, first, second, third, fourth, weight_ref, out_ref, whole_ref):
    @pl.when(pl.program_id(0) == 0)
    def _():
        for i, ref in enumerate((first, second, third, fourth)):
            whole_ref[:, pl.ds(pl.multiple_of(from_ref[i] * GW, GW), GW)] = ref[...]

    columns = pl.ds(pl.multiple_of(pl.program_id(0) * COLUMNS, COLUMNS), COLUMNS)
    out_ref[...] = jnp.dot(
        whole_ref[...], weight_ref[:, columns], preferred_element_type=jnp.float32
    ).astype(jnp.bfloat16)


def project(groups, parts, weight):
    depth, width = weight.shape
    part = pl.BlockSpec((TILE, GW), lambda n, groups: (0, 0))
    return pl.pallas_call(
        project_kernel,
        grid_spec=pltpu.PrefetchScalarGridSpec(
            num_scalar_prefetch=1,
            grid=(width // COLUMNS,),
            in_specs=[part] * 4 + [pl.BlockSpec(memory_space=pltpu.VMEM)],
            out_specs=pl.BlockSpec((TILE, COLUMNS), lambda n, groups: (0, n)),
            scratch_shapes=[pltpu.VMEM((TILE, depth), jnp.bfloat16)],
        ),
        out_shape=jax.ShapeDtypeStruct((TILE, width), jnp.bfloat16),
        compiler_params=pltpu.CompilerParams(vmem_limit_bytes=24 * 2**20),
        cost_estimate=pl.CostEstimate(
            flops=2 * TILE * depth * width, bytes_accessed=2 * depth * width, transcendentals=0
        ),
        name="project",
    )(groups, *parts, weight)


def wide_bias(table):
    halves = [
        jnp.broadcast_to(table[b][None], (TILE // EXTRA, EXTRA, HD)).reshape(TILE, HD)
        for b in range(2)
    ]
    return jnp.concatenate(halves)


def add_keys(query, state, keys, bias, values):
    ones = jnp.ones((keys.shape[0], HD), jnp.bfloat16)
    scores = lax.dot_general(
        query,
        jnp.concatenate([keys, bias], axis=1),
        CONTRACT_LAST,
        preferred_element_type=jnp.float32,
    )
    top = jnp.max(scores, axis=1, keepdims=True)
    if state is not None:
        top = jnp.maximum(top, state[0])
    weights = jnp.exp2((scores - top) * SCALE).astype(jnp.bfloat16)
    part = jnp.dot(
        weights, jnp.concatenate([values, ones], axis=1), preferred_element_type=jnp.float32
    )
    if state is not None:
        part = part + state[1] * jnp.exp2((state[0] - top) * SCALE)
    return top, part


def widened(query, first_lane):
    rows = query.shape[0]
    lanes = lax.broadcasted_iota(jnp.int32, (rows, HD), 1)
    which = lax.broadcasted_iota(jnp.int32, (rows, HD), 0) // TILE
    hot = jnp.where(lanes == first_lane + which, 1.0, 0.0).astype(jnp.bfloat16)
    return jnp.concatenate([query, hot], axis=1)


def mark_of(state):
    rows = state[1].shape[0]
    lanes = lax.broadcasted_iota(jnp.int32, (rows, HD), 1)
    return jnp.where(lanes < HD // 2, jnp.broadcast_to(state[0], (rows, HD)), state[1][:, HD:])


def near_kernel(cells, q_ref, tk_ref, tv_ref, bias_ref, *refs):
    sum_ref, mark_ref = refs[2 * cells :]
    no_bias = jnp.zeros((TXT, HD), jnp.bfloat16)
    for w in range(2):
        query = widened(q_ref[w].reshape(CELL, HD), 2 * w)
        state = add_keys(query, None, tk_ref[0], no_bias, tv_ref[0])
        for i in range(2 * cells):
            bias = wide_bias(bias_ref[i])
            keys, values = refs[2 * (i // 2)], refs[2 * (i // 2) + 1]
            state = add_keys(query, state, keys[0, i % 2], bias, values[0, i % 2])
        sum_ref[w] = state[1][:, :HD]
        mark_ref[w] = mark_of(state)


def cell_specs(number):
    def spec(kind):
        return pl.BlockSpec((1, 2, CELL, HD), lambda h: (kind, 0, 0, h))

    return [spec(0), spec(1)] * number


def doubled(cells):
    return [array for cell in cells for array in (cell, cell)]


def cost(rows, keys, heads):
    return pl.CostEstimate(
        flops=rows * keys * heads * 4 * 384,
        bytes_accessed=4 * keys * heads * HD,
        transcendentals=rows * keys * heads,
    )


def near(queries, text_all, bias, cells):
    state = pl.BlockSpec((2, CELL, HD), lambda h: (0, 0, h))
    shape = jax.ShapeDtypeStruct((2, CELL, GW), jnp.float32)
    return pl.pallas_call(
        functools.partial(near_kernel, len(cells)),
        grid=(GH,),
        in_specs=[
            pl.BlockSpec((2, 2, TILE, HD), lambda h: (0, 0, 0, h)),
            pl.BlockSpec((1, TXT, HD), lambda h: (1, 0, h)),
            pl.BlockSpec((1, TXT, HD), lambda h: (2, 0, h)),
            pl.BlockSpec(bias.shape, lambda h: (0, 0, 0, 0)),
        ]
        + cell_specs(len(cells)),
        out_specs=[state, state],
        out_shape=[shape, shape],
        compiler_params=pltpu.CompilerParams(vmem_limit_bytes=40 * 2**20),
        cost_estimate=cost(2 * CELL, 2 * len(cells) * CELL + TXT, GH),
        name="near_cells",
    )(queries, text_all, text_all, bias, *doubled(cells))


def side_kernel(valid_ref, q_ref, sum_ref, mark_ref, bias_ref, *refs):
    out_ref = refs[6]
    row = lax.broadcasted_iota(jnp.int32, (CELL, HD), 0)
    for w in range(2):
        query = widened(q_ref[w].reshape(CELL, HD), 2 * w)
        mark = mark_ref[w]
        totals = jnp.broadcast_to(mark[:, HD // 2 : HD // 2 + 1], (CELL, HD))
        state = (mark[:, :1], jnp.concatenate([sum_ref[w], totals], axis=1))
        for i in range(3):
            bias = wide_bias(bias_ref[3 * w + i])
            state = add_keys(query, state, refs[2 * i][0, w], bias, refs[2 * i + 1][0, w])
        value = state[1][:, :HD] / state[1][:, HD:]
        value = jnp.where(row % TC < valid_ref[w], value, 0.0).astype(jnp.bfloat16)
        out_ref[w] = value.reshape(2, TILE, HD)


def side(valid, queries, state, bias, cells):
    tall = pl.BlockSpec((2, CELL, HD), lambda h: (0, 0, h))
    query = pl.BlockSpec((2, 2, TILE, HD), lambda h: (0, 0, 0, h))
    return pl.pallas_call(
        side_kernel,
        grid=(GH,),
        in_specs=[
            pl.BlockSpec(memory_space=pltpu.SMEM),
            query,
            tall,
            tall,
            pl.BlockSpec(bias.shape, lambda h: (0, 0, 0, 0)),
        ]
        + cell_specs(3),
        out_specs=query,
        out_shape=jax.ShapeDtypeStruct((2, 2, TILE, GW), jnp.bfloat16),
        compiler_params=pltpu.CompilerParams(vmem_limit_bytes=40 * 2**20),
        cost_estimate=cost(2 * CELL, 3 * CELL, GH),
        name="side_cells",
    )(valid, queries, *state, bias, *doubled(cells))


def text_kernel(share_ref, q_ref, tk_ref, tv_ref, bias_ref, *refs):
    out_ref = refs[2]
    head = pl.program_id(0)
    lanes = lax.broadcasted_iota(jnp.int32, (TXT, HD), 1)
    rows = lax.broadcasted_iota(jnp.int32, (TXT, HD), 0)
    hot = jnp.where(lanes == TEXT_LANE, 1.0, 0.0).astype(jnp.bfloat16)
    query = jnp.concatenate([q_ref[0], hot], axis=1)
    share = jnp.where(rows // 8 == share_ref[0], 0.0, MASKED).astype(jnp.bfloat16)
    state = None
    for i in range(2):
        bias = wide_bias(bias_ref[i])
        state = add_keys(query, state, refs[0][0, i], bias, refs[1][0, i])
    state = add_keys(query, state, tk_ref[0], share, tv_ref[0])
    out_ref[:, pl.ds(pl.multiple_of(head * HD, HD), HD)] = state[1][:, :HD]
    mark = jnp.where(
        lanes % 8 == head, jnp.where(lanes < 8, state[0], state[1][:, HD:]), 0.0
    )

    @pl.when(head == 0)
    def _():
        out_ref[:, GW:] = mark

    @pl.when(head > 0)
    def _():
        out_ref[:, GW:] += mark


def text_part(share, text_all, bias, cells):
    def spec(kind):
        return pl.BlockSpec((1, TXT, HD), lambda h: (kind, 0, h))

    return pl.pallas_call(
        text_kernel,
        grid=(GH,),
        in_specs=[
            pl.BlockSpec(memory_space=pltpu.SMEM),
            spec(0),
            spec(1),
            spec(2),
            pl.BlockSpec(bias.shape, lambda h: (0, 0, 0, 0)),
        ]
        + cell_specs(1),
        out_specs=pl.BlockSpec((TXT, GW + HD), lambda h: (0, 0)),
        out_shape=jax.ShapeDtypeStruct((TXT, GW + HD), jnp.float32),
        compiler_params=pltpu.CompilerParams(vmem_limit_bytes=56 * 2**20),
        cost_estimate=cost(TXT, 2 * CELL + TXT, GH),
        name="text_queries",
    )(share, text_all, text_all, text_all, bias, *doubled(cells))


def text_sum_kernel(part_ref, out_ref):
    for z in range(4):
        marks = part_ref[:, z % 2, z // 2, :, :, GW:]
        top = jnp.max(marks, axis=(0, 1), keepdims=True)
        factors = jnp.exp2((marks - top) * SCALE)
        for h in range(GH):
            factor = factors[..., h : h + 1]
            total = jnp.sum(marks[..., 8 + h : 9 + h] * factor, axis=(0, 1))
            part = part_ref[:, z % 2, z // 2, :, :, h * HD : (h + 1) * HD]
            summed = jnp.sum(part * factor, axis=(0, 1)) / total
            start = z * GW + h * HD
            out_ref[:, start : start + HD] = summed.astype(jnp.bfloat16)


def text_sum(parts):
    return pl.pallas_call(
        text_sum_kernel,
        out_shape=jax.ShapeDtypeStruct((2, 4 * GW), jnp.bfloat16),
        compiler_params=pltpu.CompilerParams(vmem_limit_bytes=56 * 2**20),
        cost_estimate=pl.CostEstimate(
            flops=0, bytes_accessed=TXT * (GW + HD) * 4, transcendentals=0
        ),
        name="text_sum",
    )(parts.reshape(4, 2, 2, 8, 2, GW + HD))


def shards(
    video_query,
    video_key,
    video_value,
    text_query,
    text_key,
    text_value,
    window_lists,
    valid_columns,
    video_weight,
    text_weight,
):
    tm, space = lax.axis_index("tm"), lax.axis_index("space")
    y, zl = tm // 2, tm % 2
    zh, x, c = space // 8, space // 2 % 4, space % 2
    z = 2 * zh + zl
    moment = 2 * y + c

    packed = pack(pack_kernel, 4 * PIECE, [video_key, video_value])
    packed, lists = lax.optimization_barrier((packed, window_lists))
    got = exchange(packed, PLANES)

    other_lists = send(lists, TIME_PARTNER)
    text_rows = jnp.concatenate([text_query, text_key, text_value], axis=0)
    text_some = lax.all_gather(text_rows, AXES, axis_index_groups=SAME_PLACE, tiled=True)
    packed_queries = pack(pack_queries_kernel, 3 * PIECE, [video_query], text_some)
    got, packed_queries = lax.optimization_barrier((got, packed_queries))

    core = c.reshape(1)
    pieces, other = from_other_core(core, got)
    low, high = merge_sides(core, pieces, other)

    left, right = send(high, in_columns(1)), send(low, in_columns(-1))
    other, _ = lax.optimization_barrier((other, low))
    own = merge_keys(core, pieces, other)
    past, future = send(own, in_time(1)), send(own, in_time(-1))
    packed_queries, _ = lax.optimization_barrier((packed_queries, own))
    got_queries = exchange(packed_queries, PLANES)
    queries = merge_queries(core, *from_other_core(core, got_queries))

    text_all = got_queries[:, 2 * PIECE :].reshape(2, 2, 4, 4, 2, 3, 2, GW)
    text_all = text_all.transpose(5, 3, 1, 0, 2, 4, 6, 7).reshape(3, TXT, GW)

    got_lists = jnp.where(zl == c, lists, other_lists).reshape(2, 8, 27)
    tile_lists = lax.dynamic_slice_in_dim(got_lists, 2 * x, 2, 1).transpose(1, 0, 2).reshape(4, 27)
    key_moment = moment + jnp.arange(-1, 2, dtype=jnp.int32)[:, None, None]
    key_column = 2 * x + jnp.arange(-1, 3, dtype=jnp.int32)[None, :, None]
    key_band = jnp.arange(2, dtype=jnp.int32)[None, None, :]
    inside = (key_moment >= 0) & (key_moment < 8) & (key_column >= 0) & (key_column < 8)
    idents = jnp.where(inside, 16 * key_moment + 8 * key_band + key_column, -2)
    listed = jnp.any(idents[..., None, None] == tile_lists, axis=-1)
    places = jnp.arange(8, dtype=jnp.int32)
    columns = 2 * x + jnp.arange(-1, 3, dtype=jnp.int32)
    valid = jnp.sum(
        jnp.where(places[None, :] == columns[:, None], valid_columns[None, :], 0), axis=1
    )
    fine = (jnp.arange(EXTRA, dtype=jnp.int32) % TC)[None, :] < valid[:, None]
    listed = jnp.pad(listed, ((0, 0), (0, 0), (0, 0), (0, HD - 4)), constant_values=True)
    allowed = listed[:, :, :, None, :] & fine[None, :, None, :, None]
    bias = jnp.where(allowed, 0.0, MASKED).astype(jnp.bfloat16)
    near_bias = jnp.concatenate([bias[1, 1:3], bias[0, 1:3], bias[2, 1:3]])
    side_bias = jnp.concatenate([bias[:, 0], bias[:, 3]])

    member = (4 * y + x) * 2 + c
    parts = text_part(member.reshape(1), text_all, near_bias[:2], [own])
    left, right, _, queries = lax.optimization_barrier((left, right, parts, queries))
    parts = exchange(parts.reshape(128, 2, GW + HD), None)
    sides = join(left, right)
    past_sides, future_sides = send(sides, in_time(1)), send(sides, in_time(-1))

    state = near(queries, text_all, near_bias, [own, past, future])
    attended = side(valid[1:3], queries, state, side_bias, [past_sides, sides, future_sides])
    parts, attended = lax.optimization_barrier((parts, attended))
    attended = attended.reshape(4, TILE, GW)

    turns = jnp.arange(4, dtype=jnp.int32)
    arrived = [
        send(lax.dynamic_index_in_dim(attended, (z + turn) % 4, 0, keepdims=False), to_owner(turn))
        for turn in range(4)
    ]
    video_output = project((2 * (x % 2) + c - turns) % 4, arrived, video_weight)
    video_output = video_output.reshape(1, 1, 1, TILE, -1)
    text_attn = text_sum(parts)
    text_output = jnp.dot(text_attn, text_weight, preferred_element_type=jnp.float32)
    text_output = text_output.astype(jnp.bfloat16)
    return (video_output, text_output)


def solution(mesh):
    in_specs = (
        P("tm", "space", None, None),
        P("tm", "space", None, None),
        P("tm", "space", None, None),
        P(("tm", "space"), None),
        P(("tm", "space"), None),
        P(("tm", "space"), None),
        P("tm", None, None),
        P(),
        P(),
        P(),
    )
    out_specs = (P("tm", "space", None, None, None), P(("tm", "space"), None))
    return jax.shard_map(shards, mesh=mesh, in_specs=in_specs, out_specs=out_specs, check_vma=False)
```

time: 277 us -> 210 us (0.76)
  the two profiles are of different devices: /device:TPU:14 before, /device:TPU:13 now
where the time goes in v2:
time: 210 us; the launch traced here: 209 us
  Pallas kernels  83.5 us (40%)
  starting transfers between devices  57.4 us (27%)
  waiting for transfers between devices  29 us (14%)
  blocking collectives  14.1 us (7%)
  local copies, waits for them, and re-layouts  13.1 us (6%)
  matrix products  5.78 us (3%)
  other arithmetic  5.35 us (3%)
    ppermute x13, starting transfers between devices, send(): return lax.ppermute(value, AXES, pairs)  31.8 us
    pallas_call x1, Pallas kernels, near(): pl.pallas_call(functools.partial(near_kernel, len(cells)), grid=(GH,), in...  30.1 us
    all_to_all x3, starting transfers between devices, exchange(): lax.all_to_all(value, AXES, split_axis=0, concat_axis=0, tiled=True, axis...  25.6 us
    all_to_all x3, waiting for transfers between devices, exchange(): lax.all_to_all(value, AXES, split_axis=0, concat_axis=0, tiled=True, axis...  23.1 us
    pallas_call x1, Pallas kernels, side(): pl.pallas_call(side_kernel, grid=(GH,), in_specs=[pl.BlockSpec(memory_spa...  21.2 us
    all_gather x1, blocking collectives, shards(): lax.all_gather(text_rows, AXES, axis_index_groups=SAME_PLACE, tiled=True)  14.1 us
    pallas_call x3, Pallas kernels, merge(): pl.pallas_call(kernel, grid_spec=pltpu.PrefetchScalarGridSpec(num_scalar_...  8.01 us
    pallas_call x2, Pallas kernels, pack(): pl.pallas_call(kernel, grid=(4,), in_specs=[raster] * len(rasters) + [tex...  7.51 us
  transfers between devices with their start and end apart: 16, of which 4 were waited for; matrix products, arithmetic and copies ran while one was open for 9% of the time, Pallas kernels for 35%

profile of v2, /device:TPU:13, one launch (start us, length us, event | category | flops | bytes accessed | tf_op | source)
XLA Modules:
  0.0 209.2 jit_solution(10466266405308378275)
XLA Ops:
  0.6 3.9 %pack.2 = bf16[16,192,384]{2,1,0:T(8,128)(2,1)} custom-call(bf16[6,64,1536]{2,1,0:T(8,128)(2,1)} %bitcast.56, bf16[6,64,1536]{2,1,0:T(8,128)(2,1)} %bitcast.57), custom_call_target="tpu_custom_call" | custom-call | bytes 4718592 | tf_op jit(solution)/shard_map/pack/pallas_call | solution.py:109
  4.5 7.9 %all-to-all-start = ((bf16[16,192,384]{2,1,0:T(8,128)(2,1)}), bf16[16,192,384]{2,1,0:T(8,128)(2,1)S(1)}, u32[]{:S(2)}, u32[]{:S(2)}) async-start(bf16[16,192,384]{2,1,0:T(8,128)(2,1)} %pack.2), calls=%async_computation | async-start | bytes 4718592 | tf_op jit(solution)/shard_map/all_to_all | solution.py:84
  12.5 14.1 %all-gather = bf16[8,6,1536]{2,1,0:T(8,128)(2,1)S(1)} all-gather(bf16[1,6,1536]{2,1,0:T(8,128)(2,1)S(1)} %maximum_bitcast_fusion), channel_id=1, replica_groups={{0,1,32,33,64,65,96,97},{2,3,34,35,66,67,98,99},{4,5,36,37,68,69,100,10..., dimensions={0}, use_global_device_ids=true | all-gather | bytes 165888 | tf_op jit(solution)/shard_map/all_gather | solution.py:487
  26.5 0.7 reshape.222.text_ref
  27.3 3.6 %pack.3 = bf16[16,144,384]{2,1,0:T(8,128)(2,1)} custom-call(bf16[6,64,1536]{2,1,0:T(8,128)(2,1)} %bitcast.55, bf16[48,1536]{1,0:T(8,128)(2,1)} %reshape.222.text_ref), custom_call_target="tpu_custom_call" | custom-call | bytes 3538944 | tf_op jit(solution)/shard_map/pack/pallas_call | solution.py:109
  30.9 13.1 %all-to-all-done = bf16[16,192,384]{2,1,0:T(8,128)(2,1)S(1)} async-done(((bf16[16,192,384]{2,1,0:T(8,128)(2,1)}), bf16[16,192,384]{2,1,0:T(8,128)(2,1)S(1)}, u32[]{:S(2)}, u32[]{:S(2)}) %all-to-all-start) | async-done | bytes 2359328 | tf_op jit(solution)/shard_map/all_to_all | solution.py:84
  44.0 1.3 dynamic-slice_bitcast_fusion
  45.3 0.5 collective-permute-start
  45.8 1.9 collective-permute-start.1
  47.7 0.2 select_reduce_fusion
  47.9 0.6 copy-done.18
  48.5 0.1 slice.23.valid_ref
  48.5 0.5 and_select_fusion
  49.1 0.5 iota_multiply_fusion
  49.6 0.5 fusion.1
  50.1 1.0 copy-done.8
  51.2 2.8 %merge.3 = (bf16[2,768,384]{2,1,0:T(8,128)(2,1)}, bf16[2,768,384]{2,1,0:T(8,128)(2,1)}) custom-call(s32[1]{0:T(128)} %bitcast.5.c_ref, bf16[2,2,4,192,384]{4,3,2,1,0:T(8,128)(2,1)} %bitcast.52, bf16[2,4,192,384]{3,2,1,0:T(8,128)(2,1)} %copy-done.8), custom_call_target="tpu_custom_call" | custom-call | bytes 4718592 | tf_op jit(solution)/shard_map/merge/pallas_call | solution.py:165
  54.0 2.8 %merge.4.refs_0_.refs_1_ = bf16[2,2,768,384]{3,2,1,0:T(8,128)(2,1)} custom-call(s32[1]{0:T(128)} %bitcast.5.c_ref, bf16[2,2,4,192,384]{4,3,2,1,0:T(8,128)(2,1)} %bitcast.53, bf16[2,4,192,384]{3,2,1,0:T(8,128)(2,1)} %copy-done.8), custom_call_target="tpu_custom_call" | custom-call | bytes 4718592 | tf_op jit(solution)/shard_map/merge/pallas_call | solution.py:165
  56.8 7.1 %all-to-all-start.1 = ((bf16[16,144,384]{2,1,0:T(8,128)(2,1)}), bf16[16,144,384]{2,1,0:T(8,128)(2,1)}, u32[]{:S(2)}, u32[]{:S(2)}) async-start(bf16[16,144,384]{2,1,0:T(8,128)(2,1)} %pack.3), calls=%async_computation.1 | async-start | bytes 3538944 | tf_op jit(solution)/shard_map/all_to_all | solution.py:84
  64.0 0.1 and_and_fusion
  64.0 3.7 %collective-permute-start.5 = (bf16[2,2,768,384]{3,2,1,0:T(8,128)(2,1)S(1)}, bf16[2,2,768,384]{3,2,1,0:T(8,128)(2,1)}, u32[]{:S(2)}, u32[]{:S(2)}) collective-permute-start(bf16[2,2,768,384]{3,2,1,0:T(8,128)(2,1)S(1)} %copy-done), channel_id=1, source_target_pairs={{0,1},{1,32},{2,3},{3,34},{4,5},{5,36},{6,7},{7,38},{16,17},{17,48... | collective-permute-start | bytes 7077896 | tf_op jit(solution)/shard_map/ppermute | solution.py:80
  67.8 1.9 collective-permute-start.6
  69.7 0.1 broadcast_compare_fusion
  69.8 0.1 broadcast_add_fusion
  69.9 0.7 add_select_fusion
  70.6 0.7 select_bitcast_fusion
  71.3 0.6 compare_reduce_fusion
  72.0 2.2 %collective-permute-start.3 = (bf16[2,768,384]{2,1,0:T(8,128)(2,1)}, bf16[2,768,384]{2,1,0:T(8,128)(2,1)}, u32[]{:S(2)}, u32[]{:S(2)}) collective-permute-start(bf16[2,768,384]{2,1,0:T(8,128)(2,1)} %get-tuple-element.20), channel_id=1, source_target_pairs={{2,0},{3,1},{4,2},{5,3},{6,4},{7,5},{18,16},{19,17},{20,18},{21,19... | collective-permute-start | bytes 3538952 | tf_op jit(solution)/shard_map/ppermute | solution.py:80
  74.1 4.1 %collective-permute-start.2 = (bf16[2,768,384]{2,1,0:T(8,128)(2,1)}, bf16[2,768,384]{2,1,0:T(8,128)(2,1)}, u32[]{:S(2)}, u32[]{:S(2)}) collective-permute-start(bf16[2,768,384]{2,1,0:T(8,128)(2,1)} %get-tuple-element.24), channel_id=1, source_target_pairs={{0,2},{1,3},{2,4},{3,5},{4,6},{5,7},{16,18},{17,19},{18,20},{19,21... | collective-permute-start | bytes 3538952 | tf_op jit(solution)/shard_map/ppermute | solution.py:80
  78.3 10.0 %all-to-all-done.1 = bf16[16,144,384]{2,1,0:T(8,128)(2,1)} async-done(((bf16[16,144,384]{2,1,0:T(8,128)(2,1)}), bf16[16,144,384]{2,1,0:T(8,128)(2,1)}, u32[]{:S(2)}, u32[]{:S(2)}) %all-to-all-start.1) | async-done | bytes 1769504 | tf_op jit(solution)/shard_map/all_to_all | solution.py:84
  88.3 2.2 %dynamic-slice_bitcast_fusion.1 = bf16[2,4,144,384]{3,2,1,0:T(8,128)(2,1)} fusion(bf16[2,2,4,144,384]{4,3,2,1,0:T(8,128)(2,1)} %bitcast.13.mine_ref, s32[]{:T(128)S(6)} %select_n.113), kind=kLoop, calls=%fused_computation.2 | loop fusion | bytes 1769476 | tf_op jit(solution)/shard_map/jit(dynamic_index_in_dim)/squeeze | solution.py:159
  90.5 1.4 collective-permute-start.4
  91.8 0.1 select_convert_fusion
  92.0 0.6 pad_maximum_fusion.1.bias_ref
  92.6 0.6 pad_maximum_fusion.bias_ref
  93.2 1.1 slice.28
  94.3 0.2 reshape.213
  94.6 0.5 copy.34
  95.1 1.1 reshape.214.q_ref.tk_ref.tv_ref
  96.2 5.1 %text_queries.1 = f32[256,512]{1,0:T(8,128)} custom-call(s32[1]{0:T(128)} %bitcast.share_ref, bf16[3,256,384]{2,1,0:T(8,128)(2,1)} %reshape.214.q_ref.tk_ref.tv_ref, bf16[3,256,384]{2,1,0:T(8,128)(2,1)} %reshape.214.q_ref.tk_ref.tv_ref, bf16[3,256,384]{2,1,0:T(8,128)(2,1)} %reshape.214.q_ref.tk_ref.tv_ref, bf16[2,2,16,128]{3,2,1,0:T(8,128)(2,1)} %copy-done.9, ...), custom_call_target="tpu_custom_call" | custom-call | flops 2113929216 | bytes 2752512 | tf_op jit(solution)/shard_map/text_queries/pallas_call | solution.py:418
  101.3 2.2 %reshape.216 = f32[128,2,512]{2,1,0:T(2,128)} reshape(f32[256,512]{1,0:T(8,128)} %text_queries.1) | data formatting | bytes 1048576 | tf_op jit(solution)/shard_map/reshape | solution.py:529
  103.5 10.6 %all-to-all-start.2 = ((f32[128,2,512]{2,1,0:T(2,128)}), f32[128,2,512]{2,1,0:T(2,128)}, u32[]{:S(2)}, u32[]{:S(2)}) async-start(f32[128,2,512]{2,1,0:T(2,128)} %reshape.216), calls=%async_computation.2 | async-start | bytes 1048576 | tf_op jit(solution)/shard_map/all_to_all | solution.py:84
  114.1 2.4 %merge.5.q_ref = bf16[2,2,384,384]{3,2,1,0:T(8,128)(2,1)} custom-call(s32[1]{0:T(128)} %bitcast.5.c_ref, bf16[2,2,4,144,384]{4,3,2,1,0:T(8,128)(2,1)} %bitcast.13.mine_ref, bf16[2,4,144,384]{3,2,1,0:T(8,128)(2,1)} %collective-permute-done.4.other_ref), custom_call_target="tpu_custom_call" | custom-call | bytes 3538944 | tf_op jit(solution)/shard_map/merge/pallas_call | solution.py:165
  116.5 0.0 collective-permute-done.3.right_ref
  116.5 2.9 %join.1.refs_2_.refs_3_ = bf16[2,2,768,384]{3,2,1,0:T(8,128)(2,1)} custom-call(bf16[2,768,384]{2,1,0:T(8,128)(2,1)} %collective-permute-done.2.left_ref, bf16[2,768,384]{2,1,0:T(8,128)(2,1)} %collective-permute-done.3.right_ref), custom_call_target="tpu_custom_call" | custom-call | bytes 4718592 | tf_op jit(solution)/shard_map/join/pallas_call | solution.py:208
  119.4 3.5 %collective-permute-start.7 = (bf16[2,2,768,384]{3,2,1,0:T(8,128)(2,1)}, bf16[2,2,768,384]{3,2,1,0:T(8,128)(2,1)S(1)}, u32[]{:S(2)}, u32[]{:S(2)}) collective-permute-start(bf16[2,2,768,384]{3,2,1,0:T(8,128)(2,1)} %join.1.refs_2_.refs_3_), channel_id=1, source_target_pairs={{0,1},{1,32},{2,3},{3,34},{4,5},{5,36},{6,7},{7,38},{16,17},{17,48... | collective-permute-start | bytes 7077896 | tf_op jit(solution)/shard_map/ppermute | solution.py:80
  122.9 2.1 %collective-permute-start.8 = (bf16[2,2,768,384]{3,2,1,0:T(8,128)(2,1)}, bf16[2,2,768,384]{3,2,1,0:T(8,128)(2,1)S(1)}, u32[]{:S(2)}, u32[]{:S(2)}) collective-permute-start(bf16[2,2,768,384]{3,2,1,0:T(8,128)(2,1)} %join.1.refs_2_.refs_3_), channel_id=1, source_target_pairs={{1,0},{3,2},{5,4},{7,6},{17,16},{19,18},{21,20},{23,22},{9,8},{11,... | collective-permute-start | bytes 7077896 | tf_op jit(solution)/shard_map/ppermute | solution.py:80
  125.0 0.0 collective-permute-done.6.refs_4_.refs_5_
  125.1 1.1 copy-done.4
  126.1 0.8 copy-done.6
  126.9 30.1 %near_cells.1 = (f32[2,768,384]{2,1,0:T(8,128)S(1)}, f32[2,768,384]{2,1,0:T(8,128)S(1)}) custom-call(bf16[2,2,384,384]{3,2,1,0:T(8,128)(2,1)S(1)} %copy-done.3, bf16[3,256,384]{2,1,0:T(8,128)(2,1)S(1)} %copy-done.4, bf16[3,256,384]{2,1,0:T(8,128)(2,1)S(1)} %copy-done.4, bf16[6,2,16,128]{3,2,1,0:T(8,128)(2,1)S(1)} %copy-done.6, ...), custom_call_target="tpu_custom_call" | custom-call | flops 34426847232 | bytes 7471104 | tf_op jit(solution)/shard_map/near_cells/pallas_call | solution.py:331
  157.0 0.0 collective-permute-done.7.refs_0_.refs_1_
  157.1 21.2 %side_cells.1 = bf16[2,2,384,384]{3,2,1,0:T(8,128)(2,1)S(1)} custom-call(s32[2]{0:T(128)S(1)} %slice.23.valid_ref, bf16[2,2,384,384]{3,2,1,0:T(8,128)(2,1)S(1)} %copy-done.3, f32[2,768,384]{2,1,0:T(8,128)S(1)} %get-tuple-element.26.sum_ref, f32[2,768,384]{2,1,0:T(8,128)S(1)} %get-tuple-element.27.mark_ref, bf16[6,2,16,128]{3,2,1,0:T(8,128)(2,1)S(1)} %copy-done.5, ...), custom_call_target="tpu_custom_call" | custom-call | flops 16307453952 | bytes 3538944 | tf_op jit(solution)/shard_map/side_cells/pallas_call | solution.py:368
  178.3 0.0 slice-start
  178.3 0.1 dynamic-slice_bitcast_fusion.2
  178.5 5.7 %collective-permute-start.9 = (bf16[384,384]{1,0:T(8,128)(2,1)S(1)}, bf16[384,384]{1,0:T(8,128)(2,1)S(1)}, u32[]{:S(2)}, u32[]{:S(2)}) collective-permute-start(bf16[384,384]{1,0:T(8,128)(2,1)S(1)} %get-tuple-element.35), channel_id=1, source_target_pairs={{0,0},{1,16},{2,4},{3,20},{4,8},{5,24},{6,12},{7,28},{16,1},{17,17... | collective-permute-start | bytes 884744 | tf_op jit(solution)/shard_map/ppermute | solution.py:80
  184.2 1.2 collective-permute-start.10
  185.3 3.1 %collective-permute-start.11 = (bf16[384,384]{1,0:T(8,128)(2,1)S(1)}, bf16[384,384]{1,0:T(8,128)(2,1)S(1)}, u32[]{:S(2)}, u32[]{:S(2)}) collective-permute-start(bf16[384,384]{1,0:T(8,128)(2,1)S(1)} %get-tuple-element.33), channel_id=1, source_target_pairs={{0,2},{1,18},{2,6},{3,22},{4,10},{5,26},{6,14},{7,30},{16,3},{17,1... | collective-permute-start | bytes 884744 | tf_op jit(solution)/shard_map/ppermute | solution.py:80
  188.4 0.5 collective-permute-start.12
  189.0 2.4 %text_sum.1 = bf16[2,1536]{1,0:T(2,128)(2,1)} custom-call(f32[4,2,2,8,2,512]{5,4,3,2,1,0:T(2,128)} %bitcast.25.part_ref), custom_call_target="tpu_custom_call" | custom-call | bytes 524288 | tf_op jit(solution)/shard_map/text_sum/pallas_call | solution.py:452
  191.4 5.8 %convolution_convert_fusion = bf16[2,3072]{1,0:T(2,128)(2,1)} fusion(bf16[2,1536]{1,0:T(2,128)(2,1)} %text_sum.1, bf16[1536,3072]{1,0:T(8,128)(2,1)} %param.19), kind=kOutput, calls=%fused_computation | convolution fusion | flops 18880512 | bytes 9455616 | tf_op jit(solution)/shard_map/dot_general | solution.py:546
  197.2 4.6 %collective-permute-done.11.third = bf16[384,384]{1,0:T(8,128)(2,1)S(1)} collective-permute-done((bf16[384,384]{1,0:T(8,128)(2,1)S(1)}, bf16[384,384]{1,0:T(8,128)(2,1)S(1)}, u32[]{:S(2)}, u32[]{:S(2)}) %collective-permute-start.11) | collective-permute-done | bytes 294944 | tf_op jit(solution)/shard_map/ppermute | solution.py:80
  201.8 1.3 collective-permute-done.12.fourth
  203.0 6.2 %project.1 = bf16[384,3072]{1,0:T(8,128)(2,1)} custom-call(s32[4]{0:T(128)S(1)} %and_select_fusion.1.from_ref, bf16[384,384]{1,0:T(8,128)(2,1)S(1)} %collective-permute-done.9.first, bf16[384,384]{1,0:T(8,128)(2,1)S(1)} %collective-permute-done.10.second, bf16[384,384]{1,0:T(8,128)(2,1)S(1)} %collective-permute-done.11.third, ...), custom_call_target="tpu_custom_call" | custom-call | flops 3623878656 | bytes 9437184 | tf_op jit(solution)/shard_map/project/pallas_call | solution.py:235
  (64 shorter events, 0.2 us)
Async XLA Ops:
  4.5 7.9 %copy-start.11 = (bf16[2,1536]{1,0:T(2,128)(2,1)S(1)}, bf16[2,1536]{1,0:T(2,128)(2,1)}, u32[]{:S(2)}) copy-start(bf16[2,1536]{1,0:T(2,128)(2,1)} %param.15) | copy-start | bytes 18436
  4.5 7.9 %copy-start.12 = (bf16[2,1536]{1,0:T(2,128)(2,1)S(1)}, bf16[2,1536]{1,0:T(2,128)(2,1)}, u32[]{:S(2)}) copy-start(bf16[2,1536]{1,0:T(2,128)(2,1)} %param.14) | copy-start | bytes 18436
  4.5 7.9 %copy-start.13 = (bf16[2,1536]{1,0:T(2,128)(2,1)S(1)}, bf16[2,1536]{1,0:T(2,128)(2,1)}, u32[]{:S(2)}) copy-start(bf16[2,1536]{1,0:T(2,128)(2,1)} %param.13) | copy-start | bytes 18436
  4.5 39.4 %all-to-all-start = ((bf16[16,192,384]{2,1,0:T(8,128)(2,1)}), bf16[16,192,384]{2,1,0:T(8,128)(2,1)S(1)}, u32[]{:S(2)}, u32[]{:S(2)}) async-start(bf16[16,192,384]{2,1,0:T(8,128)(2,1)} %pack.2), calls=%async_computation | async-start | bytes 4718592 | tf_op jit(solution)/shard_map/all_to_all | solution.py:84
  27.2 18.5 %copy-start.10 = (s32[1,16,27]{2,1,0:T(8,128)S(1)}, s32[1,16,27]{2,1,0:T(8,128)}, u32[]{:S(2)}) copy-start(s32[1,16,27]{2,1,0:T(8,128)} %param.16) | copy-start | bytes 5188
  27.3 20.4 %copy-start.17 = (s32[8]{0:T(128)S(1)}, s32[8]{0:T(128)}, u32[]{:S(2)}) copy-start(s32[8]{0:T(128)} %param.17) | copy-start | bytes 100
  44.0 6.2 %copy-start.7 = (bf16[16,192,384]{2,1,0:T(8,128)(2,1)}, bf16[16,192,384]{2,1,0:T(8,128)(2,1)S(1)}, u32[]{:S(2)}) copy-start(bf16[16,192,384]{2,1,0:T(8,128)(2,1)S(1)} %all-to-all-done) | copy-start | bytes 7077892
  45.3 4.9 %collective-permute-start = (bf16[2,4,192,384]{3,2,1,0:T(8,128)(2,1)}, bf16[2,4,192,384]{3,2,1,0:T(8,128)(2,1)S(1)}, u32[]{:S(2)}, u32[]{:S(2)}) collective-permute-start(bf16[2,4,192,384]{3,2,1,0:T(8,128)(2,1)} %dynamic-slice_bitcast_fusion), channel_id=1, source_target_pairs={{0,1},{1,0},{2,3},{3,2},{4,5},{5,4},{6,7},{7,6},{16,17},{17,16},{1... | collective-permute-start | bytes 3538952 | tf_op jit(solution)/shard_map/ppermute | solution.py:80
  45.8 24.8 %collective-permute-start.1 = (s32[1,16,27]{2,1,0:T(8,128)S(1)}, s32[1,16,27]{2,1,0:T(8,128)}, u32[]{:S(2)}, u32[]{:S(2)}) collective-permute-start(s32[1,16,27]{2,1,0:T(8,128)S(1)} %copy-done.10), channel_id=1, source_target_pairs={{0,16},{1,17},{2,18},{3,19},{4,20},{5,21},{6,22},{7,23},{16,0},{17... | collective-permute-start | bytes 5192 | tf_op jit(solution)/shard_map/ppermute | solution.py:80
  47.7 9.1 %copy-start.14 = (s32[4]{0:T(128)}, s32[4]{0:T(128)S(1)}, u32[]{:S(2)}) copy-start(s32[4]{0:T(128)S(1)} %add_add_fusion) | copy-start | bytes 52
  47.9 0.6 copy-start.18
  50.1 1.0 copy-start.8
  56.8 7.3 %copy-start = (bf16[2,2,768,384]{3,2,1,0:T(8,128)(2,1)S(1)}, bf16[2,2,768,384]{3,2,1,0:T(8,128)(2,1)}, u32[]{:S(2)}) copy-start(bf16[2,2,768,384]{3,2,1,0:T(8,128)(2,1)} %merge.4.refs_0_.refs_1_) | copy-start | bytes 7077892
  56.8 12.9 %copy-start.19 = (s32[4]{0:T(128)S(1)}, s32[4]{0:T(128)}, u32[]{:S(2)}) copy-start(s32[4]{0:T(128)} %copy-done.18) | copy-start | bytes 52
  56.8 12.9 %copy-start.20 = (s32[16]{0:T(128)S(1)}, s32[16]{0:T(128)}, u32[]{:S(2)}) copy-start(s32[16]{0:T(128)} %and_select_fusion) | copy-start | bytes 196
  56.8 13.0 %copy-start.15 = (s32[2]{0:T(128)S(1)}, s32[2]{0:T(128)}, u32[]{:S(2)}) copy-start(s32[2]{0:T(128)} %iota_multiply_fusion) | copy-start | bytes 28
  56.8 13.0 %copy-start.16 = (s32[3]{0:T(128)S(1)}, s32[3]{0:T(128)}, u32[]{:S(2)}) copy-start(s32[3]{0:T(128)} %fusion.1) | copy-start | bytes 40
  56.8 31.5 %all-to-all-start.1 = ((bf16[16,144,384]{2,1,0:T(8,128)(2,1)}), bf16[16,144,384]{2,1,0:T(8,128)(2,1)}, u32[]{:S(2)}, u32[]{:S(2)}) async-start(bf16[16,144,384]{2,1,0:T(8,128)(2,1)} %pack.3), calls=%async_computation.1 | async-start | bytes 3538944 | tf_op jit(solution)/shard_map/all_to_all | solution.py:84
  64.0 61.0 %collective-permute-start.5 = (bf16[2,2,768,384]{3,2,1,0:T(8,128)(2,1)S(1)}, bf16[2,2,768,384]{3,2,1,0:T(8,128)(2,1)}, u32[]{:S(2)}, u32[]{:S(2)}) collective-permute-start(bf16[2,2,768,384]{3,2,1,0:T(8,128)(2,1)S(1)} %copy-done), channel_id=1, source_target_pairs={{0,1},{1,32},{2,3},{3,34},{4,5},{5,36},{6,7},{7,38},{16,17},{17,48... | collective-permute-start | bytes 7077896 | tf_op jit(solution)/shard_map/ppermute | solution.py:80
  67.8 57.2 %collective-permute-start.6 = (bf16[2,2,768,384]{3,2,1,0:T(8,128)(2,1)S(1)}, bf16[2,2,768,384]{3,2,1,0:T(8,128)(2,1)}, u32[]{:S(2)}, u32[]{:S(2)}) collective-permute-start(bf16[2,2,768,384]{3,2,1,0:T(8,128)(2,1)S(1)} %copy-done), channel_id=1, source_target_pairs={{1,0},{3,2},{5,4},{7,6},{17,16},{19,18},{21,20},{23,22},{9,8},{11,... | collective-permute-start | bytes 7077896 | tf_op jit(solution)/shard_map/ppermute | solution.py:80
  72.0 44.5 %collective-permute-start.3 = (bf16[2,768,384]{2,1,0:T(8,128)(2,1)}, bf16[2,768,384]{2,1,0:T(8,128)(2,1)}, u32[]{:S(2)}, u32[]{:S(2)}) collective-permute-start(bf16[2,768,384]{2,1,0:T(8,128)(2,1)} %get-tuple-element.20), channel_id=1, source_target_pairs={{2,0},{3,1},{4,2},{5,3},{6,4},{7,5},{18,16},{19,17},{20,18},{21,19... | collective-permute-start | bytes 3538952 | tf_op jit(solution)/shard_map/ppermute | solution.py:80
  74.1 42.3 %collective-permute-start.2 = (bf16[2,768,384]{2,1,0:T(8,128)(2,1)}, bf16[2,768,384]{2,1,0:T(8,128)(2,1)}, u32[]{:S(2)}, u32[]{:S(2)}) collective-permute-start(bf16[2,768,384]{2,1,0:T(8,128)(2,1)} %get-tuple-element.24), channel_id=1, source_target_pairs={{0,2},{1,3},{2,4},{3,5},{4,6},{5,7},{16,18},{17,19},{18,20},{19,21... | collective-permute-start | bytes 3538952 | tf_op jit(solution)/shard_map/ppermute | solution.py:80
  90.5 23.6 %collective-permute-start.4 = (bf16[2,4,144,384]{3,2,1,0:T(8,128)(2,1)}, bf16[2,4,144,384]{3,2,1,0:T(8,128)(2,1)}, u32[]{:S(2)}, u32[]{:S(2)}) collective-permute-start(bf16[2,4,144,384]{3,2,1,0:T(8,128)(2,1)} %dynamic-slice_bitcast_fusion.1), channel_id=1, source_target_pairs={{0,1},{1,0},{2,3},{3,2},{4,5},{5,4},{6,7},{7,6},{16,17},{17,16},{1... | collective-permute-start | bytes 2654216 | tf_op jit(solution)/shard_map/ppermute | solution.py:80
  92.6 0.6 copy-start.9
  103.5 74.9 %all-to-all-start.2 = ((f32[128,2,512]{2,1,0:T(2,128)}), f32[128,2,512]{2,1,0:T(2,128)}, u32[]{:S(2)}, u32[]{:S(2)}) async-start(f32[128,2,512]{2,1,0:T(2,128)} %reshape.216), calls=%async_computation.2 | async-start | bytes 1048576 | tf_op jit(solution)/shard_map/all_to_all | solution.py:84
  116.5 8.6 %copy-start.1 = (bf16[2,2,768,384]{3,2,1,0:T(8,128)(2,1)S(1)}, bf16[2,2,768,384]{3,2,1,0:T(8,128)(2,1)}, u32[]{:S(2)}) copy-start(bf16[2,2,768,384]{3,2,1,0:T(8,128)(2,1)} %merge.4.refs_0_.refs_1_) | copy-start | bytes 7077892
  116.5 8.6 %copy-start.3 = (bf16[2,2,384,384]{3,2,1,0:T(8,128)(2,1)S(1)}, bf16[2,2,384,384]{3,2,1,0:T(8,128)(2,1)}, u32[]{:S(2)}) copy-start(bf16[2,2,384,384]{3,2,1,0:T(8,128)(2,1)} %merge.5.q_ref) | copy-start | bytes 3538948
  116.5 40.6 %copy-start.5 = (bf16[6,2,16,128]{3,2,1,0:T(8,128)(2,1)S(1)}, bf16[6,2,16,128]{3,2,1,0:T(8,128)(2,1)}, u32[]{:S(2)}) copy-start(bf16[6,2,16,128]{3,2,1,0:T(8,128)(2,1)} %pad_maximum_fusion.1.bias_ref) | copy-start | bytes 147460
  119.4 37.6 %copy-start.2 = (bf16[2,2,768,384]{3,2,1,0:T(8,128)(2,1)S(1)}, bf16[2,2,768,384]{3,2,1,0:T(8,128)(2,1)}, u32[]{:S(2)}) copy-start(bf16[2,2,768,384]{3,2,1,0:T(8,128)(2,1)} %join.1.refs_2_.refs_3_) | copy-start | bytes 7077892
  119.4 37.6 %collective-permute-start.7 = (bf16[2,2,768,384]{3,2,1,0:T(8,128)(2,1)}, bf16[2,2,768,384]{3,2,1,0:T(8,128)(2,1)S(1)}, u32[]{:S(2)}, u32[]{:S(2)}) collective-permute-start(bf16[2,2,768,384]{3,2,1,0:T(8,128)(2,1)} %join.1.refs_2_.refs_3_), channel_id=1, source_target_pairs={{0,1},{1,32},{2,3},{3,34},{4,5},{5,36},{6,7},{7,38},{16,17},{17,48... | collective-permute-start | bytes 7077896 | tf_op jit(solution)/shard_map/ppermute | solution.py:80
  122.9 34.1 %collective-permute-start.8 = (bf16[2,2,768,384]{3,2,1,0:T(8,128)(2,1)}, bf16[2,2,768,384]{3,2,1,0:T(8,128)(2,1)S(1)}, u32[]{:S(2)}, u32[]{:S(2)}) collective-permute-start(bf16[2,2,768,384]{3,2,1,0:T(8,128)(2,1)} %join.1.refs_2_.refs_3_), channel_id=1, source_target_pairs={{1,0},{3,2},{5,4},{7,6},{17,16},{19,18},{21,20},{23,22},{9,8},{11,... | collective-permute-start | bytes 7077896 | tf_op jit(solution)/shard_map/ppermute | solution.py:80
  125.1 1.1 copy-start.4
  126.1 0.8 copy-start.6
  178.3 24.7 %slice-start = ((s8[9437184]{0:T(1024)(128)(4,1)}), s8[1048576]{0:T(1024)(128)(4,1)S(1)}, s32[]{:S(2)}) async-start(s8[9437184]{0:T(1024)(128)(4,1)} %bitcast.49), calls=%async_computation.3 | async-start | bytes 2097152
  178.5 18.7 %collective-permute-start.9 = (bf16[384,384]{1,0:T(8,128)(2,1)S(1)}, bf16[384,384]{1,0:T(8,128)(2,1)S(1)}, u32[]{:S(2)}, u32[]{:S(2)}) collective-permute-start(bf16[384,384]{1,0:T(8,128)(2,1)S(1)} %get-tuple-element.35), channel_id=1, source_target_pairs={{0,0},{1,16},{2,4},{3,20},{4,8},{5,24},{6,12},{7,28},{16,1},{17,17... | collective-permute-start | bytes 884744 | tf_op jit(solution)/shard_map/ppermute | solution.py:80
  184.2 13.0 %collective-permute-start.10 = (bf16[384,384]{1,0:T(8,128)(2,1)S(1)}, bf16[384,384]{1,0:T(8,128)(2,1)S(1)}, u32[]{:S(2)}, u32[]{:S(2)}) collective-permute-start(bf16[384,384]{1,0:T(8,128)(2,1)S(1)} %get-tuple-element.34), channel_id=1, source_target_pairs={{0,1},{1,17},{2,5},{3,21},{4,9},{5,25},{6,13},{7,29},{16,2},{17,18... | collective-permute-start | bytes 884744 | tf_op jit(solution)/shard_map/ppermute | solution.py:80
  185.3 16.4 %collective-permute-start.11 = (bf16[384,384]{1,0:T(8,128)(2,1)S(1)}, bf16[384,384]{1,0:T(8,128)(2,1)S(1)}, u32[]{:S(2)}, u32[]{:S(2)}) collective-permute-start(bf16[384,384]{1,0:T(8,128)(2,1)S(1)} %get-tuple-element.33), channel_id=1, source_target_pairs={{0,2},{1,18},{2,6},{3,22},{4,10},{5,26},{6,14},{7,30},{16,3},{17,1... | collective-permute-start | bytes 884744 | tf_op jit(solution)/shard_map/ppermute | solution.py:80
  188.4 14.6 %collective-permute-start.12 = (bf16[384,384]{1,0:T(8,128)(2,1)S(1)}, bf16[384,384]{1,0:T(8,128)(2,1)S(1)}, u32[]{:S(2)}, u32[]{:S(2)}) collective-permute-start(bf16[384,384]{1,0:T(8,128)(2,1)S(1)} %get-tuple-element.32), channel_id=1, source_target_pairs={{0,3},{1,19},{2,7},{3,23},{4,11},{5,27},{6,15},{7,31},{16,0},{17,1... | collective-permute-start | bytes 884744 | tf_op jit(solution)/shard_map/ppermute | solution.py:80
  191.4 11.7 %slice-start.1 = ((s8[9437184]{0:T(1024)(128)(4,1)}), s8[4194304]{0:T(1024)(128)(4,1)S(1)}, s32[]{:S(2)}) async-start(s8[9437184]{0:T(1024)(128)(4,1)} %bitcast.49), calls=%async_computation.4 | async-start | bytes 8388608
  191.4 11.7 %slice-start.2 = ((s8[9437184]{0:T(1024)(128)(4,1)}), s8[4194304]{0:T(1024)(128)(4,1)S(1)}, s32[]{:S(2)}) async-start(s8[9437184]{0:T(1024)(128)(4,1)} %bitcast.49), calls=%async_computation.5 | async-start | bytes 8388608

commit v3 on v2

--- a/solution.py
+++ b/solution.py
@@ -22,6 +22,7 @@
 AXES = ("tm", "space")
 SCALE = HD**-0.5 * math.log2(math.e)
 MASKED = -1e30
+TOO_FAR = 60.0 / SCALE
 TEXT_LANE = 4
 CONTRACT_LAST = (((1,), (1,)), ((), ()))
 
@@ -278,6 +279,35 @@
     return top, part
 
 
+def add_all(query, state, blocks):
+    for keys, bias, values in blocks:
+        state = add_keys(query, state, keys(), wide_bias(bias()), values())
+    return state, None
+
+
+def add_all_late(query, state, blocks):
+    peak, total = state
+    step = None
+    for keys, bias, values in blocks:
+        scores = lax.dot_general(
+            query,
+            jnp.concatenate([keys(), wide_bias(bias())], axis=1),
+            CONTRACT_LAST,
+            preferred_element_type=jnp.float32,
+        )
+        weights = jnp.exp2((scores - peak) * SCALE).astype(jnp.bfloat16)
+        ones = jnp.ones((CELL, HD), jnp.bfloat16)
+        part = jnp.dot(
+            weights, jnp.concatenate([values(), ones], axis=1), preferred_element_type=jnp.float32
+        )
+        top = jnp.maximum(peak, jnp.max(scores, axis=1, keepdims=True))
+        rise = top - peak
+        total = (total + part) * jnp.exp2(-rise * SCALE)
+        step = rise if step is None else jnp.maximum(step, rise)
+        peak = top
+    return (peak, total), jnp.max(step)
+
+
 def widened(query, first_lane):
     rows = query.shape[0]
     lanes = lax.broadcasted_iota(jnp.int32, (rows, HD), 1)
@@ -294,16 +324,25 @@
 
 def near_kernel(cells, q_ref, tk_ref, tv_ref, bias_ref, *refs):
     sum_ref, mark_ref = refs[2 * cells :]
-    no_bias = jnp.zeros((TXT, HD), jnp.bfloat16)
-    for w in range(2):
+
+    def run(w, late):
         query = widened(q_ref[w].reshape(CELL, HD), 2 * w)
+        no_bias = jnp.zeros((TXT, HD), jnp.bfloat16)
         state = add_keys(query, None, tk_ref[0], no_bias, tv_ref[0])
-        for i in range(2 * cells):
-            bias = wide_bias(bias_ref[i])
-            keys, values = refs[2 * (i // 2)], refs[2 * (i // 2) + 1]
-            state = add_keys(query, state, keys[0, i % 2], bias, values[0, i % 2])
+        blocks = [
+            (
+                functools.partial(refs[2 * (i // 2)].__getitem__, (0, i % 2)),
+                functools.partial(bias_ref.__getitem__, i),
+                functools.partial(refs[2 * (i // 2) + 1].__getitem__, (0, i % 2)),
+            )
+            for i in range(2 * cells)
+        ]
+        state, _ = late(query, state, blocks)
         sum_ref[w] = state[1][:, :HD]
         mark_ref[w] = mark_of(state)
+
+    run(0, add_all)
+    run(1, add_all)
 
 
 def cell_specs(number):
@@ -349,17 +388,32 @@
 def side_kernel(valid_ref, q_ref, sum_ref, mark_ref, bias_ref, *refs):
     out_ref = refs[6]
     row = lax.broadcasted_iota(jnp.int32, (CELL, HD), 0)
-    for w in range(2):
+
+    def run(w, late):
         query = widened(q_ref[w].reshape(CELL, HD), 2 * w)
         mark = mark_ref[w]
         totals = jnp.broadcast_to(mark[:, HD // 2 : HD // 2 + 1], (CELL, HD))
         state = (mark[:, :1], jnp.concatenate([sum_ref[w], totals], axis=1))
-        for i in range(3):
-            bias = wide_bias(bias_ref[3 * w + i])
-            state = add_keys(query, state, refs[2 * i][0, w], bias, refs[2 * i + 1][0, w])
+        blocks = [
+            (
+                functools.partial(refs[2 * i].__getitem__, (0, w)),
+                functools.partial(bias_ref.__getitem__, 3 * w + i),
+                functools.partial(refs[2 * i + 1].__getitem__, (0, w)),
+            )
+            for i in range(3)
+        ]
+        state, step = late(query, state, blocks)
         value = state[1][:, :HD] / state[1][:, HD:]
         value = jnp.where(row % TC < valid_ref[w], value, 0.0).astype(jnp.bfloat16)
         out_ref[w] = value.reshape(2, TILE, HD)
+        return step
+
+    step = jnp.maximum(run(0, add_all_late), run(1, add_all_late))
+
+    @pl.when(step > TOO_FAR)
+    def _():
+        run(0, add_all)
+        run(1, add_all)
 
 
 def side(valid, queries, state, bias, cells):
@@ -496,7 +550,6 @@
     other, _ = lax.optimization_barrier((other, low))
     own = merge_keys(core, pieces, other)
     past, future = send(own, in_time(1)), send(own, in_time(-1))
-    packed_queries, _ = lax.optimization_barrier((packed_queries, own))
     got_queries = exchange(packed_queries, PLANES)
     queries = merge_queries(core, *from_other_core(core, got_queries))
 

time: 210 us -> 196 us (0.933)
  the two profiles are of different devices: /device:TPU:13 before, /device:TPU:14 now
where the time goes in v3:
time: 196 us; the launch traced here: 193 us
  Pallas kernels  81.4 us (42%)
  starting transfers between devices  48.7 us (25%)
  waiting for transfers between devices  32.1 us (16%)
  blocking collectives  13 us (7%)
  local copies, waits for them, and re-layouts  9.44 us (5%)
  matrix products  5.78 us (3%)
    pallas_call x1, Pallas kernels, near(): pl.pallas_call(functools.partial(near_kernel, len(cells)), grid=(GH,), in...  30.2 us
    all_to_all x3, starting transfers between devices, exchange(): lax.all_to_all(value, AXES, split_axis=0, concat_axis=0, tiled=True, axis...  24.9 us
    ppermute x13, starting transfers between devices, send(): return lax.ppermute(value, AXES, pairs)  23.9 us
    all_to_all x3, waiting for transfers between devices, exchange(): lax.all_to_all(value, AXES, split_axis=0, concat_axis=0, tiled=True, axis...  22.1 us
    pallas_call x1, Pallas kernels, side(): pl.pallas_call(side_kernel, grid=(GH,), in_specs=[pl.BlockSpec(memory_spa...  19.3 us
    all_gather x1, blocking collectives, shards(): lax.all_gather(text_rows, AXES, axis_index_groups=SAME_PLACE, tiled=True)  13 us
    ppermute x13, waiting for transfers between devices, send(): return lax.ppermute(value, AXES, pairs)  9.95 us
    pallas_call x3, Pallas kernels, merge(): pl.pallas_call(kernel, grid_spec=pltpu.PrefetchScalarGridSpec(num_scalar_...  7.92 us
  transfers between devices with their start and end apart: 16, of which 6 were waited for; matrix products, arithmetic and copies ran while one was open for 7% of the time, Pallas kernels for 37%

profile of v3, /device:TPU:14, one launch (start us, length us, event | category | flops | bytes accessed | tf_op | source)
XLA Modules:
  0.0 193.4 jit_solution(1824281415628476309)
XLA Ops:
  0.6 3.9 %pack.2 = bf16[16,192,384]{2,1,0:T(8,128)(2,1)} custom-call(bf16[6,64,1536]{2,1,0:T(8,128)(2,1)} %bitcast.59, bf16[6,64,1536]{2,1,0:T(8,128)(2,1)} %bitcast.60), custom_call_target="tpu_custom_call" | custom-call | bytes 4718592 | tf_op jit(solution)/shard_map/pack/pallas_call | solution.py:110
  4.5 8.4 %all-to-all-start = ((bf16[16,192,384]{2,1,0:T(8,128)(2,1)}), bf16[16,192,384]{2,1,0:T(8,128)(2,1)S(1)}, u32[]{:S(2)}, u32[]{:S(2)}) async-start(bf16[16,192,384]{2,1,0:T(8,128)(2,1)} %pack.2), calls=%async_computation | async-start | bytes 4718592 | tf_op jit(solution)/shard_map/all_to_all | solution.py:85
  13.0 13.0 %all-gather = bf16[8,6,1536]{2,1,0:T(8,128)(2,1)S(1)} all-gather(bf16[1,6,1536]{2,1,0:T(8,128)(2,1)S(1)} %maximum_bitcast_fusion), channel_id=1, replica_groups={{0,1,32,33,64,65,96,97},{2,3,34,35,66,67,98,99},{4,5,36,37,68,69,100,10..., dimensions={0}, use_global_device_ids=true | all-gather | bytes 165888 | tf_op jit(solution)/shard_map/all_gather | solution.py:541
  26.0 0.7 reshape.222.text_ref
  26.7 3.6 %pack.3 = bf16[16,144,384]{2,1,0:T(8,128)(2,1)} custom-call(bf16[6,64,1536]{2,1,0:T(8,128)(2,1)} %bitcast.58, bf16[48,1536]{1,0:T(8,128)(2,1)} %reshape.222.text_ref), custom_call_target="tpu_custom_call" | custom-call | bytes 3538944 | tf_op jit(solution)/shard_map/pack/pallas_call | solution.py:110
  30.3 15.2 %all-to-all-done = bf16[16,192,384]{2,1,0:T(8,128)(2,1)S(1)} async-done(((bf16[16,192,384]{2,1,0:T(8,128)(2,1)}), bf16[16,192,384]{2,1,0:T(8,128)(2,1)S(1)}, u32[]{:S(2)}, u32[]{:S(2)}) %all-to-all-start) | async-done | bytes 2359328 | tf_op jit(solution)/shard_map/all_to_all | solution.py:85
  45.5 1.3 dynamic-slice_bitcast_fusion
  46.8 0.0 collective-permute-start.1
  46.8 0.1 collective-permute-start
  46.9 0.4 copy-done.4
  47.3 0.8 select_reduce_fusion
  48.1 0.6 copy-done.15
  48.7 0.1 slice.23.valid_ref
  48.8 7.1 %all-to-all-start.1 = ((bf16[16,144,384]{2,1,0:T(8,128)(2,1)}), bf16[16,144,384]{2,1,0:T(8,128)(2,1)S(1)}, u32[]{:S(2)}, u32[]{:S(2)}) async-start(bf16[16,144,384]{2,1,0:T(8,128)(2,1)} %pack.3), calls=%async_computation.1 | async-start | bytes 3538944 | tf_op jit(solution)/shard_map/all_to_all | solution.py:85
  55.9 0.1 and_and_fusion
  56.0 0.0 collective-permute-done.1.other_ref
  56.0 1.0 copy-done.6
  57.0 2.7 %merge.3 = (bf16[2,768,384]{2,1,0:T(8,128)(2,1)}, bf16[2,768,384]{2,1,0:T(8,128)(2,1)}) custom-call(s32[1]{0:T(128)} %bitcast.10.c_ref, bf16[2,2,4,192,384]{4,3,2,1,0:T(8,128)(2,1)} %bitcast.52, bf16[2,4,192,384]{3,2,1,0:T(8,128)(2,1)} %copy-done.6), custom_call_target="tpu_custom_call" | custom-call | bytes 4718592 | tf_op jit(solution)/shard_map/merge/pallas_call | solution.py:166
  59.8 2.8 %merge.4.refs_0_.refs_1_ = bf16[2,2,768,384]{3,2,1,0:T(8,128)(2,1)} custom-call(s32[1]{0:T(128)} %bitcast.10.c_ref, bf16[2,2,4,192,384]{4,3,2,1,0:T(8,128)(2,1)} %bitcast.53, bf16[2,4,192,384]{3,2,1,0:T(8,128)(2,1)} %copy-done.6), custom_call_target="tpu_custom_call" | custom-call | bytes 4718592 | tf_op jit(solution)/shard_map/merge/pallas_call | solution.py:166
  62.6 1.9 collective-permute-start.5
  64.5 3.6 %collective-permute-start.6 = (bf16[2,2,768,384]{3,2,1,0:T(8,128)(2,1)}, bf16[2,2,768,384]{3,2,1,0:T(8,128)(2,1)}, u32[]{:S(2)}, u32[]{:S(2)}) collective-permute-start(bf16[2,2,768,384]{3,2,1,0:T(8,128)(2,1)} %merge.4.refs_0_.refs_1_), channel_id=1, source_target_pairs={{1,0},{3,2},{5,4},{7,6},{17,16},{19,18},{21,20},{23,22},{9,8},{11,... | collective-permute-start | bytes 7077896 | tf_op jit(solution)/shard_map/ppermute | solution.py:81
  68.2 0.1 broadcast_compare_fusion
  68.2 0.1 broadcast_add_fusion
  68.3 0.1 add_select_fusion
  68.4 0.0 collective-permute-done
  68.5 0.6 compare_reduce_fusion
  69.1 3.8 %collective-permute-start.3 = (bf16[2,768,384]{2,1,0:T(8,128)(2,1)}, bf16[2,768,384]{2,1,0:T(8,128)(2,1)}, u32[]{:S(2)}, u32[]{:S(2)}) collective-permute-start(bf16[2,768,384]{2,1,0:T(8,128)(2,1)} %get-tuple-element.20), channel_id=1, source_target_pairs={{2,0},{3,1},{4,2},{5,3},{6,4},{7,5},{18,16},{19,17},{20,18},{21,19... | collective-permute-start | bytes 3538952 | tf_op jit(solution)/shard_map/ppermute | solution.py:81
  72.9 1.3 collective-permute-start.2
  74.2 6.9 %all-to-all-done.1 = bf16[16,144,384]{2,1,0:T(8,128)(2,1)S(1)} async-done(((bf16[16,144,384]{2,1,0:T(8,128)(2,1)}), bf16[16,144,384]{2,1,0:T(8,128)(2,1)S(1)}, u32[]{:S(2)}, u32[]{:S(2)}) %all-to-all-start.1) | async-done | bytes 1769504 | tf_op jit(solution)/shard_map/all_to_all | solution.py:85
  81.1 1.1 dynamic-slice_bitcast_fusion.1
  82.3 0.0 collective-permute-start.4
  82.3 0.1 select_convert_fusion
  82.4 0.1 slice.28
  82.5 0.2 reshape.211
  82.7 0.5 copy.34
  83.3 1.1 reshape.212.q_ref.tk_ref.tv_ref
  84.4 5.1 %text_queries.1 = f32[256,512]{1,0:T(8,128)} custom-call(s32[1]{0:T(128)} %bitcast.share_ref, bf16[3,256,384]{2,1,0:T(8,128)(2,1)} %reshape.212.q_ref.tk_ref.tv_ref, bf16[3,256,384]{2,1,0:T(8,128)(2,1)} %reshape.212.q_ref.tk_ref.tv_ref, bf16[3,256,384]{2,1,0:T(8,128)(2,1)} %reshape.212.q_ref.tk_ref.tv_ref, bf16[2,2,16,128]{3,2,1,0:T(8,128)(2,1)} %copy-done.8, ...), custom_call_target="tpu_custom_call" | custom-call | flops 2113929216 | bytes 2752512 | tf_op jit(solution)/shard_map/text_queries/pallas_call | solution.py:472
  89.5 2.2 %reshape.216 = f32[128,2,512]{2,1,0:T(2,128)} reshape(f32[256,512]{1,0:T(8,128)} %text_queries.1) | data formatting | bytes 1048576 | tf_op jit(solution)/shard_map/reshape | solution.py:582
  91.6 9.3 %all-to-all-start.2 = ((f32[128,2,512]{2,1,0:T(2,128)}), f32[128,2,512]{2,1,0:T(2,128)S(1)}, u32[]{:S(2)}, u32[]{:S(2)}) async-start(f32[128,2,512]{2,1,0:T(2,128)} %reshape.216), calls=%async_computation.2 | async-start | bytes 1048576 | tf_op jit(solution)/shard_map/all_to_all | solution.py:85
  101.0 0.0 collective-permute-done.4.other_ref
  101.0 2.4 %merge.5.q_ref = bf16[2,2,384,384]{3,2,1,0:T(8,128)(2,1)} custom-call(s32[1]{0:T(128)} %bitcast.10.c_ref, bf16[2,2,4,144,384]{4,3,2,1,0:T(8,128)(2,1)} %bitcast.55, bf16[2,4,144,384]{3,2,1,0:T(8,128)(2,1)} %collective-permute-done.4.other_ref), custom_call_target="tpu_custom_call" | custom-call | bytes 3538944 | tf_op jit(solution)/shard_map/merge/pallas_call | solution.py:166
  103.4 3.6 %collective-permute-done.2.left_ref = bf16[2,768,384]{2,1,0:T(8,128)(2,1)} collective-permute-done((bf16[2,768,384]{2,1,0:T(8,128)(2,1)}, bf16[2,768,384]{2,1,0:T(8,128)(2,1)}, u32[]{:S(2)}, u32[]{:S(2)}) %collective-permute-start.2) | collective-permute-done | bytes 1179680 | tf_op jit(solution)/shard_map/ppermute | solution.py:81
  107.0 0.0 collective-permute-done.3.right_ref
  107.0 2.7 %join.1.refs_2_.refs_3_ = bf16[2,2,768,384]{3,2,1,0:T(8,128)(2,1)} custom-call(bf16[2,768,384]{2,1,0:T(8,128)(2,1)} %collective-permute-done.2.left_ref, bf16[2,768,384]{2,1,0:T(8,128)(2,1)} %collective-permute-done.3.right_ref), custom_call_target="tpu_custom_call" | custom-call | bytes 4718592 | tf_op jit(solution)/shard_map/join/pallas_call | solution.py:209
  109.8 2.0 %collective-permute-start.7 = (bf16[2,2,768,384]{3,2,1,0:T(8,128)(2,1)}, bf16[2,2,768,384]{3,2,1,0:T(8,128)(2,1)S(1)}, u32[]{:S(2)}, u32[]{:S(2)}) collective-permute-start(bf16[2,2,768,384]{3,2,1,0:T(8,128)(2,1)} %join.1.refs_2_.refs_3_), channel_id=1, source_target_pairs={{0,1},{1,32},{2,3},{3,34},{4,5},{5,36},{6,7},{7,38},{16,17},{17,48... | collective-permute-start | bytes 7077896 | tf_op jit(solution)/shard_map/ppermute | solution.py:81
  111.8 3.8 %collective-permute-start.8 = (bf16[2,2,768,384]{3,2,1,0:T(8,128)(2,1)}, bf16[2,2,768,384]{3,2,1,0:T(8,128)(2,1)S(1)}, u32[]{:S(2)}, u32[]{:S(2)}) collective-permute-start(bf16[2,2,768,384]{3,2,1,0:T(8,128)(2,1)} %join.1.refs_2_.refs_3_), channel_id=1, source_target_pairs={{1,0},{3,2},{5,4},{7,6},{17,16},{19,18},{21,20},{23,22},{9,8},{11,... | collective-permute-start | bytes 7077896 | tf_op jit(solution)/shard_map/ppermute | solution.py:81
  115.7 0.0 collective-permute-done.6.refs_4_.refs_5_
  115.7 30.2 %near_cells.1 = (f32[2,768,384]{2,1,0:T(8,128)S(1)}, f32[2,768,384]{2,1,0:T(8,128)S(1)}) custom-call(bf16[2,2,384,384]{3,2,1,0:T(8,128)(2,1)S(1)} %copy-done.2, bf16[3,256,384]{2,1,0:T(8,128)(2,1)S(1)} %copy-done.3, bf16[3,256,384]{2,1,0:T(8,128)(2,1)S(1)} %copy-done.3, bf16[6,2,16,128]{3,2,1,0:T(8,128)(2,1)S(1)} %pad_maximum_fusion.bias_ref, ...), custom_call_target="tpu_custom_call" | custom-call | flops 34426847232 | bytes 7471104 | tf_op jit(solution)/shard_map/near_cells/pallas_call | solution.py:370
  145.9 0.0 collective-permute-done.7.refs_0_.refs_1_
  145.9 19.3 %side_cells.1 = bf16[2,2,384,384]{3,2,1,0:T(8,128)(2,1)S(1)} custom-call(s32[2]{0:T(128)S(1)} %slice.23.valid_ref, bf16[2,2,384,384]{3,2,1,0:T(8,128)(2,1)S(1)} %copy-done.2, f32[2,768,384]{2,1,0:T(8,128)S(1)} %get-tuple-element.24.sum_ref, f32[2,768,384]{2,1,0:T(8,128)S(1)} %get-tuple-element.25.mark_ref, ...), custom_call_target="tpu_custom_call" | custom-call | flops 16307453952 | bytes 3538944 | tf_op jit(solution)/shard_map/side_cells/pallas_call | solution.py:422
  165.3 0.0 copy-start.7
  165.3 0.0 slice-start
  165.3 0.1 dynamic-slice_bitcast_fusion.2
  165.4 3.8 %collective-permute-start.9 = (bf16[384,384]{1,0:T(8,128)(2,1)S(1)}, bf16[384,384]{1,0:T(8,128)(2,1)S(1)}, u32[]{:S(2)}, u32[]{:S(2)}) collective-permute-start(bf16[384,384]{1,0:T(8,128)(2,1)S(1)} %get-tuple-element.33), channel_id=1, source_target_pairs={{0,0},{1,16},{2,4},{3,20},{4,8},{5,24},{6,12},{7,28},{16,1},{17,17... | collective-permute-start | bytes 884744 | tf_op jit(solution)/shard_map/ppermute | solution.py:81
  169.2 0.8 collective-permute-start.10
  170.0 0.5 collective-permute-start.11
  170.6 2.2 %collective-permute-start.12 = (bf16[384,384]{1,0:T(8,128)(2,1)S(1)}, bf16[384,384]{1,0:T(8,128)(2,1)S(1)}, u32[]{:S(2)}, u32[]{:S(2)}) collective-permute-start(bf16[384,384]{1,0:T(8,128)(2,1)S(1)} %get-tuple-element.30), channel_id=1, source_target_pairs={{0,3},{1,19},{2,7},{3,23},{4,11},{5,27},{6,15},{7,31},{16,0},{17,1... | collective-permute-start | bytes 884744 | tf_op jit(solution)/shard_map/ppermute | solution.py:81
  172.7 2.4 %text_sum.1 = bf16[2,1536]{1,0:T(2,128)(2,1)} custom-call(f32[4,2,2,8,2,512]{5,4,3,2,1,0:T(2,128)} %bitcast.57), custom_call_target="tpu_custom_call" | custom-call | bytes 524288 | tf_op jit(solution)/shard_map/text_sum/pallas_call | solution.py:506
  175.1 5.8 %convolution_convert_fusion = bf16[2,3072]{1,0:T(2,128)(2,1)} fusion(bf16[2,1536]{1,0:T(2,128)(2,1)} %text_sum.1, bf16[1536,3072]{1,0:T(8,128)(2,1)} %param.19), kind=kOutput, calls=%fused_computation | convolution fusion | flops 18880512 | bytes 9455616 | tf_op jit(solution)/shard_map/dot_general | solution.py:599
  180.9 0.4 collective-permute-done.9.first
  181.3 0.6 collective-permute-done.10.second
  181.9 0.0 collective-permute-done.11.third
  181.9 5.3 %collective-permute-done.12.fourth = bf16[384,384]{1,0:T(8,128)(2,1)S(1)} collective-permute-done((bf16[384,384]{1,0:T(8,128)(2,1)S(1)}, bf16[384,384]{1,0:T(8,128)(2,1)S(1)}, u32[]{:S(2)}, u32[]{:S(2)}) %collective-permute-start.12) | collective-permute-done | bytes 294944 | tf_op jit(solution)/shard_map/ppermute | solution.py:81
  187.2 6.2 %project.1 = bf16[384,3072]{1,0:T(8,128)(2,1)} custom-call(s32[4]{0:T(128)S(1)} %and_select_fusion.1.from_ref, bf16[384,384]{1,0:T(8,128)(2,1)S(1)} %collective-permute-done.9.first, bf16[384,384]{1,0:T(8,128)(2,1)S(1)} %collective-permute-done.10.second, bf16[384,384]{1,0:T(8,128)(2,1)S(1)} %collective-permute-done.11.third, ...), custom_call_target="tpu_custom_call" | custom-call | flops 3623878656 | bytes 9437184 | tf_op jit(solution)/shard_map/project/pallas_call | solution.py:236
  (56 shorter events, 0.2 us)
Async XLA Ops:
  4.5 8.4 %copy-start.10 = (bf16[2,1536]{1,0:T(2,128)(2,1)S(1)}, bf16[2,1536]{1,0:T(2,128)(2,1)}, u32[]{:S(2)}) copy-start(bf16[2,1536]{1,0:T(2,128)(2,1)} %param.15) | copy-start | bytes 18436
  4.5 8.4 %copy-start.11 = (bf16[2,1536]{1,0:T(2,128)(2,1)S(1)}, bf16[2,1536]{1,0:T(2,128)(2,1)}, u32[]{:S(2)}) copy-start(bf16[2,1536]{1,0:T(2,128)(2,1)} %param.14) | copy-start | bytes 18436
  4.5 8.4 %copy-start.12 = (bf16[2,1536]{1,0:T(2,128)(2,1)S(1)}, bf16[2,1536]{1,0:T(2,128)(2,1)}, u32[]{:S(2)}) copy-start(bf16[2,1536]{1,0:T(2,128)(2,1)} %param.13) | copy-start | bytes 18436
  4.5 40.9 %all-to-all-start = ((bf16[16,192,384]{2,1,0:T(8,128)(2,1)}), bf16[16,192,384]{2,1,0:T(8,128)(2,1)S(1)}, u32[]{:S(2)}, u32[]{:S(2)}) async-start(bf16[16,192,384]{2,1,0:T(8,128)(2,1)} %pack.2), calls=%async_computation | async-start | bytes 4718592 | tf_op jit(solution)/shard_map/all_to_all | solution.py:85
  26.7 20.1 %copy-start.9 = (s32[1,16,27]{2,1,0:T(8,128)S(1)}, s32[1,16,27]{2,1,0:T(8,128)}, u32[]{:S(2)}) copy-start(s32[1,16,27]{2,1,0:T(8,128)} %param.16) | copy-start | bytes 5188
  45.5 1.8 copy-start.4
  46.8 9.2 %collective-permute-start.1 = (bf16[2,4,192,384]{3,2,1,0:T(8,128)(2,1)}, bf16[2,4,192,384]{3,2,1,0:T(8,128)(2,1)S(1)}, u32[]{:S(2)}, u32[]{:S(2)}) collective-permute-start(bf16[2,4,192,384]{3,2,1,0:T(8,128)(2,1)} %dynamic-slice_bitcast_fusion), channel_id=1, source_target_pairs={{0,1},{1,0},{2,3},{3,2},{4,5},{5,4},{6,7},{7,6},{16,17},{17,16},{1... | collective-permute-start | bytes 3538952 | tf_op jit(solution)/shard_map/ppermute | solution.py:81
  46.8 21.6 %collective-permute-start = (s32[1,16,27]{2,1,0:T(8,128)S(1)}, s32[1,16,27]{2,1,0:T(8,128)S(1)}, u32[]{:S(2)}, u32[]{:S(2)}) collective-permute-start(s32[1,16,27]{2,1,0:T(8,128)S(1)} %copy-done.9), channel_id=1, source_target_pairs={{0,16},{1,17},{2,18},{3,19},{4,20},{5,21},{6,22},{7,23},{16,0},{17... | collective-permute-start | bytes 5192 | tf_op jit(solution)/shard_map/ppermute | solution.py:81
  47.3 0.8 copy-start.13
  48.1 0.6 copy-start.15
  48.8 32.3 %all-to-all-start.1 = ((bf16[16,144,384]{2,1,0:T(8,128)(2,1)}), bf16[16,144,384]{2,1,0:T(8,128)(2,1)S(1)}, u32[]{:S(2)}, u32[]{:S(2)}) async-start(bf16[16,144,384]{2,1,0:T(8,128)(2,1)} %pack.3), calls=%async_computation.1 | async-start | bytes 3538944 | tf_op jit(solution)/shard_map/all_to_all | solution.py:85
  56.0 1.0 copy-start.6
  59.8 8.4 %copy-start.16 = (s32[4]{0:T(128)S(1)}, s32[4]{0:T(128)}, u32[]{:S(2)}) copy-start(s32[4]{0:T(128)} %copy-done.15) | copy-start | bytes 52
  59.8 8.5 %copy-start.14 = (s32[4]{0:T(128)S(1)}, s32[4]{0:T(128)}, u32[]{:S(2)}) copy-start(s32[4]{0:T(128)} %copy-done.13) | copy-start | bytes 52
  62.6 53.1 %collective-permute-start.5 = (bf16[2,2,768,384]{3,2,1,0:T(8,128)(2,1)}, bf16[2,2,768,384]{3,2,1,0:T(8,128)(2,1)}, u32[]{:S(2)}, u32[]{:S(2)}) collective-permute-start(bf16[2,2,768,384]{3,2,1,0:T(8,128)(2,1)} %merge.4.refs_0_.refs_1_), channel_id=1, source_target_pairs={{0,1},{1,32},{2,3},{3,34},{4,5},{5,36},{6,7},{7,38},{16,17},{17,48... | collective-permute-start | bytes 7077896 | tf_op jit(solution)/shard_map/ppermute | solution.py:81
  64.5 51.2 %collective-permute-start.6 = (bf16[2,2,768,384]{3,2,1,0:T(8,128)(2,1)}, bf16[2,2,768,384]{3,2,1,0:T(8,128)(2,1)}, u32[]{:S(2)}, u32[]{:S(2)}) collective-permute-start(bf16[2,2,768,384]{3,2,1,0:T(8,128)(2,1)} %merge.4.refs_0_.refs_1_), channel_id=1, source_target_pairs={{1,0},{3,2},{5,4},{7,6},{17,16},{19,18},{21,20},{23,22},{9,8},{11,... | collective-permute-start | bytes 7077896 | tf_op jit(solution)/shard_map/ppermute | solution.py:81
  69.1 37.9 %collective-permute-start.3 = (bf16[2,768,384]{2,1,0:T(8,128)(2,1)}, bf16[2,768,384]{2,1,0:T(8,128)(2,1)}, u32[]{:S(2)}, u32[]{:S(2)}) collective-permute-start(bf16[2,768,384]{2,1,0:T(8,128)(2,1)} %get-tuple-element.20), channel_id=1, source_target_pairs={{2,0},{3,1},{4,2},{5,3},{6,4},{7,5},{18,16},{19,17},{20,18},{21,19... | collective-permute-start | bytes 3538952 | tf_op jit(solution)/shard_map/ppermute | solution.py:81
  72.9 34.1 %collective-permute-start.2 = (bf16[2,768,384]{2,1,0:T(8,128)(2,1)}, bf16[2,768,384]{2,1,0:T(8,128)(2,1)}, u32[]{:S(2)}, u32[]{:S(2)}) collective-permute-start(bf16[2,768,384]{2,1,0:T(8,128)(2,1)} %get-tuple-element.22), channel_id=1, source_target_pairs={{0,2},{1,3},{2,4},{3,5},{4,6},{5,7},{16,18},{17,19},{18,20},{19,21... | collective-permute-start | bytes 3538952 | tf_op jit(solution)/shard_map/ppermute | solution.py:81
  81.1 2.1 %copy-start.5 = (bf16[16,144,384]{2,1,0:T(8,128)(2,1)}, bf16[16,144,384]{2,1,0:T(8,128)(2,1)S(1)}, u32[]{:S(2)}) copy-start(bf16[16,144,384]{2,1,0:T(8,128)(2,1)S(1)} %all-to-all-done.1) | copy-start | bytes 5308420
  82.3 18.7 %collective-permute-start.4 = (bf16[2,4,144,384]{3,2,1,0:T(8,128)(2,1)}, bf16[2,4,144,384]{3,2,1,0:T(8,128)(2,1)}, u32[]{:S(2)}, u32[]{:S(2)}) collective-permute-start(bf16[2,4,144,384]{3,2,1,0:T(8,128)(2,1)} %dynamic-slice_bitcast_fusion.1), channel_id=1, source_target_pairs={{0,1},{1,0},{2,3},{3,2},{4,5},{5,4},{6,7},{7,6},{16,17},{17,16},{1... | collective-permute-start | bytes 2654216 | tf_op jit(solution)/shard_map/ppermute | solution.py:81
  82.4 1.9 %copy-start.8 = (bf16[2,2,16,128]{3,2,1,0:T(8,128)(2,1)}, bf16[2,2,16,128]{3,2,1,0:T(8,128)(2,1)S(1)}, u32[]{:S(2)}) copy-start(bf16[2,2,16,128]{3,2,1,0:T(8,128)(2,1)S(1)} %get-tuple-element.37.bias_ref) | copy-start | bytes 49156
  91.6 73.6 %all-to-all-start.2 = ((f32[128,2,512]{2,1,0:T(2,128)}), f32[128,2,512]{2,1,0:T(2,128)S(1)}, u32[]{:S(2)}, u32[]{:S(2)}) async-start(f32[128,2,512]{2,1,0:T(2,128)} %reshape.216), calls=%async_computation.2 | async-start | bytes 1048576 | tf_op jit(solution)/shard_map/all_to_all | solution.py:85
  103.4 12.3 %copy-start = (bf16[2,2,768,384]{3,2,1,0:T(8,128)(2,1)S(1)}, bf16[2,2,768,384]{3,2,1,0:T(8,128)(2,1)}, u32[]{:S(2)}) copy-start(bf16[2,2,768,384]{3,2,1,0:T(8,128)(2,1)} %merge.4.refs_0_.refs_1_) | copy-start | bytes 7077892
  103.4 12.3 %copy-start.2 = (bf16[2,2,384,384]{3,2,1,0:T(8,128)(2,1)S(1)}, bf16[2,2,384,384]{3,2,1,0:T(8,128)(2,1)}, u32[]{:S(2)}) copy-start(bf16[2,2,384,384]{3,2,1,0:T(8,128)(2,1)} %merge.5.q_ref) | copy-start | bytes 3538948
  103.4 12.3 %copy-start.3 = (bf16[3,256,384]{2,1,0:T(8,128)(2,1)S(1)}, bf16[3,256,384]{2,1,0:T(8,128)(2,1)}, u32[]{:S(2)}) copy-start(bf16[3,256,384]{2,1,0:T(8,128)(2,1)} %reshape.212.q_ref.tk_ref.tv_ref) | copy-start | bytes 1769476
  109.8 36.1 %copy-start.1 = (bf16[2,2,768,384]{3,2,1,0:T(8,128)(2,1)S(1)}, bf16[2,2,768,384]{3,2,1,0:T(8,128)(2,1)}, u32[]{:S(2)}) copy-start(bf16[2,2,768,384]{3,2,1,0:T(8,128)(2,1)} %join.1.refs_2_.refs_3_) | copy-start | bytes 7077892
  109.8 36.1 %collective-permute-start.7 = (bf16[2,2,768,384]{3,2,1,0:T(8,128)(2,1)}, bf16[2,2,768,384]{3,2,1,0:T(8,128)(2,1)S(1)}, u32[]{:S(2)}, u32[]{:S(2)}) collective-permute-start(bf16[2,2,768,384]{3,2,1,0:T(8,128)(2,1)} %join.1.refs_2_.refs_3_), channel_id=1, source_target_pairs={{0,1},{1,32},{2,3},{3,34},{4,5},{5,36},{6,7},{7,38},{16,17},{17,48... | collective-permute-start | bytes 7077896 | tf_op jit(solution)/shard_map/ppermute | solution.py:81
  111.8 34.1 %collective-permute-start.8 = (bf16[2,2,768,384]{3,2,1,0:T(8,128)(2,1)}, bf16[2,2,768,384]{3,2,1,0:T(8,128)(2,1)S(1)}, u32[]{:S(2)}, u32[]{:S(2)}) collective-permute-start(bf16[2,2,768,384]{3,2,1,0:T(8,128)(2,1)} %join.1.refs_2_.refs_3_), channel_id=1, source_target_pairs={{1,0},{3,2},{5,4},{7,6},{17,16},{19,18},{21,20},{23,22},{9,8},{11,... | collective-permute-start | bytes 7077896 | tf_op jit(solution)/shard_map/ppermute | solution.py:81
  165.3 7.4 %copy-start.7 = (f32[128,2,512]{2,1,0:T(2,128)}, f32[128,2,512]{2,1,0:T(2,128)S(1)}, u32[]{:S(2)}) copy-start(f32[128,2,512]{2,1,0:T(2,128)S(1)} %all-to-all-done.2) | copy-start | bytes 1572868
  165.3 21.9 %slice-start = ((s8[9437184]{0:T(1024)(128)(4,1)}), s8[1048576]{0:T(1024)(128)(4,1)S(1)}, s32[]{:S(2)}) async-start(s8[9437184]{0:T(1024)(128)(4,1)} %bitcast.49), calls=%async_computation.3 | async-start | bytes 2097152
  165.4 15.9 %collective-permute-start.9 = (bf16[384,384]{1,0:T(8,128)(2,1)S(1)}, bf16[384,384]{1,0:T(8,128)(2,1)S(1)}, u32[]{:S(2)}, u32[]{:S(2)}) collective-permute-start(bf16[384,384]{1,0:T(8,128)(2,1)S(1)} %get-tuple-element.33), channel_id=1, source_target_pairs={{0,0},{1,16},{2,4},{3,20},{4,8},{5,24},{6,12},{7,28},{16,1},{17,17... | collective-permute-start | bytes 884744 | tf_op jit(solution)/shard_map/ppermute | solution.py:81
  169.2 12.7 %collective-permute-start.10 = (bf16[384,384]{1,0:T(8,128)(2,1)S(1)}, bf16[384,384]{1,0:T(8,128)(2,1)S(1)}, u32[]{:S(2)}, u32[]{:S(2)}) collective-permute-start(bf16[384,384]{1,0:T(8,128)(2,1)S(1)} %get-tuple-element.32), channel_id=1, source_target_pairs={{0,1},{1,17},{2,5},{3,21},{4,9},{5,25},{6,13},{7,29},{16,2},{17,18... | collective-permute-start | bytes 884744 | tf_op jit(solution)/shard_map/ppermute | solution.py:81
  170.0 11.9 %collective-permute-start.11 = (bf16[384,384]{1,0:T(8,128)(2,1)S(1)}, bf16[384,384]{1,0:T(8,128)(2,1)S(1)}, u32[]{:S(2)}, u32[]{:S(2)}) collective-permute-start(bf16[384,384]{1,0:T(8,128)(2,1)S(1)} %get-tuple-element.31), channel_id=1, source_target_pairs={{0,2},{1,18},{2,6},{3,22},{4,10},{5,26},{6,14},{7,30},{16,3},{17,1... | collective-permute-start | bytes 884744 | tf_op jit(solution)/shard_map/ppermute | solution.py:81
  170.6 16.6 %collective-permute-start.12 = (bf16[384,384]{1,0:T(8,128)(2,1)S(1)}, bf16[384,384]{1,0:T(8,128)(2,1)S(1)}, u32[]{:S(2)}, u32[]{:S(2)}) collective-permute-start(bf16[384,384]{1,0:T(8,128)(2,1)S(1)} %get-tuple-element.30), channel_id=1, source_target_pairs={{0,3},{1,19},{2,7},{3,23},{4,11},{5,27},{6,15},{7,31},{16,0},{17,1... | collective-permute-start | bytes 884744 | tf_op jit(solution)/shard_map/ppermute | solution.py:81
  175.1 12.1 %slice-start.1 = ((s8[9437184]{0:T(1024)(128)(4,1)}), s8[4194304]{0:T(1024)(128)(4,1)S(1)}, s32[]{:S(2)}) async-start(s8[9437184]{0:T(1024)(128)(4,1)} %bitcast.49), calls=%async_computation.4 | async-start | bytes 8388608
  175.1 12.1 %slice-start.2 = ((s8[9437184]{0:T(1024)(128)(4,1)}), s8[4194304]{0:T(1024)(128)(4,1)S(1)}, s32[]{:S(2)}) async-start(s8[9437184]{0:T(1024)(128)(4,1)} %bitcast.49), calls=%async_computation.5 | async-start | bytes 8388608

commit v4 on v3

--- a/solution.py
+++ b/solution.py
@@ -18,7 +18,7 @@
 GH = GW // HD
 TXT = 256
 EXTRA = 16
-COLUMNS = 512
+COLUMNS = 1024
 AXES = ("tm", "space")
 SCALE = HD**-0.5 * math.log2(math.e)
 MASKED = -1e30
@@ -51,12 +51,13 @@
     return pairs
 
 
-def in_time(steps):
-    def target(y, z, x, c):
-        moment = 2 * y + c + steps
-        return (moment // 2, z, x, moment % 2) if 0 <= moment < 8 else None
-
-    return route(target)
+def to_other_chip(y, z, x, c):
+    if c == 0:
+        return (y - 1, z, x, 1) if y > 0 else None
+    return (y + 1, z, x, 0) if y < 3 else None
+
+
+OTHER_CHIP = route(to_other_chip)
 
 
 def in_columns(steps):
@@ -119,24 +120,33 @@
     )(*[array.reshape(TF, 8 * TC, 4 * GW) for array in rasters], *text)
 
 
-def merge_sides_kernel(c_ref, mine_ref, other_ref, low_ref, high_ref):
+def copy_pieces(get, put):
     for x in range(4):
-        for part, get in enumerate((lambda s: mine_ref[0, 0, x, s], lambda s: other_ref[0, x, s])):
-            for w, ref in enumerate((low_ref, high_ref)):
-                for kind in range(2):
-                    start = (2 * x + part) * PIECE
-                    rows = slice((2 * w + kind) * PIECE, (2 * w + kind + 1) * PIECE)
-                    ref[kind, start : start + PIECE] = get(rows)
-
-
-def merge_kernel(c_ref, mine_ref, other_ref, own_ref):
-    for x in range(4):
-        for part, get in enumerate((lambda s: mine_ref[0, 0, x, s], lambda s: other_ref[0, x, s])):
+        for part in range(2):
             for w in range(2):
                 for kind in range(2):
                     start = (2 * x + part) * PIECE
                     rows = slice((2 * w + kind) * PIECE, (2 * w + kind + 1) * PIECE)
-                    own_ref[kind, w, start : start + PIECE] = get(rows)
+                    put(kind, w, slice(start, start + PIECE), get(part, x, rows))
+
+
+def merge_sides_kernel(c_ref, mine_ref, other_ref, low_ref, high_ref):
+    parts, columns = (mine_ref, other_ref), (low_ref, high_ref)
+
+    def put(kind, w, rows, value):
+        columns[w][kind, rows] = value
+
+    copy_pieces(lambda part, x, rows: parts[part][0, 0, x, rows], put)
+
+
+def merge_kernel(c_ref, mine_ref, other_ref, own_ref, near_ref):
+    parts = (mine_ref, other_ref)
+    for place, out_ref in ((c_ref[0], own_ref), (1 - c_ref[0], near_ref)):
+
+        def put(kind, w, rows, value, out_ref=out_ref):
+            out_ref[kind, w, rows] = value
+
+        copy_pieces(lambda part, x, rows, place=place: parts[part][0, place, x, rows], put)
 
 
 def merge_queries_kernel(c_ref, mine_ref, other_ref, q_ref):
@@ -154,25 +164,12 @@
                 q_ref[w, 0, start : start + 2 * TC] = jnp.concatenate(both).astype(jnp.bfloat16)
 
 
-def from_other_core(core, got):
-    rows = got.shape[1]
-    pieces = got.reshape(2, 2, 4, rows, GW)
-    other = send(lax.dynamic_index_in_dim(pieces, 1 - core[0], 1, keepdims=False), OTHER_CORE)
-    return pieces, other
-
-
-def merge(core, pieces, other, kernel, out_specs, out_shape):
+def merge(core, pieces, other, kernel, piece_specs, out_specs, out_shape):
     rows = pieces.shape[3]
     return pl.pallas_call(
         kernel,
         grid_spec=pltpu.PrefetchScalarGridSpec(
-            num_scalar_prefetch=1,
-            grid=(2,),
-            in_specs=[
-                pl.BlockSpec((1, 1, 4, rows, GW), lambda b, c: (b, c[0], 0, 0, 0)),
-                pl.BlockSpec((1, 4, rows, GW), lambda b, c: (b, 0, 0, 0)),
-            ],
-            out_specs=out_specs,
+            num_scalar_prefetch=1, grid=(2,), in_specs=piece_specs, out_specs=out_specs
         ),
         out_shape=out_shape,
         compiler_params=pltpu.CompilerParams(vmem_limit_bytes=56 * 2**20),
@@ -182,21 +179,32 @@
 
 
 def merge_sides(core, pieces, other):
+    piece = pl.BlockSpec((1, 1, 4, 4 * PIECE, GW), lambda b, c: (b, c[0], 0, 0, 0))
     cell = pl.BlockSpec((2, TILE, GW), lambda b, c: (0, b, 0))
     shape = jax.ShapeDtypeStruct((2, CELL, GW), jnp.bfloat16)
-    return merge(core, pieces, other, merge_sides_kernel, [cell, cell], [shape, shape])
+    return merge(
+        core, pieces, other, merge_sides_kernel, [piece, piece], [cell, cell], [shape, shape]
+    )
 
 
 def merge_keys(core, pieces, other):
+    piece = pl.BlockSpec((1, 2, 4, 4 * PIECE, GW), lambda b, c: (b, 0, 0, 0, 0))
     both = pl.BlockSpec((2, 2, TILE, GW), lambda b, c: (0, 0, b, 0))
     shape = jax.ShapeDtypeStruct((2, 2, CELL, GW), jnp.bfloat16)
-    return merge(core, pieces, other, merge_kernel, both, shape)
-
-
-def merge_queries(core, pieces, other):
+    return merge(core, pieces, other, merge_kernel, [piece, piece], [both, both], [shape, shape])
+
+
+def merge_queries(core, got):
+    rows = got.shape[1]
+    pieces = got.reshape(2, 2, 4, rows, GW)
+    other = send(lax.dynamic_index_in_dim(pieces, 1 - core[0], 1, keepdims=False), OTHER_CORE)
+    specs = [
+        pl.BlockSpec((1, 1, 4, rows, GW), lambda b, c: (b, c[0], 0, 0, 0)),
+        pl.BlockSpec((1, 4, rows, GW), lambda b, c: (b, 0, 0, 0)),
+    ]
     spec = pl.BlockSpec((2, 1, TILE, GW), lambda b, c: (0, b, 0, 0))
     shape = jax.ShapeDtypeStruct((2, 2, TILE, GW), jnp.bfloat16)
-    return merge(core, pieces, other, merge_queries_kernel, spec, shape)
+    return merge(core, pieces, other, merge_queries_kernel, specs, spec, shape)
 
 
 def join_kernel(left_ref, right_ref, out_ref):
@@ -337,12 +345,18 @@
             )
             for i in range(2 * cells)
         ]
-        state, _ = late(query, state, blocks)
+        state, step = late(query, state, blocks)
         sum_ref[w] = state[1][:, :HD]
         mark_ref[w] = mark_of(state)
-
-    run(0, add_all)
-    run(1, add_all)
+        return step
+
+    step = jnp.maximum(run(0, add_all_late), run(1, add_all_late))
+
+    @pl.when(step > TOO_FAR)
+    def _():
+        @pl.loop(0, 2)
+        def _(w):
+            run(w, add_all)
 
 
 def cell_specs(number):
@@ -379,7 +393,7 @@
         + cell_specs(len(cells)),
         out_specs=[state, state],
         out_shape=[shape, shape],
-        compiler_params=pltpu.CompilerParams(vmem_limit_bytes=40 * 2**20),
+        compiler_params=pltpu.CompilerParams(vmem_limit_bytes=52 * 2**20),
         cost_estimate=cost(2 * CELL, 2 * len(cells) * CELL + TXT, GH),
         name="near_cells",
     )(queries, text_all, text_all, bias, *doubled(cells))
@@ -412,8 +426,9 @@
 
     @pl.when(step > TOO_FAR)
     def _():
-        run(0, add_all)
-        run(1, add_all)
+        @pl.loop(0, 2)
+        def _(w):
+            run(w, add_all)
 
 
 def side(valid, queries, state, bias, cells):
@@ -432,7 +447,7 @@
         + cell_specs(3),
         out_specs=query,
         out_shape=jax.ShapeDtypeStruct((2, 2, TILE, GW), jnp.bfloat16),
-        compiler_params=pltpu.CompilerParams(vmem_limit_bytes=40 * 2**20),
+        compiler_params=pltpu.CompilerParams(vmem_limit_bytes=52 * 2**20),
         cost_estimate=cost(2 * CELL, 3 * CELL, GH),
         name="side_cells",
     )(valid, queries, *state, bias, *doubled(cells))
@@ -543,15 +558,17 @@
     got, packed_queries = lax.optimization_barrier((got, packed_queries))
 
     core = c.reshape(1)
-    pieces, other = from_other_core(core, got)
+    pieces = got.reshape(2, 2, 4, 4 * PIECE, GW)
+    other = send(pieces, OTHER_CORE)
     low, high = merge_sides(core, pieces, other)
 
     left, right = send(high, in_columns(1)), send(low, in_columns(-1))
     other, _ = lax.optimization_barrier((other, low))
-    own = merge_keys(core, pieces, other)
-    past, future = send(own, in_time(1)), send(own, in_time(-1))
+    own, beside = merge_keys(core, pieces, other)
+    beyond = send(own, OTHER_CHIP)
+
     got_queries = exchange(packed_queries, PLANES)
-    queries = merge_queries(core, *from_other_core(core, got_queries))
+    queries = merge_queries(core, got_queries)
 
     text_all = got_queries[:, 2 * PIECE :].reshape(2, 2, 4, 4, 2, 3, 2, GW)
     text_all = text_all.transpose(5, 3, 1, 0, 2, 4, 6, 7).reshape(3, TXT, GW)
@@ -573,7 +590,11 @@
     listed = jnp.pad(listed, ((0, 0), (0, 0), (0, 0), (0, HD - 4)), constant_values=True)
     allowed = listed[:, :, :, None, :] & fine[None, :, None, :, None]
     bias = jnp.where(allowed, 0.0, MASKED).astype(jnp.bfloat16)
-    near_bias = jnp.concatenate([bias[1, 1:3], bias[0, 1:3], bias[2, 1:3]])
+    even_core = c == 0
+    beside_bias = jnp.where(even_core, bias[2], bias[0])
+    beyond_bias = jnp.where(even_core, bias[0], bias[2])
+    bias = jnp.stack([bias[1], beside_bias, beyond_bias])
+    near_bias = bias[:, 1:3].reshape(6, 2, EXTRA, HD)
     side_bias = jnp.concatenate([bias[:, 0], bias[:, 3]])
 
     member = (4 * y + x) * 2 + c
@@ -581,10 +602,10 @@
     left, right, _, queries = lax.optimization_barrier((left, right, parts, queries))
     parts = exchange(parts.reshape(128, 2, GW + HD), None)
     sides = join(left, right)
-    past_sides, future_sides = send(sides, in_time(1)), send(sides, in_time(-1))
-
-    state = near(queries, text_all, near_bias, [own, past, future])
-    attended = side(valid[1:3], queries, state, side_bias, [past_sides, sides, future_sides])
+    beside_sides, beyond_sides = send(sides, OTHER_CORE), send(sides, OTHER_CHIP)
+
+    state = near(queries, text_all, near_bias, [own, beside, beyond])
+    attended = side(valid[1:3], queries, state, side_bias, [sides, beside_sides, beyond_sides])
     parts, attended = lax.optimization_barrier((parts, attended))
     attended = attended.reshape(4, TILE, GW)
 

time: 196 us -> 192 us (0.980)
  starting transfers between devices: 48.7 us -> 42.1 us
  waiting for transfers between devices: 32.1 us -> 34.9 us
    ppermute x13 -> x12, starting transfers between devices: 23.9 us -> 17.2 us  [send(): return lax.ppermute(value, AXES, pairs)]
    all_to_all x3, waiting for transfers between devices: 22.1 us -> 26.9 us  [exchange(): lax.all_to_all(value, AXES, split_axis=0, concat_axis=0, tiled=True, axis...]
    ppermute x13 -> x12, waiting for transfers between devices: 9.95 us -> 7.99 us  [send(): return lax.ppermute(value, AXES, pairs)]
  transfers between devices with their start and end apart: 16 -> 15, of which waited for: 6 -> 6; matrix products, arithmetic and copies ran while one was open for 7% -> 8% of each run, Pallas kernels for 37% -> 38%
where the time goes in v4:
time: 192 us; the launch traced here: 190 us
  Pallas kernels  81.7 us (43%)
  starting transfers between devices  42.1 us (22%)
  waiting for transfers between devices  34.9 us (18%)
  blocking collectives  13 us (7%)
  local copies, waits for them, and re-layouts  10 us (5%)
  matrix products  5.78 us (3%)
    pallas_call x1, Pallas kernels, near(): pl.pallas_call(functools.partial(near_kernel, len(cells)), grid=(GH,), in...  29.6 us
    all_to_all x3, waiting for transfers between devices, exchange(): lax.all_to_all(value, AXES, split_axis=0, concat_axis=0, tiled=True, axis...  26.9 us
    all_to_all x3, starting transfers between devices, exchange(): lax.all_to_all(value, AXES, split_axis=0, concat_axis=0, tiled=True, axis...  24.9 us
    pallas_call x1, Pallas kernels, side(): pl.pallas_call(side_kernel, grid=(GH,), in_specs=[pl.BlockSpec(memory_spa...  19.3 us
    ppermute x12, starting transfers between devices, send(): return lax.ppermute(value, AXES, pairs)  17.2 us
    all_gather x1, blocking collectives, shards(): lax.all_gather(text_rows, AXES, axis_index_groups=SAME_PLACE, tiled=True)  13 us
    pallas_call x3, Pallas kernels, merge(): pl.pallas_call(kernel, grid_spec=pltpu.PrefetchScalarGridSpec(num_scalar_...  9.18 us
    ppermute x12, waiting for transfers between devices, send(): return lax.ppermute(value, AXES, pairs)  7.99 us
  transfers between devices with their start and end apart: 15, of which 6 were waited for; matrix products, arithmetic and copies ran while one was open for 8% of the time, Pallas kernels for 38%

profile of v4, /device:TPU:14, one launch (start us, length us, event | category | flops | bytes accessed | tf_op | source)
XLA Modules:
  0.0 189.9 jit_solution(4255513334293619195)
XLA Ops:
  0.6 3.9 %pack.2 = bf16[16,192,384]{2,1,0:T(8,128)(2,1)} custom-call(bf16[6,64,1536]{2,1,0:T(8,128)(2,1)} %bitcast.49, bf16[6,64,1536]{2,1,0:T(8,128)(2,1)} %bitcast.50), custom_call_target="tpu_custom_call" | custom-call | bytes 4718592 | tf_op jit(solution)/shard_map/pack/pallas_call | solution.py:111
  4.5 8.4 %all-to-all-start = ((bf16[16,192,384]{2,1,0:T(8,128)(2,1)}), bf16[16,192,384]{2,1,0:T(8,128)(2,1)S(1)}, u32[]{:S(2)}, u32[]{:S(2)}) async-start(bf16[16,192,384]{2,1,0:T(8,128)(2,1)} %pack.2), calls=%async_computation | async-start | bytes 4718592 | tf_op jit(solution)/shard_map/all_to_all | solution.py:86
  13.0 0.0 copy-start.4
  13.0 0.0 copy-start.10
  13.0 13.0 %all-gather = bf16[8,6,1536]{2,1,0:T(8,128)(2,1)S(1)} all-gather(bf16[1,6,1536]{2,1,0:T(8,128)(2,1)S(1)} %maximum_bitcast_fusion.2), channel_id=1, replica_groups={{0,1,32,33,64,65,96,97},{2,3,34,35,66,67,98,99},{4,5,36,37,68,69,100,10..., dimensions={0}, use_global_device_ids=true | all-gather | bytes 165888 | tf_op jit(solution)/shard_map/all_gather | solution.py:556
  26.0 0.7 reshape.227.text_ref
  26.7 3.6 %pack.3 = bf16[16,144,384]{2,1,0:T(8,128)(2,1)} custom-call(bf16[6,64,1536]{2,1,0:T(8,128)(2,1)} %bitcast.48, bf16[48,1536]{1,0:T(8,128)(2,1)} %reshape.227.text_ref), custom_call_target="tpu_custom_call" | custom-call | bytes 3538944 | tf_op jit(solution)/shard_map/pack/pallas_call | solution.py:111
  30.4 15.1 %all-to-all-done = bf16[16,192,384]{2,1,0:T(8,128)(2,1)S(1)} async-done(((bf16[16,192,384]{2,1,0:T(8,128)(2,1)}), bf16[16,192,384]{2,1,0:T(8,128)(2,1)S(1)}, u32[]{:S(2)}, u32[]{:S(2)}) %all-to-all-start) | async-done | bytes 2359328 | tf_op jit(solution)/shard_map/all_to_all | solution.py:86
  45.5 0.0 collective-permute-start.1
  45.5 0.2 collective-permute-start
  45.7 0.2 select_reduce_fusion
  45.9 0.1 slice.38.valid_ref
  46.0 7.5 %all-to-all-start.1 = ((bf16[16,144,384]{2,1,0:T(8,128)(2,1)}), bf16[16,144,384]{2,1,0:T(8,128)(2,1)}, u32[]{:S(2)}, u32[]{:S(2)}) async-start(bf16[16,144,384]{2,1,0:T(8,128)(2,1)} %pack.3), calls=%async_computation.1 | async-start | bytes 3538944 | tf_op jit(solution)/shard_map/all_to_all | solution.py:86
  53.6 0.1 broadcast_compare_fusion
  53.7 0.1 and_and_fusion
  53.7 0.0 collective-permute-done.1.other_ref
  53.7 2.8 %merge.3 = (bf16[2,768,384]{2,1,0:T(8,128)(2,1)}, bf16[2,768,384]{2,1,0:T(8,128)(2,1)}) custom-call(s32[1]{0:T(128)} %bitcast.10.c_ref, bf16[2,2,4,192,384]{4,3,2,1,0:T(8,128)(2,1)} %bitcast.44, bf16[2,2,4,192,384]{4,3,2,1,0:T(8,128)(2,1)} %collective-permute-done.1.other_ref), custom_call_target="tpu_custom_call" | custom-call | bytes 4718592 | tf_op jit(solution)/shard_map/merge/pallas_call | solution.py:169
  56.6 4.0 %merge.4 = (bf16[2,2,768,384]{3,2,1,0:T(8,128)(2,1)}, bf16[2,2,768,384]{3,2,1,0:T(8,128)(2,1)}) custom-call(s32[1]{0:T(128)} %bitcast.10.c_ref, bf16[2,2,4,192,384]{4,3,2,1,0:T(8,128)(2,1)} %bitcast.45, bf16[2,2,4,192,384]{4,3,2,1,0:T(8,128)(2,1)} %collective-permute-done.1.other_ref), custom_call_target="tpu_custom_call" | custom-call | bytes 4718592 | tf_op jit(solution)/shard_map/merge/pallas_call | solution.py:169
  60.5 1.9 %collective-permute-start.5 = (bf16[2,2,768,384]{3,2,1,0:T(8,128)(2,1)}, bf16[2,2,768,384]{3,2,1,0:T(8,128)(2,1)}, u32[]{:S(2)}, u32[]{:S(2)}) collective-permute-start(bf16[2,2,768,384]{3,2,1,0:T(8,128)(2,1)} %get-tuple-element.24.refs_0_.refs_1_), channel_id=1, source_target_pairs={{1,32},{3,34},{5,36},{7,38},{17,48},{19,50},{21,52},{23,54},{9,40}... | collective-permute-start | bytes 7077896 | tf_op jit(solution)/shard_map/ppermute | solution.py:82
  62.5 0.1 broadcast_add_fusion
  62.6 0.1 add_select_fusion
  62.7 0.0 collective-permute-done
  62.7 0.6 compare_reduce_fusion
  63.3 3.8 %collective-permute-start.3 = (bf16[2,768,384]{2,1,0:T(8,128)(2,1)}, bf16[2,768,384]{2,1,0:T(8,128)(2,1)}, u32[]{:S(2)}, u32[]{:S(2)}) collective-permute-start(bf16[2,768,384]{2,1,0:T(8,128)(2,1)} %get-tuple-element.22), channel_id=1, source_target_pairs={{2,0},{3,1},{4,2},{5,3},{6,4},{7,5},{18,16},{19,17},{20,18},{21,19... | collective-permute-start | bytes 3538952 | tf_op jit(solution)/shard_map/ppermute | solution.py:82
  67.1 1.3 collective-permute-start.2
  68.4 0.1 select_convert_fusion
  68.5 11.8 %all-to-all-done.1 = bf16[16,144,384]{2,1,0:T(8,128)(2,1)} async-done(((bf16[16,144,384]{2,1,0:T(8,128)(2,1)}), bf16[16,144,384]{2,1,0:T(8,128)(2,1)}, u32[]{:S(2)}, u32[]{:S(2)}) %all-to-all-start.1) | async-done | bytes 1769504 | tf_op jit(solution)/shard_map/all_to_all | solution.py:86
  80.3 1.3 dynamic-slice_bitcast_fusion
  81.5 0.1 collective-permute-start.4
  81.7 0.6 slice_bitcast_fusion.bias_ref
  82.3 1.1 slice.45
  83.5 0.2 reshape.215
  83.7 0.5 copy.27
  84.2 1.0 reshape.216.q_ref.tk_ref.tv_ref
  85.3 5.2 %text_queries.1 = f32[256,512]{1,0:T(8,128)} custom-call(s32[1]{0:T(128)} %bitcast.share_ref, bf16[3,256,384]{2,1,0:T(8,128)(2,1)} %reshape.216.q_ref.tk_ref.tv_ref, bf16[3,256,384]{2,1,0:T(8,128)(2,1)} %reshape.216.q_ref.tk_ref.tv_ref, bf16[3,256,384]{2,1,0:T(8,128)(2,1)} %reshape.216.q_ref.tk_ref.tv_ref, ...), custom_call_target="tpu_custom_call" | custom-call | flops 2113929216 | bytes 2752512 | tf_op jit(solution)/shard_map/text_queries/pallas_call | solution.py:487
  90.4 2.2 %reshape.220 = f32[128,2,512]{2,1,0:T(2,128)} reshape(f32[256,512]{1,0:T(8,128)} %text_queries.1) | data formatting | bytes 1048576 | tf_op jit(solution)/shard_map/reshape | solution.py:603
  92.6 8.9 %all-to-all-start.2 = ((f32[128,2,512]{2,1,0:T(2,128)}), f32[128,2,512]{2,1,0:T(2,128)S(1)}, u32[]{:S(2)}, u32[]{:S(2)}) async-start(f32[128,2,512]{2,1,0:T(2,128)} %reshape.220), calls=%async_computation.2 | async-start | bytes 1048576 | tf_op jit(solution)/shard_map/all_to_all | solution.py:86
  101.5 0.0 collective-permute-done.4.other_ref
  101.5 2.4 %merge.5.q_ref = bf16[2,2,384,384]{3,2,1,0:T(8,128)(2,1)} custom-call(s32[1]{0:T(128)} %bitcast.10.c_ref, bf16[2,2,4,144,384]{4,3,2,1,0:T(8,128)(2,1)} %bitcast.12.mine_ref, bf16[2,4,144,384]{3,2,1,0:T(8,128)(2,1)} %collective-permute-done.4.other_ref), custom_call_target="tpu_custom_call" | custom-call | bytes 3538944 | tf_op jit(solution)/shard_map/merge/pallas_call | solution.py:169
  103.9 1.3 collective-permute-done.2.left_ref
  105.2 2.8 %join.1.refs_0_.refs_1_ = bf16[2,2,768,384]{3,2,1,0:T(8,128)(2,1)} custom-call(bf16[2,768,384]{2,1,0:T(8,128)(2,1)} %collective-permute-done.2.left_ref, bf16[2,768,384]{2,1,0:T(8,128)(2,1)} %collective-permute-done.3.right_ref), custom_call_target="tpu_custom_call" | custom-call | bytes 4718592 | tf_op jit(solution)/shard_map/join/pallas_call | solution.py:217
  108.0 0.0 collective-permute-start.6
  108.0 2.5 %collective-permute-start.7 = (bf16[2,2,768,384]{3,2,1,0:T(8,128)(2,1)}, bf16[2,2,768,384]{3,2,1,0:T(8,128)(2,1)S(1)}, u32[]{:S(2)}, u32[]{:S(2)}) collective-permute-start(bf16[2,2,768,384]{3,2,1,0:T(8,128)(2,1)} %join.1.refs_0_.refs_1_), channel_id=1, source_target_pairs={{1,32},{3,34},{5,36},{7,38},{17,48},{19,50},{21,52},{23,54},{9,40}... | collective-permute-start | bytes 7077896 | tf_op jit(solution)/shard_map/ppermute | solution.py:82
  110.5 0.0 collective-permute-done.5.refs_4_.refs_5_
  110.5 29.6 %near_cells.1 = (f32[2,768,384]{2,1,0:T(8,128)}, f32[2,768,384]{2,1,0:T(8,128)}) custom-call(bf16[2,2,384,384]{3,2,1,0:T(8,128)(2,1)S(1)} %copy-done, bf16[3,256,384]{2,1,0:T(8,128)(2,1)S(1)} %copy-done.1, bf16[3,256,384]{2,1,0:T(8,128)(2,1)S(1)} %copy-done.1, bf16[6,2,16,128]{3,2,1,0:T(8,128)(2,1)S(1)} %bitcast.40, ...), custom_call_target="tpu_custom_call" | custom-call | flops 34426847232 | bytes 7471104 | tf_op jit(solution)/shard_map/near_cells/pallas_call | solution.py:384
  140.2 0.0 collective-permute-done.6.refs_2_.refs_3_
  140.2 1.4 copy-done.8
  141.6 0.7 copy-done.9
  142.3 19.3 %side_cells.1 = bf16[2,2,384,384]{3,2,1,0:T(8,128)(2,1)S(1)} custom-call(s32[2]{0:T(128)S(1)} %slice.38.valid_ref, bf16[2,2,384,384]{3,2,1,0:T(8,128)(2,1)} %merge.5.q_ref, f32[2,768,384]{2,1,0:T(8,128)} %get-tuple-element.28.sum_ref, f32[2,768,384]{2,1,0:T(8,128)} %get-tuple-element.29.mark_ref, bf16[6,2,16,128]{3,2,1,0:T(8,128)(2,1)S(1)} %pad_maximum_fusion.1.bias_ref, ...), custom_call_target="tpu_custom_call" | custom-call | flops 16307453952 | bytes 3538944 | tf_op jit(solution)/shard_map/side_cells/pallas_call | solution.py:437
  161.6 0.0 all-to-all-done.2
  161.6 0.0 copy-start.3
  161.6 0.0 slice-start
  161.6 0.1 dynamic-slice_bitcast_fusion.1
  161.8 4.6 %collective-permute-start.8 = (bf16[384,384]{1,0:T(8,128)(2,1)S(1)}, bf16[384,384]{1,0:T(8,128)(2,1)S(1)}, u32[]{:S(2)}, u32[]{:S(2)}) collective-permute-start(bf16[384,384]{1,0:T(8,128)(2,1)S(1)} %get-tuple-element.37), channel_id=1, source_target_pairs={{0,0},{1,16},{2,4},{3,20},{4,8},{5,24},{6,12},{7,28},{16,1},{17,17... | collective-permute-start | bytes 884744 | tf_op jit(solution)/shard_map/ppermute | solution.py:82
  166.4 1.2 collective-permute-start.9
  167.7 0.1 collective-permute-start.10
  167.8 1.5 collective-permute-start.11
  169.3 2.4 %text_sum.1 = bf16[2,1536]{1,0:T(2,128)(2,1)} custom-call(f32[4,2,2,8,2,512]{5,4,3,2,1,0:T(2,128)} %bitcast.47), custom_call_target="tpu_custom_call" | custom-call | bytes 524288 | tf_op jit(solution)/shard_map/text_sum/pallas_call | solution.py:521
  171.7 5.8 %convolution_convert_fusion = bf16[2,3072]{1,0:T(2,128)(2,1)} fusion(bf16[2,1536]{1,0:T(2,128)(2,1)} %text_sum.1, bf16[1536,3072]{1,0:T(8,128)(2,1)} %param.19), kind=kOutput, calls=%fused_computation | convolution fusion | flops 18880512 | bytes 9455616 | tf_op jit(solution)/shard_map/dot_general | solution.py:620
  177.5 0.2 collective-permute-done.8.first
  177.7 1.8 collective-permute-done.9.second
  179.5 0.0 collective-permute-done.10.third
  179.6 4.6 %collective-permute-done.11.fourth = bf16[384,384]{1,0:T(8,128)(2,1)S(1)} collective-permute-done((bf16[384,384]{1,0:T(8,128)(2,1)S(1)}, bf16[384,384]{1,0:T(8,128)(2,1)S(1)}, u32[]{:S(2)}, u32[]{:S(2)}) %collective-permute-start.11) | collective-permute-done | bytes 294944 | tf_op jit(solution)/shard_map/ppermute | solution.py:82
  184.2 5.7 %project.1 = bf16[384,3072]{1,0:T(8,128)(2,1)} custom-call(s32[4]{0:T(128)S(1)} %and_select_fusion.1.from_ref, bf16[384,384]{1,0:T(8,128)(2,1)S(1)} %collective-permute-done.8.first, bf16[384,384]{1,0:T(8,128)(2,1)S(1)} %collective-permute-done.9.second, bf16[384,384]{1,0:T(8,128)(2,1)S(1)} %collective-permute-done.10.third, ...), custom_call_target="tpu_custom_call" | custom-call | flops 3623878656 | bytes 9437184 | tf_op jit(solution)/shard_map/project/pallas_call | solution.py:244
  (44 shorter events, 0.2 us)
Async XLA Ops:
  4.5 8.4 %copy-start.5 = (bf16[2,1536]{1,0:T(2,128)(2,1)S(1)}, bf16[2,1536]{1,0:T(2,128)(2,1)}, u32[]{:S(2)}) copy-start(bf16[2,1536]{1,0:T(2,128)(2,1)} %param.15) | copy-start | bytes 18436
  4.5 8.4 %copy-start.6 = (bf16[2,1536]{1,0:T(2,128)(2,1)S(1)}, bf16[2,1536]{1,0:T(2,128)(2,1)}, u32[]{:S(2)}) copy-start(bf16[2,1536]{1,0:T(2,128)(2,1)} %param.14) | copy-start | bytes 18436
  4.5 8.4 %copy-start.7 = (bf16[2,1536]{1,0:T(2,128)(2,1)S(1)}, bf16[2,1536]{1,0:T(2,128)(2,1)}, u32[]{:S(2)}) copy-start(bf16[2,1536]{1,0:T(2,128)(2,1)} %param.13) | copy-start | bytes 18436
  4.5 40.9 %all-to-all-start = ((bf16[16,192,384]{2,1,0:T(8,128)(2,1)}), bf16[16,192,384]{2,1,0:T(8,128)(2,1)S(1)}, u32[]{:S(2)}, u32[]{:S(2)}) async-start(bf16[16,192,384]{2,1,0:T(8,128)(2,1)} %pack.2), calls=%async_computation | async-start | bytes 4718592 | tf_op jit(solution)/shard_map/all_to_all | solution.py:86
  13.0 32.5 %copy-start.4 = (s32[1,16,27]{2,1,0:T(8,128)S(1)}, s32[1,16,27]{2,1,0:T(8,128)}, u32[]{:S(2)}) copy-start(s32[1,16,27]{2,1,0:T(8,128)} %param.16) | copy-start | bytes 5188
  13.0 32.8 %copy-start.10 = (s32[8]{0:T(128)S(1)}, s32[8]{0:T(128)}, u32[]{:S(2)}) copy-start(s32[8]{0:T(128)} %param.17) | copy-start | bytes 100
  45.5 8.3 %copy-start.2 = (bf16[16,192,384]{2,1,0:T(8,128)(2,1)}, bf16[16,192,384]{2,1,0:T(8,128)(2,1)S(1)}, u32[]{:S(2)}) copy-start(bf16[16,192,384]{2,1,0:T(8,128)(2,1)S(1)} %all-to-all-done) | copy-start | bytes 7077892
  45.5 8.2 %collective-permute-start.1 = (bf16[2,2,4,192,384]{4,3,2,1,0:T(8,128)(2,1)S(1)}, bf16[2,2,4,192,384]{4,3,2,1,0:T(8,128)(2,1)}, u32[]{:S(2)}, u32[]{:S(2)}) collective-permute-start(bf16[2,2,4,192,384]{4,3,2,1,0:T(8,128)(2,1)S(1)} %bitcast.43), channel_id=1, source_target_pairs={{0,1},{1,0},{2,3},{3,2},{4,5},{5,4},{6,7},{7,6},{16,17},{17,16},{1... | collective-permute-start | bytes 7077896 | tf_op jit(solution)/shard_map/ppermute | solution.py:82
  45.5 17.2 %collective-permute-start = (s32[1,16,27]{2,1,0:T(8,128)S(1)}, s32[1,16,27]{2,1,0:T(8,128)S(1)}, u32[]{:S(2)}, u32[]{:S(2)}) collective-permute-start(s32[1,16,27]{2,1,0:T(8,128)S(1)} %copy-done.4), channel_id=1, source_target_pairs={{0,16},{1,17},{2,18},{3,19},{4,20},{5,21},{6,22},{7,23},{16,0},{17... | collective-permute-start | bytes 5192 | tf_op jit(solution)/shard_map/ppermute | solution.py:82
  46.0 34.3 %all-to-all-start.1 = ((bf16[16,144,384]{2,1,0:T(8,128)(2,1)}), bf16[16,144,384]{2,1,0:T(8,128)(2,1)}, u32[]{:S(2)}, u32[]{:S(2)}) async-start(bf16[16,144,384]{2,1,0:T(8,128)(2,1)} %pack.3), calls=%async_computation.1 | async-start | bytes 3538944 | tf_op jit(solution)/shard_map/all_to_all | solution.py:86
  60.5 49.9 %collective-permute-start.5 = (bf16[2,2,768,384]{3,2,1,0:T(8,128)(2,1)}, bf16[2,2,768,384]{3,2,1,0:T(8,128)(2,1)}, u32[]{:S(2)}, u32[]{:S(2)}) collective-permute-start(bf16[2,2,768,384]{3,2,1,0:T(8,128)(2,1)} %get-tuple-element.24.refs_0_.refs_1_), channel_id=1, source_target_pairs={{1,32},{3,34},{5,36},{7,38},{17,48},{19,50},{21,52},{23,54},{9,40}... | collective-permute-start | bytes 7077896 | tf_op jit(solution)/shard_map/ppermute | solution.py:82
  63.3 41.9 %collective-permute-start.3 = (bf16[2,768,384]{2,1,0:T(8,128)(2,1)}, bf16[2,768,384]{2,1,0:T(8,128)(2,1)}, u32[]{:S(2)}, u32[]{:S(2)}) collective-permute-start(bf16[2,768,384]{2,1,0:T(8,128)(2,1)} %get-tuple-element.22), channel_id=1, source_target_pairs={{2,0},{3,1},{4,2},{5,3},{6,4},{7,5},{18,16},{19,17},{20,18},{21,19... | collective-permute-start | bytes 3538952 | tf_op jit(solution)/shard_map/ppermute | solution.py:82
  67.1 38.1 %collective-permute-start.2 = (bf16[2,768,384]{2,1,0:T(8,128)(2,1)}, bf16[2,768,384]{2,1,0:T(8,128)(2,1)}, u32[]{:S(2)}, u32[]{:S(2)}) collective-permute-start(bf16[2,768,384]{2,1,0:T(8,128)(2,1)} %get-tuple-element.25), channel_id=1, source_target_pairs={{0,2},{1,3},{2,4},{3,5},{4,6},{5,7},{16,18},{17,19},{18,20},{19,21... | collective-permute-start | bytes 3538952 | tf_op jit(solution)/shard_map/ppermute | solution.py:82
  81.5 20.0 %collective-permute-start.4 = (bf16[2,4,144,384]{3,2,1,0:T(8,128)(2,1)S(1)}, bf16[2,4,144,384]{3,2,1,0:T(8,128)(2,1)}, u32[]{:S(2)}, u32[]{:S(2)}) collective-permute-start(bf16[2,4,144,384]{3,2,1,0:T(8,128)(2,1)S(1)} %dynamic-slice_bitcast_fusion), channel_id=1, source_target_pairs={{0,1},{1,0},{2,3},{3,2},{4,5},{5,4},{6,7},{7,6},{16,17},{17,16},{1... | collective-permute-start | bytes 2654216 | tf_op jit(solution)/shard_map/ppermute | solution.py:82
  92.6 69.0 %all-to-all-start.2 = ((f32[128,2,512]{2,1,0:T(2,128)}), f32[128,2,512]{2,1,0:T(2,128)S(1)}, u32[]{:S(2)}, u32[]{:S(2)}) async-start(f32[128,2,512]{2,1,0:T(2,128)} %reshape.220), calls=%async_computation.2 | async-start | bytes 1048576 | tf_op jit(solution)/shard_map/all_to_all | solution.py:86
  103.9 6.6 %copy-start = (bf16[2,2,384,384]{3,2,1,0:T(8,128)(2,1)S(1)}, bf16[2,2,384,384]{3,2,1,0:T(8,128)(2,1)}, u32[]{:S(2)}) copy-start(bf16[2,2,384,384]{3,2,1,0:T(8,128)(2,1)} %merge.5.q_ref) | copy-start | bytes 3538948
  103.9 6.6 %copy-start.1 = (bf16[3,256,384]{2,1,0:T(8,128)(2,1)S(1)}, bf16[3,256,384]{2,1,0:T(8,128)(2,1)}, u32[]{:S(2)}) copy-start(bf16[3,256,384]{2,1,0:T(8,128)(2,1)} %reshape.216.q_ref.tk_ref.tv_ref) | copy-start | bytes 1769476
  108.0 32.1 %collective-permute-start.6 = (bf16[2,2,768,384]{3,2,1,0:T(8,128)(2,1)}, bf16[2,2,768,384]{3,2,1,0:T(8,128)(2,1)S(1)}, u32[]{:S(2)}, u32[]{:S(2)}) collective-permute-start(bf16[2,2,768,384]{3,2,1,0:T(8,128)(2,1)} %join.1.refs_0_.refs_1_), channel_id=1, source_target_pairs={{0,1},{1,0},{2,3},{3,2},{4,5},{5,4},{6,7},{7,6},{16,17},{17,16},{1... | collective-permute-start | bytes 7077896 | tf_op jit(solution)/shard_map/ppermute | solution.py:82
  108.0 32.1 %collective-permute-start.7 = (bf16[2,2,768,384]{3,2,1,0:T(8,128)(2,1)}, bf16[2,2,768,384]{3,2,1,0:T(8,128)(2,1)S(1)}, u32[]{:S(2)}, u32[]{:S(2)}) collective-permute-start(bf16[2,2,768,384]{3,2,1,0:T(8,128)(2,1)} %join.1.refs_0_.refs_1_), channel_id=1, source_target_pairs={{1,32},{3,34},{5,36},{7,38},{17,48},{19,50},{21,52},{23,54},{9,40}... | collective-permute-start | bytes 7077896 | tf_op jit(solution)/shard_map/ppermute | solution.py:82
  140.2 1.4 copy-start.8
  140.2 2.1 %copy-start.9 = (bf16[2,2,768,384]{3,2,1,0:T(8,128)(2,1)}, bf16[2,2,768,384]{3,2,1,0:T(8,128)(2,1)S(1)}, u32[]{:S(2)}) copy-start(bf16[2,2,768,384]{3,2,1,0:T(8,128)(2,1)S(1)} %collective-permute-done.7.refs_4_.refs_5_) | copy-start | bytes 7077892
  161.6 7.7 %copy-start.3 = (f32[128,2,512]{2,1,0:T(2,128)}, f32[128,2,512]{2,1,0:T(2,128)S(1)}, u32[]{:S(2)}) copy-start(f32[128,2,512]{2,1,0:T(2,128)S(1)} %all-to-all-done.2) | copy-start | bytes 1572868
  161.6 22.5 %slice-start = ((s8[9437184]{0:T(1024)(128)(4,1)}), s8[1048576]{0:T(1024)(128)(4,1)S(1)}, s32[]{:S(2)}) async-start(s8[9437184]{0:T(1024)(128)(4,1)} %bitcast.41), calls=%async_computation.3 | async-start | bytes 2097152
  161.8 15.9 %collective-permute-start.8 = (bf16[384,384]{1,0:T(8,128)(2,1)S(1)}, bf16[384,384]{1,0:T(8,128)(2,1)S(1)}, u32[]{:S(2)}, u32[]{:S(2)}) collective-permute-start(bf16[384,384]{1,0:T(8,128)(2,1)S(1)} %get-tuple-element.37), channel_id=1, source_target_pairs={{0,0},{1,16},{2,4},{3,20},{4,8},{5,24},{6,12},{7,28},{16,1},{17,17... | collective-permute-start | bytes 884744 | tf_op jit(solution)/shard_map/ppermute | solution.py:82
  166.4 13.1 %collective-permute-start.9 = (bf16[384,384]{1,0:T(8,128)(2,1)S(1)}, bf16[384,384]{1,0:T(8,128)(2,1)S(1)}, u32[]{:S(2)}, u32[]{:S(2)}) collective-permute-start(bf16[384,384]{1,0:T(8,128)(2,1)S(1)} %get-tuple-element.36), channel_id=1, source_target_pairs={{0,1},{1,17},{2,5},{3,21},{4,9},{5,25},{6,13},{7,29},{16,2},{17,18... | collective-permute-start | bytes 884744 | tf_op jit(solution)/shard_map/ppermute | solution.py:82
  167.7 11.9 %collective-permute-start.10 = (bf16[384,384]{1,0:T(8,128)(2,1)S(1)}, bf16[384,384]{1,0:T(8,128)(2,1)S(1)}, u32[]{:S(2)}, u32[]{:S(2)}) collective-permute-start(bf16[384,384]{1,0:T(8,128)(2,1)S(1)} %get-tuple-element.35), channel_id=1, source_target_pairs={{0,2},{1,18},{2,6},{3,22},{4,10},{5,26},{6,14},{7,30},{16,3},{17,1... | collective-permute-start | bytes 884744 | tf_op jit(solution)/shard_map/ppermute | solution.py:82
  167.8 16.4 %collective-permute-start.11 = (bf16[384,384]{1,0:T(8,128)(2,1)S(1)}, bf16[384,384]{1,0:T(8,128)(2,1)S(1)}, u32[]{:S(2)}, u32[]{:S(2)}) collective-permute-start(bf16[384,384]{1,0:T(8,128)(2,1)S(1)} %get-tuple-element.34), channel_id=1, source_target_pairs={{0,3},{1,19},{2,7},{3,23},{4,11},{5,27},{6,15},{7,31},{16,0},{17,1... | collective-permute-start | bytes 884744 | tf_op jit(solution)/shard_map/ppermute | solution.py:82
  171.7 12.4 %slice-start.1 = ((s8[9437184]{0:T(1024)(128)(4,1)}), s8[4194304]{0:T(1024)(128)(4,1)S(1)}, s32[]{:S(2)}) async-start(s8[9437184]{0:T(1024)(128)(4,1)} %bitcast.41), calls=%async_computation.4 | async-start | bytes 8388608
  171.7 12.4 %slice-start.2 = ((s8[9437184]{0:T(1024)(128)(4,1)}), s8[4194304]{0:T(1024)(128)(4,1)S(1)}, s32[]{:S(2)}) async-start(s8[9437184]{0:T(1024)(128)(4,1)} %bitcast.41), calls=%async_computation.5 | async-start | bytes 8388608

commit v5 on v4

--- a/solution.py
+++ b/solution.py
@@ -42,6 +42,11 @@
 ]
 
 
+EVERYONE = [
+    [device(y, z, x, c) for z in range(4) for x in range(4) for y in range(4) for c in range(2)]
+]
+
+
 def route(target):
     pairs = []
     for place in PLACES:
@@ -130,27 +135,31 @@
                     put(kind, w, slice(start, start + PIECE), get(part, x, rows))
 
 
-def merge_sides_kernel(c_ref, mine_ref, other_ref, low_ref, high_ref):
+def merge_kernel(c_ref, mine_ref, other_ref, low_ref, high_ref, own_ref, beside_ref):
     parts, columns = (mine_ref, other_ref), (low_ref, high_ref)
+    place = c_ref[0]
 
     def put(kind, w, rows, value):
         columns[w][kind, rows] = value
-
-    copy_pieces(lambda part, x, rows: parts[part][0, 0, x, rows], put)
-
-
-def merge_kernel(c_ref, mine_ref, other_ref, own_ref, near_ref):
-    parts = (mine_ref, other_ref)
-    for place, out_ref in ((c_ref[0], own_ref), (1 - c_ref[0], near_ref)):
-
-        def put(kind, w, rows, value, out_ref=out_ref):
-            out_ref[kind, w, rows] = value
-
-        copy_pieces(lambda part, x, rows, place=place: parts[part][0, place, x, rows], put)
-
-
-def merge_queries_kernel(c_ref, mine_ref, other_ref, q_ref):
+        own_ref[kind, w, rows] = value
+
+    def put_beside(kind, w, rows, value):
+        beside_ref[kind, w, rows] = value
+
+    copy_pieces(lambda part, x, rows: parts[part][0, place, x, rows], put)
+    copy_pieces(lambda part, x, rows: parts[part][0, 1 - place, x, rows], put_beside)
+
+
+def merge_queries_kernel(c_ref, mine_ref, other_ref, rows_ref, q_ref, text_ref):
     even_core = c_ref[0] == 0
+
+    @pl.when(pl.program_id(0) == 0)
+    def _():
+        for source in range(16):
+            for kind in range(3):
+                rows = rows_ref[source, 16 * kind : 16 * (kind + 1)]
+                text_ref[kind, 16 * source : 16 * (source + 1)] = rows
+
     for x in range(4):
         for f in range(TF):
             rows = slice(2 * TC * f, 2 * TC * (f + 1))
@@ -164,8 +173,8 @@
                 q_ref[w, 0, start : start + 2 * TC] = jnp.concatenate(both).astype(jnp.bfloat16)
 
 
-def merge(core, pieces, other, kernel, piece_specs, out_specs, out_shape):
-    rows = pieces.shape[3]
+def merge(core, arrays, kernel, piece_specs, out_specs, out_shape):
+    size = sum(math.prod(shape.shape) for shape in out_shape)
     return pl.pallas_call(
         kernel,
         grid_spec=pltpu.PrefetchScalarGridSpec(
@@ -173,38 +182,39 @@
         ),
         out_shape=out_shape,
         compiler_params=pltpu.CompilerParams(vmem_limit_bytes=56 * 2**20),
-        cost_estimate=pl.CostEstimate(flops=0, bytes_accessed=16 * rows * GW * 4, transcendentals=0),
+        cost_estimate=pl.CostEstimate(flops=0, bytes_accessed=4 * size, transcendentals=0),
         name="merge",
-    )(core, pieces, other)
-
-
-def merge_sides(core, pieces, other):
-    piece = pl.BlockSpec((1, 1, 4, 4 * PIECE, GW), lambda b, c: (b, c[0], 0, 0, 0))
+    )(core, *arrays)
+
+
+def merge_keys(core, pieces, other):
+    piece = pl.BlockSpec((1, 2, 4, 4 * PIECE, GW), lambda b, c: (b, 0, 0, 0, 0))
     cell = pl.BlockSpec((2, TILE, GW), lambda b, c: (0, b, 0))
     shape = jax.ShapeDtypeStruct((2, CELL, GW), jnp.bfloat16)
-    return merge(
-        core, pieces, other, merge_sides_kernel, [piece, piece], [cell, cell], [shape, shape]
-    )
-
-
-def merge_keys(core, pieces, other):
-    piece = pl.BlockSpec((1, 2, 4, 4 * PIECE, GW), lambda b, c: (b, 0, 0, 0, 0))
     both = pl.BlockSpec((2, 2, TILE, GW), lambda b, c: (0, 0, b, 0))
-    shape = jax.ShapeDtypeStruct((2, 2, CELL, GW), jnp.bfloat16)
-    return merge(core, pieces, other, merge_kernel, [piece, piece], [both, both], [shape, shape])
+    both_shape = jax.ShapeDtypeStruct((2, 2, CELL, GW), jnp.bfloat16)
+    specs, shapes = [cell, cell, both, both], [shape, shape, both_shape, both_shape]
+    return merge(core, [pieces, other], merge_kernel, [piece, piece], specs, shapes)
 
 
 def merge_queries(core, got):
-    rows = got.shape[1]
-    pieces = got.reshape(2, 2, 4, rows, GW)
-    other = send(lax.dynamic_index_in_dim(pieces, 1 - core[0], 1, keepdims=False), OTHER_CORE)
+    pieces = got.reshape(2, 2, 4, 3 * PIECE, GW)
+    leaving = pieces[:, :, :, : 2 * PIECE]
+    other = send(lax.dynamic_index_in_dim(leaving, 1 - core[0], 1, keepdims=False), OTHER_CORE)
     specs = [
-        pl.BlockSpec((1, 1, 4, rows, GW), lambda b, c: (b, c[0], 0, 0, 0)),
-        pl.BlockSpec((1, 4, rows, GW), lambda b, c: (b, 0, 0, 0)),
+        pl.BlockSpec((1, 1, 4, 2 * PIECE, GW), lambda b, c: (b, c[0], 0, 0, 0)),
+        pl.BlockSpec((1, 4, 2 * PIECE, GW), lambda b, c: (b, 0, 0, 0)),
+        pl.BlockSpec((16, PIECE, GW), lambda b, c: (0, 2, 0)),
     ]
-    spec = pl.BlockSpec((2, 1, TILE, GW), lambda b, c: (0, b, 0, 0))
-    shape = jax.ShapeDtypeStruct((2, 2, TILE, GW), jnp.bfloat16)
-    return merge(core, pieces, other, merge_queries_kernel, specs, spec, shape)
+    out_specs = [
+        pl.BlockSpec((2, 1, TILE, GW), lambda b, c: (0, b, 0, 0)),
+        pl.BlockSpec((3, TXT, GW), lambda b, c: (0, 0, 0)),
+    ]
+    shapes = [
+        jax.ShapeDtypeStruct((2, 2, TILE, GW), jnp.bfloat16),
+        jax.ShapeDtypeStruct((3, TXT, GW), jnp.bfloat16),
+    ]
+    return merge(core, [pieces, other, got], merge_queries_kernel, specs, out_specs, shapes)
 
 
 def join_kernel(left_ref, right_ref, out_ref):
@@ -505,14 +515,14 @@
 
 def text_sum_kernel(part_ref, out_ref):
     for z in range(4):
-        marks = part_ref[:, z % 2, z // 2, :, :, GW:]
-        top = jnp.max(marks, axis=(0, 1), keepdims=True)
+        marks = part_ref[z, :, :, GW:]
+        top = jnp.max(marks, axis=0, keepdims=True)
         factors = jnp.exp2((marks - top) * SCALE)
         for h in range(GH):
             factor = factors[..., h : h + 1]
-            total = jnp.sum(marks[..., 8 + h : 9 + h] * factor, axis=(0, 1))
-            part = part_ref[:, z % 2, z // 2, :, :, h * HD : (h + 1) * HD]
-            summed = jnp.sum(part * factor, axis=(0, 1)) / total
+            total = jnp.sum(marks[..., 8 + h : 9 + h] * factor, axis=0)
+            part = part_ref[z, :, :, h * HD : (h + 1) * HD]
+            summed = jnp.sum(part * factor, axis=0) / total
             start = z * GW + h * HD
             out_ref[:, start : start + HD] = summed.astype(jnp.bfloat16)
 
@@ -526,7 +536,7 @@
             flops=0, bytes_accessed=TXT * (GW + HD) * 4, transcendentals=0
         ),
         name="text_sum",
-    )(parts.reshape(4, 2, 2, 8, 2, GW + HD))
+    )(parts.reshape(4, 32, 2, GW + HD))
 
 
 def shards(
@@ -554,24 +564,20 @@
     other_lists = send(lists, TIME_PARTNER)
     text_rows = jnp.concatenate([text_query, text_key, text_value], axis=0)
     text_some = lax.all_gather(text_rows, AXES, axis_index_groups=SAME_PLACE, tiled=True)
+    text_some = text_some.reshape(8, 3, 2, 4 * GW).transpose(1, 0, 2, 3).reshape(PIECE, 4 * GW)
     packed_queries = pack(pack_queries_kernel, 3 * PIECE, [video_query], text_some)
     got, packed_queries = lax.optimization_barrier((got, packed_queries))
 
     core = c.reshape(1)
     pieces = got.reshape(2, 2, 4, 4 * PIECE, GW)
     other = send(pieces, OTHER_CORE)
-    low, high = merge_sides(core, pieces, other)
+    low, high, own, beside = merge_keys(core, pieces, other)
 
     left, right = send(high, in_columns(1)), send(low, in_columns(-1))
-    other, _ = lax.optimization_barrier((other, low))
-    own, beside = merge_keys(core, pieces, other)
     beyond = send(own, OTHER_CHIP)
 
     got_queries = exchange(packed_queries, PLANES)
-    queries = merge_queries(core, got_queries)
-
-    text_all = got_queries[:, 2 * PIECE :].reshape(2, 2, 4, 4, 2, 3, 2, GW)
-    text_all = text_all.transpose(5, 3, 1, 0, 2, 4, 6, 7).reshape(3, TXT, GW)
+    queries, text_all = merge_queries(core, got_queries)
 
     got_lists = jnp.where(zl == c, lists, other_lists).reshape(2, 8, 27)
     tile_lists = lax.dynamic_slice_in_dim(got_lists, 2 * x, 2, 1).transpose(1, 0, 2).reshape(4, 27)
@@ -600,7 +606,7 @@
     member = (4 * y + x) * 2 + c
     parts = text_part(member.reshape(1), text_all, near_bias[:2], [own])
     left, right, _, queries = lax.optimization_barrier((left, right, parts, queries))
-    parts = exchange(parts.reshape(128, 2, GW + HD), None)
+    parts = exchange(parts.reshape(128, 2, GW + HD), EVERYONE)
     sides = join(left, right)
     beside_sides, beyond_sides = send(sides, OTHER_CORE), send(sides, OTHER_CHIP)
 

time: 192 us -> 191 us (level)
  local copies, waits for them, and re-layouts: 10 us -> 7.32 us
  waiting for transfers between devices: 34.9 us -> 37.3 us
    ppermute x12, waiting for transfers between devices: 7.99 us -> 11.8 us  [send(): return lax.ppermute(value, AXES, pairs)]
    pallas_call x3 -> x2, Pallas kernels: 9.18 us -> 7.55 us  [merge(): pl.pallas_call(kernel, grid_spec=pltpu.PrefetchScalarGridSpec(num_scalar_...]
    reshape x4 -> x2, local copies, waits for them, and re-layouts: 3.92 us -> 2.84 us  [the longest x1 2.13 us: shards(): parts = exchange(parts.reshape(128, 2, GW + HD), EVERYONE)]
  transfers between devices with their start and end apart: 15 -> 15, of which waited for: 6 -> 6; matrix products, arithmetic and copies ran while one was open for 8% -> 6% of each run, Pallas kernels for 38% -> 37%
where the time goes in v5:
time: 191 us; the launch traced here: 190 us
  Pallas kernels  80.3 us (42%)
  starting transfers between devices  43.7 us (23%)
  waiting for transfers between devices  37.3 us (20%)
  blocking collectives  13 us (7%)
  local copies, waits for them, and re-layouts  7.32 us (4%)
  matrix products  5.78 us (3%)
    pallas_call x1, Pallas kernels, near(): pl.pallas_call(functools.partial(near_kernel, len(cells)), grid=(GH,), in...  29.7 us
    all_to_all x3, waiting for transfers between devices, exchange(): lax.all_to_all(value, AXES, split_axis=0, concat_axis=0, tiled=True, axis...  25.6 us
    all_to_all x3, starting transfers between devices, exchange(): lax.all_to_all(value, AXES, split_axis=0, concat_axis=0, tiled=True, axis...  25.1 us
    pallas_call x1, Pallas kernels, side(): pl.pallas_call(side_kernel, grid=(GH,), in_specs=[pl.BlockSpec(memory_spa...  19.4 us
    ppermute x12, starting transfers between devices, send(): return lax.ppermute(value, AXES, pairs)  18.6 us
    all_gather x1, blocking collectives, shards(): lax.all_gather(text_rows, AXES, axis_index_groups=SAME_PLACE, tiled=True)  13 us
    ppermute x12, waiting for transfers between devices, send(): return lax.ppermute(value, AXES, pairs)  11.8 us
    pallas_call x2, Pallas kernels, merge(): pl.pallas_call(kernel, grid_spec=pltpu.PrefetchScalarGridSpec(num_scalar_...  7.55 us
  transfers between devices with their start and end apart: 15, of which 6 were waited for; matrix products, arithmetic and copies ran while one was open for 6% of the time, Pallas kernels for 37%

profile of v5, /device:TPU:14, one launch (start us, length us, event | category | flops | bytes accessed | tf_op | source)
XLA Modules:
  0.0 189.8 jit_solution(9961533426892254168)
XLA Ops:
  0.6 3.9 %pack.2 = bf16[16,192,384]{2,1,0:T(8,128)(2,1)} custom-call(bf16[6,64,1536]{2,1,0:T(8,128)(2,1)} %bitcast.47, bf16[6,64,1536]{2,1,0:T(8,128)(2,1)} %bitcast.48), custom_call_target="tpu_custom_call" | custom-call | bytes 4718592 | tf_op jit(solution)/shard_map/pack/pallas_call | solution.py:116
  4.5 8.4 %all-to-all-start = ((bf16[16,192,384]{2,1,0:T(8,128)(2,1)}), bf16[16,192,384]{2,1,0:T(8,128)(2,1)}, u32[]{:S(2)}, u32[]{:S(2)}) async-start(bf16[16,192,384]{2,1,0:T(8,128)(2,1)} %pack.2), calls=%async_computation | async-start | bytes 4718592 | tf_op jit(solution)/shard_map/all_to_all | solution.py:91
  13.0 0.0 copy-start.5
  13.0 0.0 copy-start.11
  13.0 13.0 %all-gather = bf16[8,6,1536]{2,1,0:T(8,128)(2,1)S(1)} all-gather(bf16[1,6,1536]{2,1,0:T(8,128)(2,1)S(1)} %maximum_bitcast_fusion.2), channel_id=1, replica_groups={{0,1,32,33,64,65,96,97},{2,3,34,35,66,67,98,99},{4,5,36,37,68,69,100,10..., dimensions={0}, use_global_device_ids=true | all-gather | bytes 165888 | tf_op jit(solution)/shard_map/all_gather | solution.py:566
  26.1 0.1 copy.26
  26.2 0.7 reshape.217.text_ref
  26.9 3.6 %pack.3 = bf16[16,144,384]{2,1,0:T(8,128)(2,1)} custom-call(bf16[6,64,1536]{2,1,0:T(8,128)(2,1)} %bitcast.46, bf16[48,1536]{1,0:T(8,128)(2,1)} %reshape.217.text_ref), custom_call_target="tpu_custom_call" | custom-call | bytes 3538944 | tf_op jit(solution)/shard_map/pack/pallas_call | solution.py:116
  30.5 15.1 %all-to-all-done = bf16[16,192,384]{2,1,0:T(8,128)(2,1)} async-done(((bf16[16,192,384]{2,1,0:T(8,128)(2,1)}), bf16[16,192,384]{2,1,0:T(8,128)(2,1)}, u32[]{:S(2)}, u32[]{:S(2)}) %all-to-all-start) | async-done | bytes 2359328 | tf_op jit(solution)/shard_map/all_to_all | solution.py:91
  45.6 0.0 collective-permute-start.2
  45.6 0.1 collective-permute-start.1
  45.8 0.2 select_reduce_fusion
  45.9 0.1 slice.38.valid_ref
  46.1 7.4 %all-to-all-start.1 = ((bf16[16,144,384]{2,1,0:T(8,128)(2,1)}), bf16[16,144,384]{2,1,0:T(8,128)(2,1)S(1)}, u32[]{:S(2)}, u32[]{:S(2)}) async-start(bf16[16,144,384]{2,1,0:T(8,128)(2,1)} %pack.3), calls=%async_computation.1 | async-start | bytes 3538944 | tf_op jit(solution)/shard_map/all_to_all | solution.py:91
  53.5 0.1 broadcast_compare_fusion
  53.6 0.1 and_and_fusion
  53.6 0.0 collective-permute-done.2.other_ref
  53.6 4.8 %merge.3 = (bf16[2,768,384]{2,1,0:T(8,128)(2,1)}, bf16[2,768,384]{2,1,0:T(8,128)(2,1)}, bf16[2,2,768,384]{3,2,1,0:T(8,128)(2,1)}, bf16[2,2,768,384]{3,2,1,0:T(8,128)(2,1)}) custom-call(s32[1]{0:T(128)} %bitcast.1.c_ref, bf16[2,2,4,192,384]{4,3,2,1,0:T(8,128)(2,1)} %bitcast.14.mine_ref, bf16[2,2,4,192,384]{4,3,2,1,0:T(8,128)(2,1)} %collective-permute-done.2.other_ref), custom_call_target="tpu_custom_call" | custom-call | bytes 14155776 | tf_op jit(solution)/shard_map/merge/pallas_call | solution.py:178
  58.5 1.9 %collective-permute-start.5 = (bf16[2,2,768,384]{3,2,1,0:T(8,128)(2,1)}, bf16[2,2,768,384]{3,2,1,0:T(8,128)(2,1)}, u32[]{:S(2)}, u32[]{:S(2)}) collective-permute-start(bf16[2,2,768,384]{3,2,1,0:T(8,128)(2,1)} %get-tuple-element.24.refs_0_.refs_1_), channel_id=1, source_target_pairs={{1,32},{3,34},{5,36},{7,38},{17,48},{19,50},{21,52},{23,54},{9,40}... | collective-permute-start | bytes 7077896 | tf_op jit(solution)/shard_map/ppermute | solution.py:87
  60.4 0.1 broadcast_add_fusion
  60.5 0.1 add_select_fusion
  60.6 0.0 collective-permute-done.1
  60.6 0.6 compare_reduce_fusion
  61.3 1.3 collective-permute-start.3
  62.6 5.6 %collective-permute-start.4 = (bf16[2,768,384]{2,1,0:T(8,128)(2,1)}, bf16[2,768,384]{2,1,0:T(8,128)(2,1)}, u32[]{:S(2)}, u32[]{:S(2)}) collective-permute-start(bf16[2,768,384]{2,1,0:T(8,128)(2,1)} %get-tuple-element.26), channel_id=1, source_target_pairs={{2,0},{3,1},{4,2},{5,3},{6,4},{7,5},{18,16},{19,17},{20,18},{21,19... | collective-permute-start | bytes 3538952 | tf_op jit(solution)/shard_map/ppermute | solution.py:87
  68.1 0.1 select_convert_fusion
  68.2 10.5 %all-to-all-done.1.rows_ref = bf16[16,144,384]{2,1,0:T(8,128)(2,1)S(1)} async-done(((bf16[16,144,384]{2,1,0:T(8,128)(2,1)}), bf16[16,144,384]{2,1,0:T(8,128)(2,1)S(1)}, u32[]{:S(2)}, u32[]{:S(2)}) %all-to-all-start.1) | async-done | bytes 1769504 | tf_op jit(solution)/shard_map/all_to_all | solution.py:91
  78.7 0.1 slice.45
  78.9 0.1 dynamic-slice_bitcast_fusion
  79.0 0.1 collective-permute-start
  79.1 0.8 slice_bitcast_fusion.bias_ref
  80.0 1.1 collective-permute-done.other_ref
  81.0 0.8 copy-done.4
  81.9 2.7 %merge.2 = (bf16[2,2,384,384]{3,2,1,0:T(8,128)(2,1)}, bf16[3,256,384]{2,1,0:T(8,128)(2,1)}) custom-call(s32[1]{0:T(128)} %bitcast.1.c_ref, bf16[2,2,4,144,384]{4,3,2,1,0:T(8,128)(2,1)} %bitcast.44, bf16[2,4,96,384]{3,2,1,0:T(8,128)(2,1)} %copy-done.4, bf16[16,144,384]{2,1,0:T(8,128)(2,1)} %copy-done.2), custom_call_target="tpu_custom_call" | custom-call | bytes 3538944 | tf_op jit(solution)/shard_map/merge/pallas_call | solution.py:178
  84.6 5.1 %text_queries.1 = f32[256,512]{1,0:T(8,128)} custom-call(s32[1]{0:T(128)} %bitcast.share_ref, bf16[3,256,384]{2,1,0:T(8,128)(2,1)} %get-tuple-element.21.q_ref.tk_ref.tv_ref, bf16[3,256,384]{2,1,0:T(8,128)(2,1)} %get-tuple-element.21.q_ref.tk_ref.tv_ref, bf16[3,256,384]{2,1,0:T(8,128)(2,1)} %get-tuple-element.21.q_ref.tk_ref.tv_ref, ...), custom_call_target="tpu_custom_call" | custom-call | flops 2113929216 | bytes 2752512 | tf_op jit(solution)/shard_map/text_queries/pallas_call | solution.py:497
  89.6 2.1 %reshape.221 = f32[128,2,512]{2,1,0:T(2,128)} reshape(f32[256,512]{1,0:T(8,128)} %text_queries.1) | data formatting | bytes 1048576 | tf_op jit(solution)/shard_map/reshape | solution.py:609
  91.8 9.2 %all-to-all-start.2 = ((f32[128,2,512]{2,1,0:T(2,128)}), f32[128,2,512]{2,1,0:T(2,128)S(1)}, u32[]{:S(2)}, u32[]{:S(2)}) async-start(f32[128,2,512]{2,1,0:T(2,128)} %reshape.221), calls=%async_computation.2 | async-start | bytes 1048576 | tf_op jit(solution)/shard_map/all_to_all | solution.py:91
  101.0 3.6 %collective-permute-done.3.left_ref = bf16[2,768,384]{2,1,0:T(8,128)(2,1)} collective-permute-done((bf16[2,768,384]{2,1,0:T(8,128)(2,1)}, bf16[2,768,384]{2,1,0:T(8,128)(2,1)}, u32[]{:S(2)}, u32[]{:S(2)}) %collective-permute-start.3) | collective-permute-done | bytes 1179680 | tf_op jit(solution)/shard_map/ppermute | solution.py:87
  104.6 0.0 collective-permute-done.4.right_ref
  104.6 2.9 %join.1.refs_0_.refs_1_ = bf16[2,2,768,384]{3,2,1,0:T(8,128)(2,1)} custom-call(bf16[2,768,384]{2,1,0:T(8,128)(2,1)} %collective-permute-done.3.left_ref, bf16[2,768,384]{2,1,0:T(8,128)(2,1)} %collective-permute-done.4.right_ref), custom_call_target="tpu_custom_call" | custom-call | bytes 4718592 | tf_op jit(solution)/shard_map/join/pallas_call | solution.py:227
  107.6 0.0 collective-permute-start.6
  107.6 2.5 %collective-permute-start.7 = (bf16[2,2,768,384]{3,2,1,0:T(8,128)(2,1)}, bf16[2,2,768,384]{3,2,1,0:T(8,128)(2,1)S(1)}, u32[]{:S(2)}, u32[]{:S(2)}) collective-permute-start(bf16[2,2,768,384]{3,2,1,0:T(8,128)(2,1)} %join.1.refs_0_.refs_1_), channel_id=1, source_target_pairs={{1,32},{3,34},{5,36},{7,38},{17,48},{19,50},{21,52},{23,54},{9,40}... | collective-permute-start | bytes 7077896 | tf_op jit(solution)/shard_map/ppermute | solution.py:87
  110.0 0.0 collective-permute-done.5.refs_4_.refs_5_
  110.1 29.7 %near_cells.1 = (f32[2,768,384]{2,1,0:T(8,128)}, f32[2,768,384]{2,1,0:T(8,128)}) custom-call(bf16[2,2,384,384]{3,2,1,0:T(8,128)(2,1)S(1)} %copy-done, bf16[3,256,384]{2,1,0:T(8,128)(2,1)S(1)} %copy-done.1, bf16[3,256,384]{2,1,0:T(8,128)(2,1)S(1)} %copy-done.1, bf16[6,2,16,128]{3,2,1,0:T(8,128)(2,1)S(1)} %bitcast.40, ...), custom_call_target="tpu_custom_call" | custom-call | flops 34426847232 | bytes 7471104 | tf_op jit(solution)/shard_map/near_cells/pallas_call | solution.py:394
  139.8 0.0 collective-permute-done.6.refs_2_.refs_3_
  139.8 0.0 copy-start.9
  139.8 0.0 collective-permute-done.7.refs_4_.refs_5_
  139.8 1.4 copy-done.9
  141.2 0.8 copy-done.10
  142.0 19.4 %side_cells.1 = bf16[2,2,384,384]{3,2,1,0:T(8,128)(2,1)S(1)} custom-call(s32[2]{0:T(128)S(1)} %slice.38.valid_ref, bf16[2,2,384,384]{3,2,1,0:T(8,128)(2,1)} %get-tuple-element.28.q_ref, f32[2,768,384]{2,1,0:T(8,128)} %get-tuple-element.30.sum_ref, f32[2,768,384]{2,1,0:T(8,128)} %get-tuple-element.31.mark_ref, ...), custom_call_target="tpu_custom_call" | custom-call | flops 16307453952 | bytes 3538944 | tf_op jit(solution)/shard_map/side_cells/pallas_call | solution.py:447
  161.4 0.0 all-to-all-done.2
  161.4 0.0 copy-start.3
  161.4 0.0 slice-start
  161.4 0.1 dynamic-slice_bitcast_fusion.1
  161.6 3.2 %collective-permute-start.8 = (bf16[384,384]{1,0:T(8,128)(2,1)S(1)}, bf16[384,384]{1,0:T(8,128)(2,1)S(1)}, u32[]{:S(2)}, u32[]{:S(2)}) collective-permute-start(bf16[384,384]{1,0:T(8,128)(2,1)S(1)} %get-tuple-element.39), channel_id=1, source_target_pairs={{0,0},{1,16},{2,4},{3,20},{4,8},{5,24},{6,12},{7,28},{16,1},{17,17... | collective-permute-start | bytes 884744 | tf_op jit(solution)/shard_map/ppermute | solution.py:87
  164.7 0.9 collective-permute-start.9
  165.6 1.4 collective-permute-start.10
  167.0 1.7 collective-permute-start.11
  168.8 2.4 %text_sum.1 = bf16[2,1536]{1,0:T(2,128)(2,1)} custom-call(f32[4,32,2,512]{3,2,1,0:T(2,128)} %bitcast.45), custom_call_target="tpu_custom_call" | custom-call | bytes 524288 | tf_op jit(solution)/shard_map/text_sum/pallas_call | solution.py:531
  171.2 5.8 %convolution_convert_fusion = bf16[2,3072]{1,0:T(2,128)(2,1)} fusion(bf16[2,1536]{1,0:T(2,128)(2,1)} %text_sum.1, bf16[1536,3072]{1,0:T(8,128)(2,1)} %param.19), kind=kOutput, calls=%fused_computation | convolution fusion | flops 18880512 | bytes 9455616 | tf_op jit(solution)/shard_map/dot_general | solution.py:626
  177.0 1.2 collective-permute-done.8.first
  178.2 0.0 collective-permute-done.9.second
  178.2 5.8 %collective-permute-done.11.fourth = bf16[384,384]{1,0:T(8,128)(2,1)S(1)} collective-permute-done((bf16[384,384]{1,0:T(8,128)(2,1)S(1)}, bf16[384,384]{1,0:T(8,128)(2,1)S(1)}, u32[]{:S(2)}, u32[]{:S(2)}) %collective-permute-start.11) | collective-permute-done | bytes 294944 | tf_op jit(solution)/shard_map/ppermute | solution.py:87
  184.0 5.7 %project.1 = bf16[384,3072]{1,0:T(8,128)(2,1)} custom-call(s32[4]{0:T(128)S(1)} %and_select_fusion.1.from_ref, bf16[384,384]{1,0:T(8,128)(2,1)S(1)} %collective-permute-done.8.first, bf16[384,384]{1,0:T(8,128)(2,1)S(1)} %collective-permute-done.9.second, bf16[384,384]{1,0:T(8,128)(2,1)S(1)} %collective-permute-done.10.third, ...), custom_call_target="tpu_custom_call" | custom-call | flops 3623878656 | bytes 9437184 | tf_op jit(solution)/shard_map/project/pallas_call | solution.py:254
  (44 shorter events, 0.3 us)
Async XLA Ops:
  4.5 8.4 %copy-start.6 = (bf16[2,1536]{1,0:T(2,128)(2,1)S(1)}, bf16[2,1536]{1,0:T(2,128)(2,1)}, u32[]{:S(2)}) copy-start(bf16[2,1536]{1,0:T(2,128)(2,1)} %param.15) | copy-start | bytes 18436
  4.5 8.4 %copy-start.7 = (bf16[2,1536]{1,0:T(2,128)(2,1)S(1)}, bf16[2,1536]{1,0:T(2,128)(2,1)}, u32[]{:S(2)}) copy-start(bf16[2,1536]{1,0:T(2,128)(2,1)} %param.14) | copy-start | bytes 18436
  4.5 8.4 %copy-start.8 = (bf16[2,1536]{1,0:T(2,128)(2,1)S(1)}, bf16[2,1536]{1,0:T(2,128)(2,1)}, u32[]{:S(2)}) copy-start(bf16[2,1536]{1,0:T(2,128)(2,1)} %param.13) | copy-start | bytes 18436
  4.5 41.1 %all-to-all-start = ((bf16[16,192,384]{2,1,0:T(8,128)(2,1)}), bf16[16,192,384]{2,1,0:T(8,128)(2,1)}, u32[]{:S(2)}, u32[]{:S(2)}) async-start(bf16[16,192,384]{2,1,0:T(8,128)(2,1)} %pack.2), calls=%async_computation | async-start | bytes 4718592 | tf_op jit(solution)/shard_map/all_to_all | solution.py:91
  13.0 32.6 %copy-start.5 = (s32[1,16,27]{2,1,0:T(8,128)S(1)}, s32[1,16,27]{2,1,0:T(8,128)}, u32[]{:S(2)}) copy-start(s32[1,16,27]{2,1,0:T(8,128)} %param.16) | copy-start | bytes 5188
  13.0 32.8 %copy-start.11 = (s32[8]{0:T(128)S(1)}, s32[8]{0:T(128)}, u32[]{:S(2)}) copy-start(s32[8]{0:T(128)} %param.17) | copy-start | bytes 100
  45.6 8.1 %collective-permute-start.2 = (bf16[2,2,4,192,384]{4,3,2,1,0:T(8,128)(2,1)}, bf16[2,2,4,192,384]{4,3,2,1,0:T(8,128)(2,1)}, u32[]{:S(2)}, u32[]{:S(2)}) collective-permute-start(bf16[2,2,4,192,384]{4,3,2,1,0:T(8,128)(2,1)} %bitcast.14.mine_ref), channel_id=1, source_target_pairs={{0,1},{1,0},{2,3},{3,2},{4,5},{5,4},{6,7},{7,6},{16,17},{17,16},{1... | collective-permute-start | bytes 7077896 | tf_op jit(solution)/shard_map/ppermute | solution.py:87
  45.6 15.0 %collective-permute-start.1 = (s32[1,16,27]{2,1,0:T(8,128)S(1)}, s32[1,16,27]{2,1,0:T(8,128)S(1)}, u32[]{:S(2)}, u32[]{:S(2)}) collective-permute-start(s32[1,16,27]{2,1,0:T(8,128)S(1)} %copy-done.5), channel_id=1, source_target_pairs={{0,16},{1,17},{2,18},{3,19},{4,20},{5,21},{6,22},{7,23},{16,0},{17... | collective-permute-start | bytes 5192 | tf_op jit(solution)/shard_map/ppermute | solution.py:87
  46.1 32.7 %all-to-all-start.1 = ((bf16[16,144,384]{2,1,0:T(8,128)(2,1)}), bf16[16,144,384]{2,1,0:T(8,128)(2,1)S(1)}, u32[]{:S(2)}, u32[]{:S(2)}) async-start(bf16[16,144,384]{2,1,0:T(8,128)(2,1)} %pack.3), calls=%async_computation.1 | async-start | bytes 3538944 | tf_op jit(solution)/shard_map/all_to_all | solution.py:91
  58.5 51.6 %collective-permute-start.5 = (bf16[2,2,768,384]{3,2,1,0:T(8,128)(2,1)}, bf16[2,2,768,384]{3,2,1,0:T(8,128)(2,1)}, u32[]{:S(2)}, u32[]{:S(2)}) collective-permute-start(bf16[2,2,768,384]{3,2,1,0:T(8,128)(2,1)} %get-tuple-element.24.refs_0_.refs_1_), channel_id=1, source_target_pairs={{1,32},{3,34},{5,36},{7,38},{17,48},{19,50},{21,52},{23,54},{9,40}... | collective-permute-start | bytes 7077896 | tf_op jit(solution)/shard_map/ppermute | solution.py:87
  61.3 43.4 %collective-permute-start.3 = (bf16[2,768,384]{2,1,0:T(8,128)(2,1)}, bf16[2,768,384]{2,1,0:T(8,128)(2,1)}, u32[]{:S(2)}, u32[]{:S(2)}) collective-permute-start(bf16[2,768,384]{2,1,0:T(8,128)(2,1)} %get-tuple-element.25), channel_id=1, source_target_pairs={{0,2},{1,3},{2,4},{3,5},{4,6},{5,7},{16,18},{17,19},{18,20},{19,21... | collective-permute-start | bytes 3538952 | tf_op jit(solution)/shard_map/ppermute | solution.py:87
  62.6 42.1 %collective-permute-start.4 = (bf16[2,768,384]{2,1,0:T(8,128)(2,1)}, bf16[2,768,384]{2,1,0:T(8,128)(2,1)}, u32[]{:S(2)}, u32[]{:S(2)}) collective-permute-start(bf16[2,768,384]{2,1,0:T(8,128)(2,1)} %get-tuple-element.26), channel_id=1, source_target_pairs={{2,0},{3,1},{4,2},{5,3},{6,4},{7,5},{18,16},{19,17},{20,18},{21,19... | collective-permute-start | bytes 3538952 | tf_op jit(solution)/shard_map/ppermute | solution.py:87
  78.7 2.3 %copy-start.2 = (bf16[16,144,384]{2,1,0:T(8,128)(2,1)}, bf16[16,144,384]{2,1,0:T(8,128)(2,1)S(1)}, u32[]{:S(2)}) copy-start(bf16[16,144,384]{2,1,0:T(8,128)(2,1)S(1)} %all-to-all-done.1.rows_ref) | copy-start | bytes 5308420
  79.0 2.1 %collective-permute-start = (bf16[2,4,96,384]{3,2,1,0:T(8,128)(2,1)S(1)}, bf16[2,4,96,384]{3,2,1,0:T(8,128)(2,1)S(1)}, u32[]{:S(2)}, u32[]{:S(2)}) collective-permute-start(bf16[2,4,96,384]{3,2,1,0:T(8,128)(2,1)S(1)} %dynamic-slice_bitcast_fusion), channel_id=1, source_target_pairs={{0,1},{1,0},{2,3},{3,2},{4,5},{5,4},{6,7},{7,6},{16,17},{17,16},{1... | collective-permute-start | bytes 1769480 | tf_op jit(solution)/shard_map/ppermute | solution.py:87
  81.0 0.8 copy-start.4
  91.8 69.6 %all-to-all-start.2 = ((f32[128,2,512]{2,1,0:T(2,128)}), f32[128,2,512]{2,1,0:T(2,128)S(1)}, u32[]{:S(2)}, u32[]{:S(2)}) async-start(f32[128,2,512]{2,1,0:T(2,128)} %reshape.221), calls=%async_computation.2 | async-start | bytes 1048576 | tf_op jit(solution)/shard_map/all_to_all | solution.py:91
  104.6 5.4 %copy-start = (bf16[2,2,384,384]{3,2,1,0:T(8,128)(2,1)S(1)}, bf16[2,2,384,384]{3,2,1,0:T(8,128)(2,1)}, u32[]{:S(2)}) copy-start(bf16[2,2,384,384]{3,2,1,0:T(8,128)(2,1)} %get-tuple-element.28.q_ref) | copy-start | bytes 3538948
  104.6 5.4 %copy-start.1 = (bf16[3,256,384]{2,1,0:T(8,128)(2,1)S(1)}, bf16[3,256,384]{2,1,0:T(8,128)(2,1)}, u32[]{:S(2)}) copy-start(bf16[3,256,384]{2,1,0:T(8,128)(2,1)} %get-tuple-element.21.q_ref.tk_ref.tv_ref) | copy-start | bytes 1769476
  107.6 32.2 %collective-permute-start.6 = (bf16[2,2,768,384]{3,2,1,0:T(8,128)(2,1)}, bf16[2,2,768,384]{3,2,1,0:T(8,128)(2,1)S(1)}, u32[]{:S(2)}, u32[]{:S(2)}) collective-permute-start(bf16[2,2,768,384]{3,2,1,0:T(8,128)(2,1)} %join.1.refs_0_.refs_1_), channel_id=1, source_target_pairs={{0,1},{1,0},{2,3},{3,2},{4,5},{5,4},{6,7},{7,6},{16,17},{17,16},{1... | collective-permute-start | bytes 7077896 | tf_op jit(solution)/shard_map/ppermute | solution.py:87
  107.6 32.2 %collective-permute-start.7 = (bf16[2,2,768,384]{3,2,1,0:T(8,128)(2,1)}, bf16[2,2,768,384]{3,2,1,0:T(8,128)(2,1)S(1)}, u32[]{:S(2)}, u32[]{:S(2)}) collective-permute-start(bf16[2,2,768,384]{3,2,1,0:T(8,128)(2,1)} %join.1.refs_0_.refs_1_), channel_id=1, source_target_pairs={{1,32},{3,34},{5,36},{7,38},{17,48},{19,50},{21,52},{23,54},{9,40}... | collective-permute-start | bytes 7077896 | tf_op jit(solution)/shard_map/ppermute | solution.py:87
  139.8 1.4 copy-start.9
  139.8 2.2 %copy-start.10 = (bf16[2,2,768,384]{3,2,1,0:T(8,128)(2,1)}, bf16[2,2,768,384]{3,2,1,0:T(8,128)(2,1)S(1)}, u32[]{:S(2)}) copy-start(bf16[2,2,768,384]{3,2,1,0:T(8,128)(2,1)S(1)} %collective-permute-done.7.refs_4_.refs_5_) | copy-start | bytes 7077892
  161.4 7.4 %copy-start.3 = (f32[128,2,512]{2,1,0:T(2,128)}, f32[128,2,512]{2,1,0:T(2,128)S(1)}, u32[]{:S(2)}) copy-start(f32[128,2,512]{2,1,0:T(2,128)S(1)} %all-to-all-done.2) | copy-start | bytes 1572868
  161.4 22.6 %slice-start = ((s8[9437184]{0:T(1024)(128)(4,1)}), s8[1048576]{0:T(1024)(128)(4,1)S(1)}, s32[]{:S(2)}) async-start(s8[9437184]{0:T(1024)(128)(4,1)} %bitcast.41), calls=%async_computation.3 | async-start | bytes 2097152
  161.6 16.6 %collective-permute-start.8 = (bf16[384,384]{1,0:T(8,128)(2,1)S(1)}, bf16[384,384]{1,0:T(8,128)(2,1)S(1)}, u32[]{:S(2)}, u32[]{:S(2)}) collective-permute-start(bf16[384,384]{1,0:T(8,128)(2,1)S(1)} %get-tuple-element.39), channel_id=1, source_target_pairs={{0,0},{1,16},{2,4},{3,20},{4,8},{5,24},{6,12},{7,28},{16,1},{17,17... | collective-permute-start | bytes 884744 | tf_op jit(solution)/shard_map/ppermute | solution.py:87
  164.7 13.4 %collective-permute-start.9 = (bf16[384,384]{1,0:T(8,128)(2,1)S(1)}, bf16[384,384]{1,0:T(8,128)(2,1)S(1)}, u32[]{:S(2)}, u32[]{:S(2)}) collective-permute-start(bf16[384,384]{1,0:T(8,128)(2,1)S(1)} %get-tuple-element.38), channel_id=1, source_target_pairs={{0,1},{1,17},{2,5},{3,21},{4,9},{5,25},{6,13},{7,29},{16,2},{17,18... | collective-permute-start | bytes 884744 | tf_op jit(solution)/shard_map/ppermute | solution.py:87
  165.6 12.5 %collective-permute-start.10 = (bf16[384,384]{1,0:T(8,128)(2,1)S(1)}, bf16[384,384]{1,0:T(8,128)(2,1)S(1)}, u32[]{:S(2)}, u32[]{:S(2)}) collective-permute-start(bf16[384,384]{1,0:T(8,128)(2,1)S(1)} %get-tuple-element.37), channel_id=1, source_target_pairs={{0,2},{1,18},{2,6},{3,22},{4,10},{5,26},{6,14},{7,30},{16,3},{17,1... | collective-permute-start | bytes 884744 | tf_op jit(solution)/shard_map/ppermute | solution.py:87
  167.0 17.0 %collective-permute-start.11 = (bf16[384,384]{1,0:T(8,128)(2,1)S(1)}, bf16[384,384]{1,0:T(8,128)(2,1)S(1)}, u32[]{:S(2)}, u32[]{:S(2)}) collective-permute-start(bf16[384,384]{1,0:T(8,128)(2,1)S(1)} %get-tuple-element.36), channel_id=1, source_target_pairs={{0,3},{1,19},{2,7},{3,23},{4,11},{5,27},{6,15},{7,31},{16,0},{17,1... | collective-permute-start | bytes 884744 | tf_op jit(solution)/shard_map/ppermute | solution.py:87
  171.2 12.8 %slice-start.1 = ((s8[9437184]{0:T(1024)(128)(4,1)}), s8[4194304]{0:T(1024)(128)(4,1)S(1)}, s32[]{:S(2)}) async-start(s8[9437184]{0:T(1024)(128)(4,1)} %bitcast.41), calls=%async_computation.4 | async-start | bytes 8388608
  171.2 12.8 %slice-start.2 = ((s8[9437184]{0:T(1024)(128)(4,1)}), s8[4194304]{0:T(1024)(128)(4,1)S(1)}, s32[]{:S(2)}) async-start(s8[9437184]{0:T(1024)(128)(4,1)} %bitcast.41), calls=%async_computation.5 | async-start | bytes 8388608

commit v6 on v5

--- a/solution.py
+++ b/solution.py
@@ -334,10 +334,8 @@
     return jnp.concatenate([query, hot], axis=1)
 
 
-def mark_of(state):
-    rows = state[1].shape[0]
-    lanes = lax.broadcasted_iota(jnp.int32, (rows, HD), 1)
-    return jnp.where(lanes < HD // 2, jnp.broadcast_to(state[0], (rows, HD)), state[1][:, HD:])
+def lanes_of(rows):
+    return lax.broadcasted_iota(jnp.int32, (rows, HD), 1)
 
 
 def near_kernel(cells, q_ref, tk_ref, tv_ref, bias_ref, *refs):
@@ -357,7 +355,10 @@
         ]
         state, step = late(query, state, blocks)
         sum_ref[w] = state[1][:, :HD]
-        mark_ref[w] = mark_of(state)
+        lanes, head = lanes_of(CELL), pl.program_id(0)
+        mark = jnp.where(lanes < 8, jnp.broadcast_to(state[0], (CELL, HD)), state[1][:, HD:])
+        others = jnp.where(head == 0, 0.0, mark_ref[w])
+        mark_ref[w] = jnp.where(lanes % 8 == head, mark, others)
         return step
 
     step = jnp.maximum(run(0, add_all_late), run(1, add_all_late))
@@ -401,8 +402,8 @@
             pl.BlockSpec(bias.shape, lambda h: (0, 0, 0, 0)),
         ]
         + cell_specs(len(cells)),
-        out_specs=[state, state],
-        out_shape=[shape, shape],
+        out_specs=[state, pl.BlockSpec((2, CELL, HD), lambda h: (0, 0, 0))],
+        out_shape=[shape, jax.ShapeDtypeStruct((2, CELL, HD), jnp.float32)],
         compiler_params=pltpu.CompilerParams(vmem_limit_bytes=52 * 2**20),
         cost_estimate=cost(2 * CELL, 2 * len(cells) * CELL + TXT, GH),
         name="near_cells",
@@ -416,8 +417,11 @@
     def run(w, late):
         query = widened(q_ref[w].reshape(CELL, HD), 2 * w)
         mark = mark_ref[w]
-        totals = jnp.broadcast_to(mark[:, HD // 2 : HD // 2 + 1], (CELL, HD))
-        state = (mark[:, :1], jnp.concatenate([sum_ref[w], totals], axis=1))
+        lanes, head = lanes_of(CELL), pl.program_id(0)
+        peak = jnp.sum(jnp.where(lanes == head, mark, 0.0), axis=1, keepdims=True)
+        total = jnp.sum(jnp.where(lanes == 8 + head, mark, 0.0), axis=1, keepdims=True)
+        totals = jnp.broadcast_to(total, (CELL, HD))
+        state = (peak, jnp.concatenate([sum_ref[w], totals], axis=1))
         blocks = [
             (
                 functools.partial(refs[2 * i].__getitem__, (0, w)),
@@ -451,7 +455,7 @@
             pl.BlockSpec(memory_space=pltpu.SMEM),
             query,
             tall,
-            tall,
+            pl.BlockSpec((2, CELL, HD), lambda h: (0, 0, 0)),
             pl.BlockSpec(bias.shape, lambda h: (0, 0, 0, 0)),
         ]
         + cell_specs(3),

time: 191 us -> 187 us (0.979)
  Pallas kernels: 80.3 us -> 76.4 us
    pallas_call x1, Pallas kernels: 19.4 us -> 15.7 us  [side(): pl.pallas_call(side_kernel, grid=(GH,), in_specs=[pl.BlockSpec(memory_spa...]
  transfers between devices with their start and end apart: 15 -> 15, of which waited for: 6 -> 6; matrix products, arithmetic and copies ran while one was open for 6% -> 6% of each run, Pallas kernels for 37% -> 36%
where the time goes in v6:
time: 187 us; the launch traced here: 186 us
  Pallas kernels  76.4 us (41%)
  starting transfers between devices  43.7 us (23%)
  waiting for transfers between devices  37.3 us (20%)
  blocking collectives  13 us (7%)
  local copies, waits for them, and re-layouts  7.35 us (4%)
  matrix products  5.78 us (3%)
    pallas_call x1, Pallas kernels, near(): pl.pallas_call(functools.partial(near_kernel, len(cells)), grid=(GH,), in...  29.6 us
    all_to_all x3, waiting for transfers between devices, exchange(): lax.all_to_all(value, AXES, split_axis=0, concat_axis=0, tiled=True, axis...  25.6 us
    all_to_all x3, starting transfers between devices, exchange(): lax.all_to_all(value, AXES, split_axis=0, concat_axis=0, tiled=True, axis...  25.1 us
    ppermute x12, starting transfers between devices, send(): return lax.ppermute(value, AXES, pairs)  18.6 us
    pallas_call x1, Pallas kernels, side(): pl.pallas_call(side_kernel, grid=(GH,), in_specs=[pl.BlockSpec(memory_spa...  15.7 us
    all_gather x1, blocking collectives, shards(): lax.all_gather(text_rows, AXES, axis_index_groups=SAME_PLACE, tiled=True)  13 us
    ppermute x12, waiting for transfers between devices, send(): return lax.ppermute(value, AXES, pairs)  11.7 us
    pallas_call x2, Pallas kernels, merge(): pl.pallas_call(kernel, grid_spec=pltpu.PrefetchScalarGridSpec(num_scalar_...  7.54 us
  transfers between devices with their start and end apart: 15, of which 6 were waited for; matrix products, arithmetic and copies ran while one was open for 6% of the time, Pallas kernels for 36%

profile of v6, /device:TPU:14, one launch (start us, length us, event | category | flops | bytes accessed | tf_op | source)
XLA Modules:
  0.0 185.8 jit_solution(3061730417610634562)
XLA Ops:
  0.6 3.9 %pack.2 = bf16[16,192,384]{2,1,0:T(8,128)(2,1)} custom-call(bf16[6,64,1536]{2,1,0:T(8,128)(2,1)} %bitcast.47, bf16[6,64,1536]{2,1,0:T(8,128)(2,1)} %bitcast.48), custom_call_target="tpu_custom_call" | custom-call | bytes 4718592 | tf_op jit(solution)/shard_map/pack/pallas_call | solution.py:116
  4.5 8.4 %all-to-all-start = ((bf16[16,192,384]{2,1,0:T(8,128)(2,1)}), bf16[16,192,384]{2,1,0:T(8,128)(2,1)}, u32[]{:S(2)}, u32[]{:S(2)}) async-start(bf16[16,192,384]{2,1,0:T(8,128)(2,1)} %pack.2), calls=%async_computation | async-start | bytes 4718592 | tf_op jit(solution)/shard_map/all_to_all | solution.py:91
  13.0 0.0 copy-start.4
  13.0 0.0 copy-start.10
  13.0 13.0 %all-gather = bf16[8,6,1536]{2,1,0:T(8,128)(2,1)S(1)} all-gather(bf16[1,6,1536]{2,1,0:T(8,128)(2,1)S(1)} %maximum_bitcast_fusion.2), channel_id=1, replica_groups={{0,1,32,33,64,65,96,97},{2,3,34,35,66,67,98,99},{4,5,36,37,68,69,100,10..., dimensions={0}, use_global_device_ids=true | all-gather | bytes 165888 | tf_op jit(solution)/shard_map/all_gather | solution.py:570
  26.1 0.1 copy.26
  26.2 0.7 reshape.217.text_ref
  26.9 3.6 %pack.3 = bf16[16,144,384]{2,1,0:T(8,128)(2,1)} custom-call(bf16[6,64,1536]{2,1,0:T(8,128)(2,1)} %bitcast.46, bf16[48,1536]{1,0:T(8,128)(2,1)} %reshape.217.text_ref), custom_call_target="tpu_custom_call" | custom-call | bytes 3538944 | tf_op jit(solution)/shard_map/pack/pallas_call | solution.py:116
  30.5 15.1 %all-to-all-done = bf16[16,192,384]{2,1,0:T(8,128)(2,1)} async-done(((bf16[16,192,384]{2,1,0:T(8,128)(2,1)}), bf16[16,192,384]{2,1,0:T(8,128)(2,1)}, u32[]{:S(2)}, u32[]{:S(2)}) %all-to-all-start) | async-done | bytes 2359328 | tf_op jit(solution)/shard_map/all_to_all | solution.py:91
  45.6 0.0 collective-permute-start.2
  45.6 0.1 collective-permute-start.1
  45.8 0.2 select_reduce_fusion
  45.9 0.1 slice.38.valid_ref
  46.1 7.4 %all-to-all-start.1 = ((bf16[16,144,384]{2,1,0:T(8,128)(2,1)}), bf16[16,144,384]{2,1,0:T(8,128)(2,1)S(1)}, u32[]{:S(2)}, u32[]{:S(2)}) async-start(bf16[16,144,384]{2,1,0:T(8,128)(2,1)} %pack.3), calls=%async_computation.1 | async-start | bytes 3538944 | tf_op jit(solution)/shard_map/all_to_all | solution.py:91
  53.5 0.1 broadcast_compare_fusion
  53.6 0.1 and_and_fusion
  53.6 0.0 collective-permute-done.2.other_ref
  53.6 4.9 %merge.3 = (bf16[2,768,384]{2,1,0:T(8,128)(2,1)}, bf16[2,768,384]{2,1,0:T(8,128)(2,1)}, bf16[2,2,768,384]{3,2,1,0:T(8,128)(2,1)}, bf16[2,2,768,384]{3,2,1,0:T(8,128)(2,1)}) custom-call(s32[1]{0:T(128)} %bitcast.1.c_ref, bf16[2,2,4,192,384]{4,3,2,1,0:T(8,128)(2,1)} %bitcast.14.mine_ref, bf16[2,2,4,192,384]{4,3,2,1,0:T(8,128)(2,1)} %collective-permute-done.2.other_ref), custom_call_target="tpu_custom_call" | custom-call | bytes 14155776 | tf_op jit(solution)/shard_map/merge/pallas_call | solution.py:178
  58.5 1.9 %collective-permute-start.5 = (bf16[2,2,768,384]{3,2,1,0:T(8,128)(2,1)}, bf16[2,2,768,384]{3,2,1,0:T(8,128)(2,1)}, u32[]{:S(2)}, u32[]{:S(2)}) collective-permute-start(bf16[2,2,768,384]{3,2,1,0:T(8,128)(2,1)} %get-tuple-element.24.refs_0_.refs_1_), channel_id=1, source_target_pairs={{1,32},{3,34},{5,36},{7,38},{17,48},{19,50},{21,52},{23,54},{9,40}... | collective-permute-start | bytes 7077896 | tf_op jit(solution)/shard_map/ppermute | solution.py:87
  60.4 0.1 broadcast_add_fusion
  60.5 0.1 add_select_fusion
  60.6 0.0 collective-permute-done.1
  60.7 0.6 compare_reduce_fusion
  61.3 1.3 collective-permute-start.3
  62.6 5.6 %collective-permute-start.4 = (bf16[2,768,384]{2,1,0:T(8,128)(2,1)}, bf16[2,768,384]{2,1,0:T(8,128)(2,1)}, u32[]{:S(2)}, u32[]{:S(2)}) collective-permute-start(bf16[2,768,384]{2,1,0:T(8,128)(2,1)} %get-tuple-element.26), channel_id=1, source_target_pairs={{2,0},{3,1},{4,2},{5,3},{6,4},{7,5},{18,16},{19,17},{20,18},{21,19... | collective-permute-start | bytes 3538952 | tf_op jit(solution)/shard_map/ppermute | solution.py:87
  68.2 0.1 select_convert_fusion
  68.3 10.5 %all-to-all-done.1.rows_ref = bf16[16,144,384]{2,1,0:T(8,128)(2,1)S(1)} async-done(((bf16[16,144,384]{2,1,0:T(8,128)(2,1)}), bf16[16,144,384]{2,1,0:T(8,128)(2,1)S(1)}, u32[]{:S(2)}, u32[]{:S(2)}) %all-to-all-start.1) | async-done | bytes 1769504 | tf_op jit(solution)/shard_map/all_to_all | solution.py:91
  78.7 0.1 slice.45
  78.9 0.1 dynamic-slice_bitcast_fusion
  79.0 0.1 collective-permute-start
  79.1 0.8 slice_bitcast_fusion.bias_ref
  80.0 1.1 collective-permute-done.other_ref
  81.0 0.8 copy-done.3
  81.9 2.7 %merge.2 = (bf16[2,2,384,384]{3,2,1,0:T(8,128)(2,1)}, bf16[3,256,384]{2,1,0:T(8,128)(2,1)}) custom-call(s32[1]{0:T(128)} %bitcast.1.c_ref, bf16[2,2,4,144,384]{4,3,2,1,0:T(8,128)(2,1)} %bitcast.44, bf16[2,4,96,384]{3,2,1,0:T(8,128)(2,1)} %copy-done.3, bf16[16,144,384]{2,1,0:T(8,128)(2,1)} %copy-done.1), custom_call_target="tpu_custom_call" | custom-call | bytes 3538944 | tf_op jit(solution)/shard_map/merge/pallas_call | solution.py:178
  84.6 5.1 %text_queries.1 = f32[256,512]{1,0:T(8,128)} custom-call(s32[1]{0:T(128)} %bitcast.share_ref, bf16[3,256,384]{2,1,0:T(8,128)(2,1)} %get-tuple-element.21.q_ref.tk_ref.tv_ref, bf16[3,256,384]{2,1,0:T(8,128)(2,1)} %get-tuple-element.21.q_ref.tk_ref.tv_ref, bf16[3,256,384]{2,1,0:T(8,128)(2,1)} %get-tuple-element.21.q_ref.tk_ref.tv_ref, ...), custom_call_target="tpu_custom_call" | custom-call | flops 2113929216 | bytes 2752512 | tf_op jit(solution)/shard_map/text_queries/pallas_call | solution.py:501
  89.7 2.1 %reshape.221 = f32[128,2,512]{2,1,0:T(2,128)} reshape(f32[256,512]{1,0:T(8,128)} %text_queries.1) | data formatting | bytes 1048576 | tf_op jit(solution)/shard_map/reshape | solution.py:613
  91.8 9.2 %all-to-all-start.2 = ((f32[128,2,512]{2,1,0:T(2,128)}), f32[128,2,512]{2,1,0:T(2,128)S(1)}, u32[]{:S(2)}, u32[]{:S(2)}) async-start(f32[128,2,512]{2,1,0:T(2,128)} %reshape.221), calls=%async_computation.2 | async-start | bytes 1048576 | tf_op jit(solution)/shard_map/all_to_all | solution.py:91
  101.0 3.6 %collective-permute-done.3.left_ref = bf16[2,768,384]{2,1,0:T(8,128)(2,1)} collective-permute-done((bf16[2,768,384]{2,1,0:T(8,128)(2,1)}, bf16[2,768,384]{2,1,0:T(8,128)(2,1)}, u32[]{:S(2)}, u32[]{:S(2)}) %collective-permute-start.3) | collective-permute-done | bytes 1179680 | tf_op jit(solution)/shard_map/ppermute | solution.py:87
  104.6 0.0 collective-permute-done.4.right_ref
  104.6 2.9 %join.1.refs_0_.refs_1_ = bf16[2,2,768,384]{3,2,1,0:T(8,128)(2,1)} custom-call(bf16[2,768,384]{2,1,0:T(8,128)(2,1)} %collective-permute-done.3.left_ref, bf16[2,768,384]{2,1,0:T(8,128)(2,1)} %collective-permute-done.4.right_ref), custom_call_target="tpu_custom_call" | custom-call | bytes 4718592 | tf_op jit(solution)/shard_map/join/pallas_call | solution.py:227
  107.5 0.0 collective-permute-start.6
  107.5 2.5 %collective-permute-start.7 = (bf16[2,2,768,384]{3,2,1,0:T(8,128)(2,1)}, bf16[2,2,768,384]{3,2,1,0:T(8,128)(2,1)S(1)}, u32[]{:S(2)}, u32[]{:S(2)}) collective-permute-start(bf16[2,2,768,384]{3,2,1,0:T(8,128)(2,1)} %join.1.refs_0_.refs_1_), channel_id=1, source_target_pairs={{1,32},{3,34},{5,36},{7,38},{17,48},{19,50},{21,52},{23,54},{9,40}... | collective-permute-start | bytes 7077896 | tf_op jit(solution)/shard_map/ppermute | solution.py:87
  110.0 0.0 collective-permute-done.5.refs_4_.refs_5_
  110.0 29.6 %near_cells.1 = (f32[2,768,384]{2,1,0:T(8,128)}, f32[2,768,128]{2,1,0:T(8,128)S(1)}) custom-call(bf16[2,2,384,384]{3,2,1,0:T(8,128)(2,1)} %get-tuple-element.28.q_ref, bf16[3,256,384]{2,1,0:T(8,128)(2,1)S(1)} %copy-done, bf16[3,256,384]{2,1,0:T(8,128)(2,1)S(1)} %copy-done, bf16[6,2,16,128]{3,2,1,0:T(8,128)(2,1)S(1)} %bitcast.40, ...), custom_call_target="tpu_custom_call" | custom-call | flops 34426847232 | bytes 7471104 | tf_op jit(solution)/shard_map/near_cells/pallas_call | solution.py:395
  139.6 0.0 collective-permute-done.6.refs_2_.refs_3_
  139.6 0.0 copy-start.8
  139.6 0.0 collective-permute-done.7.refs_4_.refs_5_
  139.6 1.4 copy-done.8
  141.0 0.8 copy-done.9
  141.8 15.7 %side_cells.1 = bf16[2,2,384,384]{3,2,1,0:T(8,128)(2,1)S(1)} custom-call(s32[2]{0:T(128)S(1)} %slice.38.valid_ref, bf16[2,2,384,384]{3,2,1,0:T(8,128)(2,1)} %get-tuple-element.28.q_ref, f32[2,768,384]{2,1,0:T(8,128)} %get-tuple-element.30.sum_ref, f32[2,768,128]{2,1,0:T(8,128)S(1)} %get-tuple-element.31.mark_ref, ...), custom_call_target="tpu_custom_call" | custom-call | flops 16307453952 | bytes 3538944 | tf_op jit(solution)/shard_map/side_cells/pallas_call | solution.py:451
  157.5 0.0 copy-start.2
  157.5 0.0 slice-start
  157.5 0.1 dynamic-slice_bitcast_fusion.1
  157.6 3.1 %collective-permute-start.8 = (bf16[384,384]{1,0:T(8,128)(2,1)S(1)}, bf16[384,384]{1,0:T(8,128)(2,1)S(1)}, u32[]{:S(2)}, u32[]{:S(2)}) collective-permute-start(bf16[384,384]{1,0:T(8,128)(2,1)S(1)} %get-tuple-element.39), channel_id=1, source_target_pairs={{0,0},{1,16},{2,4},{3,20},{4,8},{5,24},{6,12},{7,28},{16,1},{17,17... | collective-permute-start | bytes 884744 | tf_op jit(solution)/shard_map/ppermute | solution.py:87
  160.8 0.9 collective-permute-start.9
  161.7 1.4 collective-permute-start.10
  163.1 1.7 collective-permute-start.11
  164.8 2.4 %text_sum.1 = bf16[2,1536]{1,0:T(2,128)(2,1)} custom-call(f32[4,32,2,512]{3,2,1,0:T(2,128)} %bitcast.45), custom_call_target="tpu_custom_call" | custom-call | bytes 524288 | tf_op jit(solution)/shard_map/text_sum/pallas_call | solution.py:535
  167.2 5.8 %convolution_convert_fusion = bf16[2,3072]{1,0:T(2,128)(2,1)} fusion(bf16[2,1536]{1,0:T(2,128)(2,1)} %text_sum.1, bf16[1536,3072]{1,0:T(8,128)(2,1)} %param.19), kind=kOutput, calls=%fused_computation | convolution fusion | flops 18880512 | bytes 9455616 | tf_op jit(solution)/shard_map/dot_general | solution.py:630
  173.0 1.2 collective-permute-done.8.first
  174.2 0.0 collective-permute-done.9.second
  174.2 0.0 collective-permute-done.10.third
  174.2 5.9 %collective-permute-done.11.fourth = bf16[384,384]{1,0:T(8,128)(2,1)S(1)} collective-permute-done((bf16[384,384]{1,0:T(8,128)(2,1)S(1)}, bf16[384,384]{1,0:T(8,128)(2,1)S(1)}, u32[]{:S(2)}, u32[]{:S(2)}) %collective-permute-start.11) | collective-permute-done | bytes 294944 | tf_op jit(solution)/shard_map/ppermute | solution.py:87
  180.1 5.7 %project.1 = bf16[384,3072]{1,0:T(8,128)(2,1)} custom-call(s32[4]{0:T(128)S(1)} %and_select_fusion.1.from_ref, bf16[384,384]{1,0:T(8,128)(2,1)S(1)} %collective-permute-done.8.first, bf16[384,384]{1,0:T(8,128)(2,1)S(1)} %collective-permute-done.9.second, bf16[384,384]{1,0:T(8,128)(2,1)S(1)} %collective-permute-done.10.third, ...), custom_call_target="tpu_custom_call" | custom-call | flops 3623878656 | bytes 9437184 | tf_op jit(solution)/shard_map/project/pallas_call | solution.py:254
  (42 shorter events, 0.3 us)
Async XLA Ops:
  4.5 8.4 %copy-start.5 = (bf16[2,1536]{1,0:T(2,128)(2,1)S(1)}, bf16[2,1536]{1,0:T(2,128)(2,1)}, u32[]{:S(2)}) copy-start(bf16[2,1536]{1,0:T(2,128)(2,1)} %param.15) | copy-start | bytes 18436
  4.5 8.4 %copy-start.6 = (bf16[2,1536]{1,0:T(2,128)(2,1)S(1)}, bf16[2,1536]{1,0:T(2,128)(2,1)}, u32[]{:S(2)}) copy-start(bf16[2,1536]{1,0:T(2,128)(2,1)} %param.14) | copy-start | bytes 18436
  4.5 8.4 %copy-start.7 = (bf16[2,1536]{1,0:T(2,128)(2,1)S(1)}, bf16[2,1536]{1,0:T(2,128)(2,1)}, u32[]{:S(2)}) copy-start(bf16[2,1536]{1,0:T(2,128)(2,1)} %param.13) | copy-start | bytes 18436
  4.5 41.1 %all-to-all-start = ((bf16[16,192,384]{2,1,0:T(8,128)(2,1)}), bf16[16,192,384]{2,1,0:T(8,128)(2,1)}, u32[]{:S(2)}, u32[]{:S(2)}) async-start(bf16[16,192,384]{2,1,0:T(8,128)(2,1)} %pack.2), calls=%async_computation | async-start | bytes 4718592 | tf_op jit(solution)/shard_map/all_to_all | solution.py:91
  13.0 32.6 %copy-start.4 = (s32[1,16,27]{2,1,0:T(8,128)S(1)}, s32[1,16,27]{2,1,0:T(8,128)}, u32[]{:S(2)}) copy-start(s32[1,16,27]{2,1,0:T(8,128)} %param.16) | copy-start | bytes 5188
  13.0 32.8 %copy-start.10 = (s32[8]{0:T(128)S(1)}, s32[8]{0:T(128)}, u32[]{:S(2)}) copy-start(s32[8]{0:T(128)} %param.17) | copy-start | bytes 100
  45.6 8.1 %collective-permute-start.2 = (bf16[2,2,4,192,384]{4,3,2,1,0:T(8,128)(2,1)}, bf16[2,2,4,192,384]{4,3,2,1,0:T(8,128)(2,1)}, u32[]{:S(2)}, u32[]{:S(2)}) collective-permute-start(bf16[2,2,4,192,384]{4,3,2,1,0:T(8,128)(2,1)} %bitcast.14.mine_ref), channel_id=1, source_target_pairs={{0,1},{1,0},{2,3},{3,2},{4,5},{5,4},{6,7},{7,6},{16,17},{17,16},{1... | collective-permute-start | bytes 7077896 | tf_op jit(solution)/shard_map/ppermute | solution.py:87
  45.6 15.0 %collective-permute-start.1 = (s32[1,16,27]{2,1,0:T(8,128)S(1)}, s32[1,16,27]{2,1,0:T(8,128)S(1)}, u32[]{:S(2)}, u32[]{:S(2)}) collective-permute-start(s32[1,16,27]{2,1,0:T(8,128)S(1)} %copy-done.4), channel_id=1, source_target_pairs={{0,16},{1,17},{2,18},{3,19},{4,20},{5,21},{6,22},{7,23},{16,0},{17... | collective-permute-start | bytes 5192 | tf_op jit(solution)/shard_map/ppermute | solution.py:87
  46.1 32.7 %all-to-all-start.1 = ((bf16[16,144,384]{2,1,0:T(8,128)(2,1)}), bf16[16,144,384]{2,1,0:T(8,128)(2,1)S(1)}, u32[]{:S(2)}, u32[]{:S(2)}) async-start(bf16[16,144,384]{2,1,0:T(8,128)(2,1)} %pack.3), calls=%async_computation.1 | async-start | bytes 3538944 | tf_op jit(solution)/shard_map/all_to_all | solution.py:91
  58.5 51.5 %collective-permute-start.5 = (bf16[2,2,768,384]{3,2,1,0:T(8,128)(2,1)}, bf16[2,2,768,384]{3,2,1,0:T(8,128)(2,1)}, u32[]{:S(2)}, u32[]{:S(2)}) collective-permute-start(bf16[2,2,768,384]{3,2,1,0:T(8,128)(2,1)} %get-tuple-element.24.refs_0_.refs_1_), channel_id=1, source_target_pairs={{1,32},{3,34},{5,36},{7,38},{17,48},{19,50},{21,52},{23,54},{9,40}... | collective-permute-start | bytes 7077896 | tf_op jit(solution)/shard_map/ppermute | solution.py:87
  61.3 43.4 %collective-permute-start.3 = (bf16[2,768,384]{2,1,0:T(8,128)(2,1)}, bf16[2,768,384]{2,1,0:T(8,128)(2,1)}, u32[]{:S(2)}, u32[]{:S(2)}) collective-permute-start(bf16[2,768,384]{2,1,0:T(8,128)(2,1)} %get-tuple-element.25), channel_id=1, source_target_pairs={{0,2},{1,3},{2,4},{3,5},{4,6},{5,7},{16,18},{17,19},{18,20},{19,21... | collective-permute-start | bytes 3538952 | tf_op jit(solution)/shard_map/ppermute | solution.py:87
  62.6 42.1 %collective-permute-start.4 = (bf16[2,768,384]{2,1,0:T(8,128)(2,1)}, bf16[2,768,384]{2,1,0:T(8,128)(2,1)}, u32[]{:S(2)}, u32[]{:S(2)}) collective-permute-start(bf16[2,768,384]{2,1,0:T(8,128)(2,1)} %get-tuple-element.26), channel_id=1, source_target_pairs={{2,0},{3,1},{4,2},{5,3},{6,4},{7,5},{18,16},{19,17},{20,18},{21,19... | collective-permute-start | bytes 3538952 | tf_op jit(solution)/shard_map/ppermute | solution.py:87
  78.7 2.3 %copy-start.1 = (bf16[16,144,384]{2,1,0:T(8,128)(2,1)}, bf16[16,144,384]{2,1,0:T(8,128)(2,1)S(1)}, u32[]{:S(2)}) copy-start(bf16[16,144,384]{2,1,0:T(8,128)(2,1)S(1)} %all-to-all-done.1.rows_ref) | copy-start | bytes 5308420
  79.0 2.1 %collective-permute-start = (bf16[2,4,96,384]{3,2,1,0:T(8,128)(2,1)S(1)}, bf16[2,4,96,384]{3,2,1,0:T(8,128)(2,1)S(1)}, u32[]{:S(2)}, u32[]{:S(2)}) collective-permute-start(bf16[2,4,96,384]{3,2,1,0:T(8,128)(2,1)S(1)} %dynamic-slice_bitcast_fusion), channel_id=1, source_target_pairs={{0,1},{1,0},{2,3},{3,2},{4,5},{5,4},{6,7},{7,6},{16,17},{17,16},{1... | collective-permute-start | bytes 1769480 | tf_op jit(solution)/shard_map/ppermute | solution.py:87
  81.0 0.8 copy-start.3
  91.8 65.6 %all-to-all-start.2 = ((f32[128,2,512]{2,1,0:T(2,128)}), f32[128,2,512]{2,1,0:T(2,128)S(1)}, u32[]{:S(2)}, u32[]{:S(2)}) async-start(f32[128,2,512]{2,1,0:T(2,128)} %reshape.221), calls=%async_computation.2 | async-start | bytes 1048576 | tf_op jit(solution)/shard_map/all_to_all | solution.py:91
  104.6 5.3 %copy-start = (bf16[3,256,384]{2,1,0:T(8,128)(2,1)S(1)}, bf16[3,256,384]{2,1,0:T(8,128)(2,1)}, u32[]{:S(2)}) copy-start(bf16[3,256,384]{2,1,0:T(8,128)(2,1)} %get-tuple-element.21.q_ref.tk_ref.tv_ref) | copy-start | bytes 1769476
  107.5 32.1 %collective-permute-start.6 = (bf16[2,2,768,384]{3,2,1,0:T(8,128)(2,1)}, bf16[2,2,768,384]{3,2,1,0:T(8,128)(2,1)S(1)}, u32[]{:S(2)}, u32[]{:S(2)}) collective-permute-start(bf16[2,2,768,384]{3,2,1,0:T(8,128)(2,1)} %join.1.refs_0_.refs_1_), channel_id=1, source_target_pairs={{0,1},{1,0},{2,3},{3,2},{4,5},{5,4},{6,7},{7,6},{16,17},{17,16},{1... | collective-permute-start | bytes 7077896 | tf_op jit(solution)/shard_map/ppermute | solution.py:87
  107.5 32.1 %collective-permute-start.7 = (bf16[2,2,768,384]{3,2,1,0:T(8,128)(2,1)}, bf16[2,2,768,384]{3,2,1,0:T(8,128)(2,1)S(1)}, u32[]{:S(2)}, u32[]{:S(2)}) collective-permute-start(bf16[2,2,768,384]{3,2,1,0:T(8,128)(2,1)} %join.1.refs_0_.refs_1_), channel_id=1, source_target_pairs={{1,32},{3,34},{5,36},{7,38},{17,48},{19,50},{21,52},{23,54},{9,40}... | collective-permute-start | bytes 7077896 | tf_op jit(solution)/shard_map/ppermute | solution.py:87
  139.6 1.4 copy-start.8
  139.6 2.2 %copy-start.9 = (bf16[2,2,768,384]{3,2,1,0:T(8,128)(2,1)}, bf16[2,2,768,384]{3,2,1,0:T(8,128)(2,1)S(1)}, u32[]{:S(2)}) copy-start(bf16[2,2,768,384]{3,2,1,0:T(8,128)(2,1)S(1)} %collective-permute-done.7.refs_4_.refs_5_) | copy-start | bytes 7077892
  157.5 7.3 %copy-start.2 = (f32[128,2,512]{2,1,0:T(2,128)}, f32[128,2,512]{2,1,0:T(2,128)S(1)}, u32[]{:S(2)}) copy-start(f32[128,2,512]{2,1,0:T(2,128)S(1)} %all-to-all-done.2) | copy-start | bytes 1572868
  157.5 22.6 %slice-start = ((s8[9437184]{0:T(1024)(128)(4,1)}), s8[1048576]{0:T(1024)(128)(4,1)S(1)}, s32[]{:S(2)}) async-start(s8[9437184]{0:T(1024)(128)(4,1)} %bitcast.41), calls=%async_computation.3 | async-start | bytes 2097152
  157.6 16.5 %collective-permute-start.8 = (bf16[384,384]{1,0:T(8,128)(2,1)S(1)}, bf16[384,384]{1,0:T(8,128)(2,1)S(1)}, u32[]{:S(2)}, u32[]{:S(2)}) collective-permute-start(bf16[384,384]{1,0:T(8,128)(2,1)S(1)} %get-tuple-element.39), channel_id=1, source_target_pairs={{0,0},{1,16},{2,4},{3,20},{4,8},{5,24},{6,12},{7,28},{16,1},{17,17... | collective-permute-start | bytes 884744 | tf_op jit(solution)/shard_map/ppermute | solution.py:87
  160.8 13.4 %collective-permute-start.9 = (bf16[384,384]{1,0:T(8,128)(2,1)S(1)}, bf16[384,384]{1,0:T(8,128)(2,1)S(1)}, u32[]{:S(2)}, u32[]{:S(2)}) collective-permute-start(bf16[384,384]{1,0:T(8,128)(2,1)S(1)} %get-tuple-element.38), channel_id=1, source_target_pairs={{0,1},{1,17},{2,5},{3,21},{4,9},{5,25},{6,13},{7,29},{16,2},{17,18... | collective-permute-start | bytes 884744 | tf_op jit(solution)/shard_map/ppermute | solution.py:87
  161.7 12.5 %collective-permute-start.10 = (bf16[384,384]{1,0:T(8,128)(2,1)S(1)}, bf16[384,384]{1,0:T(8,128)(2,1)S(1)}, u32[]{:S(2)}, u32[]{:S(2)}) collective-permute-start(bf16[384,384]{1,0:T(8,128)(2,1)S(1)} %get-tuple-element.37), channel_id=1, source_target_pairs={{0,2},{1,18},{2,6},{3,22},{4,10},{5,26},{6,14},{7,30},{16,3},{17,1... | collective-permute-start | bytes 884744 | tf_op jit(solution)/shard_map/ppermute | solution.py:87
  163.1 17.0 %collective-permute-start.11 = (bf16[384,384]{1,0:T(8,128)(2,1)S(1)}, bf16[384,384]{1,0:T(8,128)(2,1)S(1)}, u32[]{:S(2)}, u32[]{:S(2)}) collective-permute-start(bf16[384,384]{1,0:T(8,128)(2,1)S(1)} %get-tuple-element.36), channel_id=1, source_target_pairs={{0,3},{1,19},{2,7},{3,23},{4,11},{5,27},{6,15},{7,31},{16,0},{17,1... | collective-permute-start | bytes 884744 | tf_op jit(solution)/shard_map/ppermute | solution.py:87
  167.2 12.8 %slice-start.1 = ((s8[9437184]{0:T(1024)(128)(4,1)}), s8[4194304]{0:T(1024)(128)(4,1)S(1)}, s32[]{:S(2)}) async-start(s8[9437184]{0:T(1024)(128)(4,1)} %bitcast.41), calls=%async_computation.4 | async-start | bytes 8388608
  167.2 12.8 %slice-start.2 = ((s8[9437184]{0:T(1024)(128)(4,1)}), s8[4194304]{0:T(1024)(128)(4,1)S(1)}, s32[]{:S(2)}) async-start(s8[9437184]{0:T(1024)(128)(4,1)} %bitcast.41), calls=%async_computation.5 | async-start | bytes 8388608

commit v7 on v6

--- a/solution.py
+++ b/solution.py
@@ -94,7 +94,7 @@
 
 
 def pack_kernel(k_ref, v_ref, out_ref):
-    for p in range(4):
+    for p in range(2):
         columns = slice(2 * TC * p, 2 * TC * (p + 1))
         for kind, ref in enumerate((k_ref, v_ref)):
             cut = ref[:, columns, :].astype(jnp.float32).reshape(TF, 2, TC, GW)
@@ -104,20 +104,20 @@
 
 
 def pack_queries_kernel(q_ref, text_ref, out_ref):
-    for p in range(4):
+    for p in range(2):
         rows = q_ref[:, 2 * TC * p : 2 * TC * (p + 1), :].reshape(2 * PIECE, GW)
         out_ref[p, : 2 * PIECE] = rows
         out_ref[p, 2 * PIECE :] = text_ref[...]
 
 
 def pack(kernel, rows, rasters, *text):
-    raster = pl.BlockSpec((TF, 8 * TC, GW), lambda g: (0, 0, g))
-    text_spec = pl.BlockSpec((PIECE, GW), lambda g: (0, g))
+    raster = pl.BlockSpec((TF, 4 * TC, GW), lambda g, half: (0, half, g))
+    text_spec = pl.BlockSpec((PIECE, GW), lambda g, half: (0, g))
     return pl.pallas_call(
         kernel,
-        grid=(4,),
+        grid=(4, 2),
         in_specs=[raster] * len(rasters) + [text_spec] * len(text),
-        out_specs=pl.BlockSpec((4, rows, GW), lambda g: (g, 0, 0)),
+        out_specs=pl.BlockSpec((2, rows, GW), lambda g, half: (2 * g + half, 0, 0)),
         out_shape=jax.ShapeDtypeStruct((16, rows, GW), jnp.bfloat16),
         compiler_params=pltpu.CompilerParams(vmem_limit_bytes=56 * 2**20),
         cost_estimate=pl.CostEstimate(flops=0, bytes_accessed=16 * rows * GW * 4, transcendentals=0),

time: 187 us -> 189 us (1.011)
  Pallas kernels: 76.4 us -> 80.3 us
  waiting for transfers between devices: 37.3 us -> 35.4 us
    pallas_call x2, Pallas kernels: 7.47 us -> 11.4 us  [pack(): pl.pallas_call(kernel, grid=(4, 2), in_specs=[raster] * len(rasters) + [t...]
  transfers between devices with their start and end apart: 15 -> 15, of which waited for: 6 -> 6; matrix products, arithmetic and copies ran while one was open for 6% -> 6% of each run, Pallas kernels for 36% -> 37%
where the time goes in v7:
time: 189 us; the launch traced here: 188 us
  Pallas kernels  80.3 us (42%)
  starting transfers between devices  43.7 us (23%)
  waiting for transfers between devices  35.4 us (19%)
  blocking collectives  13 us (7%)
  local copies, waits for them, and re-layouts  7.35 us (4%)
  matrix products  5.78 us (3%)
    pallas_call x1, Pallas kernels, near(): pl.pallas_call(functools.partial(near_kernel, len(cells)), grid=(GH,), in...  29.6 us
    all_to_all x3, starting transfers between devices, exchange(): lax.all_to_all(value, AXES, split_axis=0, concat_axis=0, tiled=True, axis...  25.1 us
    all_to_all x3, waiting for transfers between devices, exchange(): lax.all_to_all(value, AXES, split_axis=0, concat_axis=0, tiled=True, axis...  23.7 us
    ppermute x12, starting transfers between devices, send(): return lax.ppermute(value, AXES, pairs)  18.6 us
    pallas_call x1, Pallas kernels, side(): pl.pallas_call(side_kernel, grid=(GH,), in_specs=[pl.BlockSpec(memory_spa...  15.7 us
    all_gather x1, blocking collectives, shards(): lax.all_gather(text_rows, AXES, axis_index_groups=SAME_PLACE, tiled=True)  13 us
    ppermute x12, waiting for transfers between devices, send(): return lax.ppermute(value, AXES, pairs)  11.7 us
    pallas_call x2, Pallas kernels, pack(): pl.pallas_call(kernel, grid=(4, 2), in_specs=[raster] * len(rasters) + [t...  11.4 us
  transfers between devices with their start and end apart: 15, of which 6 were waited for; matrix products, arithmetic and copies ran while one was open for 6% of the time, Pallas kernels for 37%

profile of v7, /device:TPU:14, one launch (start us, length us, event | category | flops | bytes accessed | tf_op | source)
XLA Modules:
  0.0 187.9 jit_solution(12283194468370316140)
XLA Ops:
  0.6 6.0 %pack.2 = bf16[16,192,384]{2,1,0:T(8,128)(2,1)} custom-call(bf16[6,64,1536]{2,1,0:T(8,128)(2,1)} %bitcast.47, bf16[6,64,1536]{2,1,0:T(8,128)(2,1)} %bitcast.48), custom_call_target="tpu_custom_call" | custom-call | bytes 4718592 | tf_op jit(solution)/shard_map/pack/pallas_call | solution.py:116
  6.6 8.4 %all-to-all-start = ((bf16[16,192,384]{2,1,0:T(8,128)(2,1)}), bf16[16,192,384]{2,1,0:T(8,128)(2,1)}, u32[]{:S(2)}, u32[]{:S(2)}) async-start(bf16[16,192,384]{2,1,0:T(8,128)(2,1)} %pack.2), calls=%async_computation | async-start | bytes 4718592 | tf_op jit(solution)/shard_map/all_to_all | solution.py:91
  15.0 0.0 copy-start.4
  15.0 0.0 copy-start.10
  15.1 13.0 %all-gather = bf16[8,6,1536]{2,1,0:T(8,128)(2,1)S(1)} all-gather(bf16[1,6,1536]{2,1,0:T(8,128)(2,1)S(1)} %maximum_bitcast_fusion.2), channel_id=1, replica_groups={{0,1,32,33,64,65,96,97},{2,3,34,35,66,67,98,99},{4,5,36,37,68,69,100,10..., dimensions={0}, use_global_device_ids=true | all-gather | bytes 165888 | tf_op jit(solution)/shard_map/all_gather | solution.py:570
  28.1 0.1 copy.26
  28.3 0.7 reshape.217.text_ref
  29.0 5.5 %pack.3 = bf16[16,144,384]{2,1,0:T(8,128)(2,1)} custom-call(bf16[6,64,1536]{2,1,0:T(8,128)(2,1)} %bitcast.46, bf16[48,1536]{1,0:T(8,128)(2,1)} %reshape.217.text_ref), custom_call_target="tpu_custom_call" | custom-call | bytes 3538944 | tf_op jit(solution)/shard_map/pack/pallas_call | solution.py:116
  34.4 13.2 %all-to-all-done = bf16[16,192,384]{2,1,0:T(8,128)(2,1)} async-done(((bf16[16,192,384]{2,1,0:T(8,128)(2,1)}), bf16[16,192,384]{2,1,0:T(8,128)(2,1)}, u32[]{:S(2)}, u32[]{:S(2)}) %all-to-all-start) | async-done | bytes 2359328 | tf_op jit(solution)/shard_map/all_to_all | solution.py:91
  47.6 0.0 collective-permute-start.2
  47.6 0.1 collective-permute-start.1
  47.8 0.2 select_reduce_fusion
  48.0 0.1 slice.38.valid_ref
  48.1 7.4 %all-to-all-start.1 = ((bf16[16,144,384]{2,1,0:T(8,128)(2,1)}), bf16[16,144,384]{2,1,0:T(8,128)(2,1)S(1)}, u32[]{:S(2)}, u32[]{:S(2)}) async-start(bf16[16,144,384]{2,1,0:T(8,128)(2,1)} %pack.3), calls=%async_computation.1 | async-start | bytes 3538944 | tf_op jit(solution)/shard_map/all_to_all | solution.py:91
  55.6 0.1 broadcast_compare_fusion
  55.6 0.1 and_and_fusion
  55.7 0.0 collective-permute-done.2.other_ref
  55.7 4.9 %merge.3 = (bf16[2,768,384]{2,1,0:T(8,128)(2,1)}, bf16[2,768,384]{2,1,0:T(8,128)(2,1)}, bf16[2,2,768,384]{3,2,1,0:T(8,128)(2,1)}, bf16[2,2,768,384]{3,2,1,0:T(8,128)(2,1)}) custom-call(s32[1]{0:T(128)} %bitcast.1.c_ref, bf16[2,2,4,192,384]{4,3,2,1,0:T(8,128)(2,1)} %bitcast.14.mine_ref, bf16[2,2,4,192,384]{4,3,2,1,0:T(8,128)(2,1)} %collective-permute-done.2.other_ref), custom_call_target="tpu_custom_call" | custom-call | bytes 14155776 | tf_op jit(solution)/shard_map/merge/pallas_call | solution.py:178
  60.6 1.9 %collective-permute-start.5 = (bf16[2,2,768,384]{3,2,1,0:T(8,128)(2,1)}, bf16[2,2,768,384]{3,2,1,0:T(8,128)(2,1)}, u32[]{:S(2)}, u32[]{:S(2)}) collective-permute-start(bf16[2,2,768,384]{3,2,1,0:T(8,128)(2,1)} %get-tuple-element.24.refs_0_.refs_1_), channel_id=1, source_target_pairs={{1,32},{3,34},{5,36},{7,38},{17,48},{19,50},{21,52},{23,54},{9,40}... | collective-permute-start | bytes 7077896 | tf_op jit(solution)/shard_map/ppermute | solution.py:87
  62.5 0.1 broadcast_add_fusion
  62.6 0.1 add_select_fusion
  62.7 0.0 collective-permute-done.1
  62.7 0.6 compare_reduce_fusion
  63.3 1.3 collective-permute-start.3
  64.6 5.6 %collective-permute-start.4 = (bf16[2,768,384]{2,1,0:T(8,128)(2,1)}, bf16[2,768,384]{2,1,0:T(8,128)(2,1)}, u32[]{:S(2)}, u32[]{:S(2)}) collective-permute-start(bf16[2,768,384]{2,1,0:T(8,128)(2,1)} %get-tuple-element.26), channel_id=1, source_target_pairs={{2,0},{3,1},{4,2},{5,3},{6,4},{7,5},{18,16},{19,17},{20,18},{21,19... | collective-permute-start | bytes 3538952 | tf_op jit(solution)/shard_map/ppermute | solution.py:87
  70.2 0.1 select_convert_fusion
  70.3 10.5 %all-to-all-done.1.rows_ref = bf16[16,144,384]{2,1,0:T(8,128)(2,1)S(1)} async-done(((bf16[16,144,384]{2,1,0:T(8,128)(2,1)}), bf16[16,144,384]{2,1,0:T(8,128)(2,1)S(1)}, u32[]{:S(2)}, u32[]{:S(2)}) %all-to-all-start.1) | async-done | bytes 1769504 | tf_op jit(solution)/shard_map/all_to_all | solution.py:91
  80.8 0.1 slice.45
  80.9 0.1 dynamic-slice_bitcast_fusion
  81.0 0.1 collective-permute-start
  81.2 0.8 slice_bitcast_fusion.bias_ref
  82.0 1.1 collective-permute-done.other_ref
  83.1 0.8 copy-done.3
  83.9 2.7 %merge.2 = (bf16[2,2,384,384]{3,2,1,0:T(8,128)(2,1)}, bf16[3,256,384]{2,1,0:T(8,128)(2,1)}) custom-call(s32[1]{0:T(128)} %bitcast.1.c_ref, bf16[2,2,4,144,384]{4,3,2,1,0:T(8,128)(2,1)} %bitcast.44, bf16[2,4,96,384]{3,2,1,0:T(8,128)(2,1)} %copy-done.3, bf16[16,144,384]{2,1,0:T(8,128)(2,1)} %copy-done.1), custom_call_target="tpu_custom_call" | custom-call | bytes 3538944 | tf_op jit(solution)/shard_map/merge/pallas_call | solution.py:178
  86.6 5.1 %text_queries.1 = f32[256,512]{1,0:T(8,128)} custom-call(s32[1]{0:T(128)} %bitcast.share_ref, bf16[3,256,384]{2,1,0:T(8,128)(2,1)} %get-tuple-element.21.q_ref.tk_ref.tv_ref, bf16[3,256,384]{2,1,0:T(8,128)(2,1)} %get-tuple-element.21.q_ref.tk_ref.tv_ref, bf16[3,256,384]{2,1,0:T(8,128)(2,1)} %get-tuple-element.21.q_ref.tk_ref.tv_ref, ...), custom_call_target="tpu_custom_call" | custom-call | flops 2113929216 | bytes 2752512 | tf_op jit(solution)/shard_map/text_queries/pallas_call | solution.py:501
  91.7 2.1 %reshape.221 = f32[128,2,512]{2,1,0:T(2,128)} reshape(f32[256,512]{1,0:T(8,128)} %text_queries.1) | data formatting | bytes 1048576 | tf_op jit(solution)/shard_map/reshape | solution.py:613
  93.9 9.2 %all-to-all-start.2 = ((f32[128,2,512]{2,1,0:T(2,128)}), f32[128,2,512]{2,1,0:T(2,128)S(1)}, u32[]{:S(2)}, u32[]{:S(2)}) async-start(f32[128,2,512]{2,1,0:T(2,128)} %reshape.221), calls=%async_computation.2 | async-start | bytes 1048576 | tf_op jit(solution)/shard_map/all_to_all | solution.py:91
  103.1 3.6 %collective-permute-done.3.left_ref = bf16[2,768,384]{2,1,0:T(8,128)(2,1)} collective-permute-done((bf16[2,768,384]{2,1,0:T(8,128)(2,1)}, bf16[2,768,384]{2,1,0:T(8,128)(2,1)}, u32[]{:S(2)}, u32[]{:S(2)}) %collective-permute-start.3) | collective-permute-done | bytes 1179680 | tf_op jit(solution)/shard_map/ppermute | solution.py:87
  106.7 0.0 collective-permute-done.4.right_ref
  106.7 2.9 %join.1.refs_0_.refs_1_ = bf16[2,2,768,384]{3,2,1,0:T(8,128)(2,1)} custom-call(bf16[2,768,384]{2,1,0:T(8,128)(2,1)} %collective-permute-done.3.left_ref, bf16[2,768,384]{2,1,0:T(8,128)(2,1)} %collective-permute-done.4.right_ref), custom_call_target="tpu_custom_call" | custom-call | bytes 4718592 | tf_op jit(solution)/shard_map/join/pallas_call | solution.py:227
  109.6 0.0 collective-permute-start.6
  109.6 2.5 %collective-permute-start.7 = (bf16[2,2,768,384]{3,2,1,0:T(8,128)(2,1)}, bf16[2,2,768,384]{3,2,1,0:T(8,128)(2,1)S(1)}, u32[]{:S(2)}, u32[]{:S(2)}) collective-permute-start(bf16[2,2,768,384]{3,2,1,0:T(8,128)(2,1)} %join.1.refs_0_.refs_1_), channel_id=1, source_target_pairs={{1,32},{3,34},{5,36},{7,38},{17,48},{19,50},{21,52},{23,54},{9,40}... | collective-permute-start | bytes 7077896 | tf_op jit(solution)/shard_map/ppermute | solution.py:87
  112.0 0.0 collective-permute-done.5.refs_4_.refs_5_
  112.0 29.6 %near_cells.1 = (f32[2,768,384]{2,1,0:T(8,128)}, f32[2,768,128]{2,1,0:T(8,128)S(1)}) custom-call(bf16[2,2,384,384]{3,2,1,0:T(8,128)(2,1)} %get-tuple-element.28.q_ref, bf16[3,256,384]{2,1,0:T(8,128)(2,1)S(1)} %copy-done, bf16[3,256,384]{2,1,0:T(8,128)(2,1)S(1)} %copy-done, bf16[6,2,16,128]{3,2,1,0:T(8,128)(2,1)S(1)} %bitcast.40, ...), custom_call_target="tpu_custom_call" | custom-call | flops 34426847232 | bytes 7471104 | tf_op jit(solution)/shard_map/near_cells/pallas_call | solution.py:395
  141.7 0.0 collective-permute-done.6.refs_2_.refs_3_
  141.7 0.0 copy-start.8
  141.7 0.0 collective-permute-done.7.refs_4_.refs_5_
  141.7 1.4 copy-done.8
  143.1 0.8 copy-done.9
  143.9 15.7 %side_cells.1 = bf16[2,2,384,384]{3,2,1,0:T(8,128)(2,1)S(1)} custom-call(s32[2]{0:T(128)S(1)} %slice.38.valid_ref, bf16[2,2,384,384]{3,2,1,0:T(8,128)(2,1)} %get-tuple-element.28.q_ref, f32[2,768,384]{2,1,0:T(8,128)} %get-tuple-element.30.sum_ref, f32[2,768,128]{2,1,0:T(8,128)S(1)} %get-tuple-element.31.mark_ref, ...), custom_call_target="tpu_custom_call" | custom-call | flops 16307453952 | bytes 3538944 | tf_op jit(solution)/shard_map/side_cells/pallas_call | solution.py:451
  159.5 0.0 all-to-all-done.2
  159.5 0.0 copy-start.2
  159.6 0.0 slice-start
  159.6 0.1 dynamic-slice_bitcast_fusion.1
  159.7 3.1 %collective-permute-start.8 = (bf16[384,384]{1,0:T(8,128)(2,1)S(1)}, bf16[384,384]{1,0:T(8,128)(2,1)S(1)}, u32[]{:S(2)}, u32[]{:S(2)}) collective-permute-start(bf16[384,384]{1,0:T(8,128)(2,1)S(1)} %get-tuple-element.39), channel_id=1, source_target_pairs={{0,0},{1,16},{2,4},{3,20},{4,8},{5,24},{6,12},{7,28},{16,1},{17,17... | collective-permute-start | bytes 884744 | tf_op jit(solution)/shard_map/ppermute | solution.py:87
  162.9 0.9 collective-permute-start.9
  163.7 1.4 collective-permute-start.10
  165.1 1.7 collective-permute-start.11
  166.9 2.4 %text_sum.1 = bf16[2,1536]{1,0:T(2,128)(2,1)} custom-call(f32[4,32,2,512]{3,2,1,0:T(2,128)} %bitcast.45), custom_call_target="tpu_custom_call" | custom-call | bytes 524288 | tf_op jit(solution)/shard_map/text_sum/pallas_call | solution.py:535
  169.3 5.8 %convolution_convert_fusion = bf16[2,3072]{1,0:T(2,128)(2,1)} fusion(bf16[2,1536]{1,0:T(2,128)(2,1)} %text_sum.1, bf16[1536,3072]{1,0:T(8,128)(2,1)} %param.19), kind=kOutput, calls=%fused_computation | convolution fusion | flops 18880512 | bytes 9455616 | tf_op jit(solution)/shard_map/dot_general | solution.py:630
  175.1 1.2 collective-permute-done.8.first
  176.2 0.0 collective-permute-done.9.second
  176.2 5.9 %collective-permute-done.11.fourth = bf16[384,384]{1,0:T(8,128)(2,1)S(1)} collective-permute-done((bf16[384,384]{1,0:T(8,128)(2,1)S(1)}, bf16[384,384]{1,0:T(8,128)(2,1)S(1)}, u32[]{:S(2)}, u32[]{:S(2)}) %collective-permute-start.11) | collective-permute-done | bytes 294944 | tf_op jit(solution)/shard_map/ppermute | solution.py:87
  182.1 5.7 %project.1 = bf16[384,3072]{1,0:T(8,128)(2,1)} custom-call(s32[4]{0:T(128)S(1)} %and_select_fusion.1.from_ref, bf16[384,384]{1,0:T(8,128)(2,1)S(1)} %collective-permute-done.8.first, bf16[384,384]{1,0:T(8,128)(2,1)S(1)} %collective-permute-done.9.second, bf16[384,384]{1,0:T(8,128)(2,1)S(1)} %collective-permute-done.10.third, ...), custom_call_target="tpu_custom_call" | custom-call | flops 3623878656 | bytes 9437184 | tf_op jit(solution)/shard_map/project/pallas_call | solution.py:254
  (42 shorter events, 0.3 us)
Async XLA Ops:
  6.6 8.4 %copy-start.5 = (bf16[2,1536]{1,0:T(2,128)(2,1)S(1)}, bf16[2,1536]{1,0:T(2,128)(2,1)}, u32[]{:S(2)}) copy-start(bf16[2,1536]{1,0:T(2,128)(2,1)} %param.15) | copy-start | bytes 18436
  6.6 8.4 %copy-start.6 = (bf16[2,1536]{1,0:T(2,128)(2,1)S(1)}, bf16[2,1536]{1,0:T(2,128)(2,1)}, u32[]{:S(2)}) copy-start(bf16[2,1536]{1,0:T(2,128)(2,1)} %param.14) | copy-start | bytes 18436
  6.6 8.4 %copy-start.7 = (bf16[2,1536]{1,0:T(2,128)(2,1)S(1)}, bf16[2,1536]{1,0:T(2,128)(2,1)}, u32[]{:S(2)}) copy-start(bf16[2,1536]{1,0:T(2,128)(2,1)} %param.13) | copy-start | bytes 18436
  6.6 41.1 %all-to-all-start = ((bf16[16,192,384]{2,1,0:T(8,128)(2,1)}), bf16[16,192,384]{2,1,0:T(8,128)(2,1)}, u32[]{:S(2)}, u32[]{:S(2)}) async-start(bf16[16,192,384]{2,1,0:T(8,128)(2,1)} %pack.2), calls=%async_computation | async-start | bytes 4718592 | tf_op jit(solution)/shard_map/all_to_all | solution.py:91
  15.0 32.6 %copy-start.4 = (s32[1,16,27]{2,1,0:T(8,128)S(1)}, s32[1,16,27]{2,1,0:T(8,128)}, u32[]{:S(2)}) copy-start(s32[1,16,27]{2,1,0:T(8,128)} %param.16) | copy-start | bytes 5188
  15.0 32.8 %copy-start.10 = (s32[8]{0:T(128)S(1)}, s32[8]{0:T(128)}, u32[]{:S(2)}) copy-start(s32[8]{0:T(128)} %param.17) | copy-start | bytes 100
  47.6 8.1 %collective-permute-start.2 = (bf16[2,2,4,192,384]{4,3,2,1,0:T(8,128)(2,1)}, bf16[2,2,4,192,384]{4,3,2,1,0:T(8,128)(2,1)}, u32[]{:S(2)}, u32[]{:S(2)}) collective-permute-start(bf16[2,2,4,192,384]{4,3,2,1,0:T(8,128)(2,1)} %bitcast.14.mine_ref), channel_id=1, source_target_pairs={{0,1},{1,0},{2,3},{3,2},{4,5},{5,4},{6,7},{7,6},{16,17},{17,16},{1... | collective-permute-start | bytes 7077896 | tf_op jit(solution)/shard_map/ppermute | solution.py:87
  47.6 15.0 %collective-permute-start.1 = (s32[1,16,27]{2,1,0:T(8,128)S(1)}, s32[1,16,27]{2,1,0:T(8,128)S(1)}, u32[]{:S(2)}, u32[]{:S(2)}) collective-permute-start(s32[1,16,27]{2,1,0:T(8,128)S(1)} %copy-done.4), channel_id=1, source_target_pairs={{0,16},{1,17},{2,18},{3,19},{4,20},{5,21},{6,22},{7,23},{16,0},{17... | collective-permute-start | bytes 5192 | tf_op jit(solution)/shard_map/ppermute | solution.py:87
  48.1 32.7 %all-to-all-start.1 = ((bf16[16,144,384]{2,1,0:T(8,128)(2,1)}), bf16[16,144,384]{2,1,0:T(8,128)(2,1)S(1)}, u32[]{:S(2)}, u32[]{:S(2)}) async-start(bf16[16,144,384]{2,1,0:T(8,128)(2,1)} %pack.3), calls=%async_computation.1 | async-start | bytes 3538944 | tf_op jit(solution)/shard_map/all_to_all | solution.py:91
  60.6 51.5 %collective-permute-start.5 = (bf16[2,2,768,384]{3,2,1,0:T(8,128)(2,1)}, bf16[2,2,768,384]{3,2,1,0:T(8,128)(2,1)}, u32[]{:S(2)}, u32[]{:S(2)}) collective-permute-start(bf16[2,2,768,384]{3,2,1,0:T(8,128)(2,1)} %get-tuple-element.24.refs_0_.refs_1_), channel_id=1, source_target_pairs={{1,32},{3,34},{5,36},{7,38},{17,48},{19,50},{21,52},{23,54},{9,40}... | collective-permute-start | bytes 7077896 | tf_op jit(solution)/shard_map/ppermute | solution.py:87
  63.3 43.4 %collective-permute-start.3 = (bf16[2,768,384]{2,1,0:T(8,128)(2,1)}, bf16[2,768,384]{2,1,0:T(8,128)(2,1)}, u32[]{:S(2)}, u32[]{:S(2)}) collective-permute-start(bf16[2,768,384]{2,1,0:T(8,128)(2,1)} %get-tuple-element.25), channel_id=1, source_target_pairs={{0,2},{1,3},{2,4},{3,5},{4,6},{5,7},{16,18},{17,19},{18,20},{19,21... | collective-permute-start | bytes 3538952 | tf_op jit(solution)/shard_map/ppermute | solution.py:87
  64.6 42.1 %collective-permute-start.4 = (bf16[2,768,384]{2,1,0:T(8,128)(2,1)}, bf16[2,768,384]{2,1,0:T(8,128)(2,1)}, u32[]{:S(2)}, u32[]{:S(2)}) collective-permute-start(bf16[2,768,384]{2,1,0:T(8,128)(2,1)} %get-tuple-element.26), channel_id=1, source_target_pairs={{2,0},{3,1},{4,2},{5,3},{6,4},{7,5},{18,16},{19,17},{20,18},{21,19... | collective-permute-start | bytes 3538952 | tf_op jit(solution)/shard_map/ppermute | solution.py:87
  80.8 2.3 %copy-start.1 = (bf16[16,144,384]{2,1,0:T(8,128)(2,1)}, bf16[16,144,384]{2,1,0:T(8,128)(2,1)S(1)}, u32[]{:S(2)}) copy-start(bf16[16,144,384]{2,1,0:T(8,128)(2,1)S(1)} %all-to-all-done.1.rows_ref) | copy-start | bytes 5308420
  81.0 2.1 %collective-permute-start = (bf16[2,4,96,384]{3,2,1,0:T(8,128)(2,1)S(1)}, bf16[2,4,96,384]{3,2,1,0:T(8,128)(2,1)S(1)}, u32[]{:S(2)}, u32[]{:S(2)}) collective-permute-start(bf16[2,4,96,384]{3,2,1,0:T(8,128)(2,1)S(1)} %dynamic-slice_bitcast_fusion), channel_id=1, source_target_pairs={{0,1},{1,0},{2,3},{3,2},{4,5},{5,4},{6,7},{7,6},{16,17},{17,16},{1... | collective-permute-start | bytes 1769480 | tf_op jit(solution)/shard_map/ppermute | solution.py:87
  83.1 0.8 copy-start.3
  93.9 65.7 %all-to-all-start.2 = ((f32[128,2,512]{2,1,0:T(2,128)}), f32[128,2,512]{2,1,0:T(2,128)S(1)}, u32[]{:S(2)}, u32[]{:S(2)}) async-start(f32[128,2,512]{2,1,0:T(2,128)} %reshape.221), calls=%async_computation.2 | async-start | bytes 1048576 | tf_op jit(solution)/shard_map/all_to_all | solution.py:91
  106.7 5.3 %copy-start = (bf16[3,256,384]{2,1,0:T(8,128)(2,1)S(1)}, bf16[3,256,384]{2,1,0:T(8,128)(2,1)}, u32[]{:S(2)}) copy-start(bf16[3,256,384]{2,1,0:T(8,128)(2,1)} %get-tuple-element.21.q_ref.tk_ref.tv_ref) | copy-start | bytes 1769476
  109.6 32.1 %collective-permute-start.6 = (bf16[2,2,768,384]{3,2,1,0:T(8,128)(2,1)}, bf16[2,2,768,384]{3,2,1,0:T(8,128)(2,1)S(1)}, u32[]{:S(2)}, u32[]{:S(2)}) collective-permute-start(bf16[2,2,768,384]{3,2,1,0:T(8,128)(2,1)} %join.1.refs_0_.refs_1_), channel_id=1, source_target_pairs={{0,1},{1,0},{2,3},{3,2},{4,5},{5,4},{6,7},{7,6},{16,17},{17,16},{1... | collective-permute-start | bytes 7077896 | tf_op jit(solution)/shard_map/ppermute | solution.py:87
  109.6 32.1 %collective-permute-start.7 = (bf16[2,2,768,384]{3,2,1,0:T(8,128)(2,1)}, bf16[2,2,768,384]{3,2,1,0:T(8,128)(2,1)S(1)}, u32[]{:S(2)}, u32[]{:S(2)}) collective-permute-start(bf16[2,2,768,384]{3,2,1,0:T(8,128)(2,1)} %join.1.refs_0_.refs_1_), channel_id=1, source_target_pairs={{1,32},{3,34},{5,36},{7,38},{17,48},{19,50},{21,52},{23,54},{9,40}... | collective-permute-start | bytes 7077896 | tf_op jit(solution)/shard_map/ppermute | solution.py:87
  141.7 1.4 copy-start.8
  141.7 2.2 %copy-start.9 = (bf16[2,2,768,384]{3,2,1,0:T(8,128)(2,1)}, bf16[2,2,768,384]{3,2,1,0:T(8,128)(2,1)S(1)}, u32[]{:S(2)}) copy-start(bf16[2,2,768,384]{3,2,1,0:T(8,128)(2,1)S(1)} %collective-permute-done.7.refs_4_.refs_5_) | copy-start | bytes 7077892
  159.5 7.3 %copy-start.2 = (f32[128,2,512]{2,1,0:T(2,128)}, f32[128,2,512]{2,1,0:T(2,128)S(1)}, u32[]{:S(2)}) copy-start(f32[128,2,512]{2,1,0:T(2,128)S(1)} %all-to-all-done.2) | copy-start | bytes 1572868
  159.6 22.6 %slice-start = ((s8[9437184]{0:T(1024)(128)(4,1)}), s8[1048576]{0:T(1024)(128)(4,1)S(1)}, s32[]{:S(2)}) async-start(s8[9437184]{0:T(1024)(128)(4,1)} %bitcast.41), calls=%async_computation.3 | async-start | bytes 2097152
  159.7 16.5 %collective-permute-start.8 = (bf16[384,384]{1,0:T(8,128)(2,1)S(1)}, bf16[384,384]{1,0:T(8,128)(2,1)S(1)}, u32[]{:S(2)}, u32[]{:S(2)}) collective-permute-start(bf16[384,384]{1,0:T(8,128)(2,1)S(1)} %get-tuple-element.39), channel_id=1, source_target_pairs={{0,0},{1,16},{2,4},{3,20},{4,8},{5,24},{6,12},{7,28},{16,1},{17,17... | collective-permute-start | bytes 884744 | tf_op jit(solution)/shard_map/ppermute | solution.py:87
  162.9 13.4 %collective-permute-start.9 = (bf16[384,384]{1,0:T(8,128)(2,1)S(1)}, bf16[384,384]{1,0:T(8,128)(2,1)S(1)}, u32[]{:S(2)}, u32[]{:S(2)}) collective-permute-start(bf16[384,384]{1,0:T(8,128)(2,1)S(1)} %get-tuple-element.38), channel_id=1, source_target_pairs={{0,1},{1,17},{2,5},{3,21},{4,9},{5,25},{6,13},{7,29},{16,2},{17,18... | collective-permute-start | bytes 884744 | tf_op jit(solution)/shard_map/ppermute | solution.py:87
  163.7 12.5 %collective-permute-start.10 = (bf16[384,384]{1,0:T(8,128)(2,1)S(1)}, bf16[384,384]{1,0:T(8,128)(2,1)S(1)}, u32[]{:S(2)}, u32[]{:S(2)}) collective-permute-start(bf16[384,384]{1,0:T(8,128)(2,1)S(1)} %get-tuple-element.37), channel_id=1, source_target_pairs={{0,2},{1,18},{2,6},{3,22},{4,10},{5,26},{6,14},{7,30},{16,3},{17,1... | collective-permute-start | bytes 884744 | tf_op jit(solution)/shard_map/ppermute | solution.py:87
  165.1 17.0 %collective-permute-start.11 = (bf16[384,384]{1,0:T(8,128)(2,1)S(1)}, bf16[384,384]{1,0:T(8,128)(2,1)S(1)}, u32[]{:S(2)}, u32[]{:S(2)}) collective-permute-start(bf16[384,384]{1,0:T(8,128)(2,1)S(1)} %get-tuple-element.36), channel_id=1, source_target_pairs={{0,3},{1,19},{2,7},{3,23},{4,11},{5,27},{6,15},{7,31},{16,0},{17,1... | collective-permute-start | bytes 884744 | tf_op jit(solution)/shard_map/ppermute | solution.py:87
  169.3 12.8 %slice-start.1 = ((s8[9437184]{0:T(1024)(128)(4,1)}), s8[4194304]{0:T(1024)(128)(4,1)S(1)}, s32[]{:S(2)}) async-start(s8[9437184]{0:T(1024)(128)(4,1)} %bitcast.41), calls=%async_computation.4 | async-start | bytes 8388608
  169.3 12.8 %slice-start.2 = ((s8[9437184]{0:T(1024)(128)(4,1)}), s8[4194304]{0:T(1024)(128)(4,1)S(1)}, s32[]{:S(2)}) async-start(s8[9437184]{0:T(1024)(128)(4,1)} %bitcast.41), calls=%async_computation.5 | async-start | bytes 8388608
